TPU v7x, 128 devices: a whole 4x4x4 slice. The times are simulated.
128 devices in a mesh: dp: 4 (over y), ctx: 32 (over z, x, core).
Axes of the slice: x: 4, y: 4, z: 4, core: 2. Of those that a mesh axis runs over, the one named last changes fastest.
Arguments:
- hidden: bfloat16 [4, 4096, 8192], P('dp', 'ctx'), may hold values from -8 to 8
- grad_out: bfloat16 [4, 4096, 2560], P('dp', 'ctx'), may hold values from -8 to 8
- segment: int32 [4, 4096], P('dp', 'ctx'), may hold values from 0 to 31, as said below
Outputs:
- weight_grad: float32 [8192, 2560], P('ctx', 'dp')
Inputs may be any that keep to these rules, and one draw needn't show every extreme that they name: `segment`: ids never fall along a row; each of the 32 documents of a row has 1 to 256 tokens; in every row the first and last documents have one token and the second and second-last exactly 256.
All inputs are finite; a program needn't handle non-finite values.
Results may differ from a plain program's by a relative error of at most 0.00074.
Values may be sent and summed in bfloat16 or wider, within the bound.
No kernel may reach another device: no remote copies, remote signals or barrier semaphores. Data moves between devices by JAX's collectives and lax.ppermute only.
A program may use at most 128 MiB of HBM per device.

v0:
```python
import math

import jax
import jax.numpy as jnp
from jax import lax
from jax.sharding import PartitionSpec as P


def from_behind(block, axis, distance):
    devices = range(lax.axis_size(axis))
    route = [(i - distance, i) for i in devices if i - distance in devices]
    return lax.ppermute(block, axis, route)


def pair_terms(own_hidden, own_grad, own_ident, far_hidden, far_grad, far_ident):
    inner_hidden = lax.dot_general(
        own_hidden, far_hidden, (((1,), (1,)), ((), ())), preferred_element_type=jnp.float32
    )
    inner_grad = lax.dot_general(
        own_grad, far_grad, (((1,), (1,)), ((), ())), preferred_element_type=jnp.float32
    )
    same_doc = own_ident[:, None] == far_ident[None, :]
    return jnp.sum(jnp.where(same_doc, inner_hidden * inner_grad, jnp.float32(0.0)), axis=1)


def body(hidden, grad_out, segment):
    row_count = lax.axis_size("dp")
    doc_count = lax.axis_size("ctx")
    own_hidden = hidden[0]
    own_grad = grad_out[0]
    own_ident = (segment[0] + 1).astype(jnp.bfloat16)
    own_block = (own_hidden, own_grad, own_ident)
    prior_one = from_behind((own_hidden, own_grad, own_ident), "ctx", 1)
    prior_two = from_behind((own_hidden, own_grad, own_ident), "ctx", 2)
    pair_sum = pair_terms(*own_block, *own_block)
    pair_sum = pair_sum + 2.0 * pair_terms(*own_block, *prior_one)
    pair_sum = pair_sum + 2.0 * pair_terms(*own_block, *prior_two)
    onehot = (segment[0][:, None] == jnp.arange(doc_count, dtype=jnp.int32)[None, :]).astype(
        jnp.float32
    )
    partial_norms = jnp.dot(pair_sum, onehot, precision=lax.Precision.HIGHEST)
    doc_norms = lax.psum(partial_norms, "ctx")
    token_count = own_hidden.shape[0]
    width_hidden = hidden.shape[2]
    width_grad = grad_out.shape[2]
    clip_bound = math.sqrt(token_count * width_hidden * width_grad)
    clip_factor = clip_bound / jnp.maximum(jnp.sqrt(doc_norms), clip_bound)
    factor = jnp.dot(onehot, clip_factor, precision=lax.Precision.HIGHEST)
    scaled = (own_grad.astype(jnp.float32) * factor[:, None] / row_count).astype(jnp.bfloat16)
    columns = lax.all_to_all(hidden, "ctx", split_axis=2, concat_axis=1, tiled=True)
    every_hidden = lax.all_gather(columns, "dp", axis=0, tiled=True)
    split_scaled = lax.all_to_all(scaled[None], "dp", split_axis=2, concat_axis=0, tiled=True)
    return jnp.einsum(
        "rtf,rtd->fd",
        every_hidden,
        lax.all_gather(split_scaled, "ctx", axis=1, tiled=True),
        preferred_element_type=jnp.float32,
    )


def solution(mesh):
    in_specs = (P("dp", "ctx", None), P("dp", "ctx", None), P("dp", "ctx"))
    out_specs = P("ctx", "dp")
    return jax.shard_map(body, mesh=mesh, in_specs=in_specs, out_specs=out_specs, check_vma=False)
```

profile of v0, /device:TPU:1, one launch (start us, length us, event | category | flops | bytes accessed | tf_op | source)
XLA Modules:
  0.0 412.5 jit_solution(9148870218713893982)
XLA Ops:
  6.5 0.0 all-gather.4.cloned.1.call-start
  6.5 9.5 %copy.19 = bf16[1,128,8192]{1,0,2:T(2,128)(2,1)} copy(bf16[1,128,8192]{2,1,0:T(8,128)(2,1)} %param.3) | data formatting | bytes 4194304 | tf_op args[0]
  16.0 0.5 broadcast.28
  16.5 45.2 %reduce = bf16[8192,128]{1,0:T(8,128)(2,1)S(1)} reduce(bf16[8192,1,128]{2,1,0:T(2,128)(2,1)} %bitcast.59, bf16[]{:T(256)} %broadcast.28), dimensions={1}, to_apply=%bitcast.48.reduce_sub_computation | reduce | bytes 4194306
  61.7 2.1 reshape.21
  63.8 37.8 %all_to_all.36 = bf16[32,2,16384]{2,1,0:T(2,128)(2,1)S(1)} all-to-all(bf16[32,2,16384]{2,1,0:T(2,128)(2,1)} %reshape.21), channel_id=1, replica_groups=mesh['dp'=4,'ctx'=32] {'ctx'}, dimensions={0} | all-to-all | bytes 4194304 | tf_op jit(solution)/shard_map/all_to_all | solution.py:50
  101.6 6.8 %reshape.22 = bf16[8192,1,128]{2,1,0:T(2,128)(2,1)} reshape(bf16[32,2,16384]{2,1,0:T(2,128)(2,1)S(1)} %all_to_all.36) | data formatting | bytes 4194304
  108.4 2.5 copy.23
  110.9 0.0 copy-start.1
  110.9 2.9 copy.20
  113.8 0.0 all-gather.4.cloned.1.call-update
  113.9 0.0 all-gather.6.cloned.1.call-start
  113.9 1.5 copy-done
  115.4 2.4 collective-permute-start.4
  117.8 2.6 collective-permute-start.1
  120.5 0.0 copy-done.1
  120.5 2.2 collective-permute-start.5
  122.7 3.3 collective-permute-start.2
  125.9 0.0 copy-done.2
  125.9 2.8 collective-permute-start.3
  128.8 0.3 fusion.24
  129.1 0.7 fusion.6
  129.8 69.8 %collective-permute-done.5 = bf16[128,2560]{1,0:T(8,128)(2,1)S(1)} collective-permute-done((bf16[128,2560]{1,0:T(8,128)(2,1)S(1)}, bf16[128,2560]{1,0:T(8,128)(2,1)S(1)}, u32[]{:S(2)}, u32[]{:S(2)}) %collective-permute-start.5) | collective-permute-done | bytes 655392 | tf_op jit(solution)/shard_map/ppermute | solution.py:12
  199.6 1.9 collective-permute-start
  201.6 0.3 fusion.20
  201.9 4.8 %collective-permute-done.2 = bf16[128,2560]{1,0:T(8,128)(2,1)S(1)} collective-permute-done((bf16[128,2560]{1,0:T(8,128)(2,1)S(1)}, bf16[128,2560]{1,0:T(8,128)(2,1)S(1)}, u32[]{:S(2)}, u32[]{:S(2)}) %collective-permute-start.2) | collective-permute-done | bytes 655392 | tf_op jit(solution)/shard_map/ppermute | solution.py:12
  206.7 0.3 fusion.22
  207.0 0.0 collective-permute-done.3
  207.0 0.0 collective-permute-done.4
  207.0 0.7 select_reduce_fusion
  207.7 0.0 collective-permute-done
  207.7 0.0 collective-permute-done.1
  207.8 0.7 select_reduce_fusion.1
  208.5 0.2 convolution_bitcast_fusion.1
  208.7 61.6 %psum.7 = f32[32]{0:T(128)S(1)} all-reduce(f32[32]{0:T(128)S(1)} %convolution_bitcast_fusion.1), channel_id=1, replica_groups=mesh['dp'=4,'ctx'=32] {'ctx'}, use_global_device_ids=true, to_apply=%region_3.4 | all-reduce | flops 32 | bytes 256 | tf_op jit(solution)/shard_map/psum | solution.py:42
  270.3 0.2 convolution_bitcast_fusion
  270.5 0.3 multiply_convert_fusion
  270.8 1.0 copy.18
  271.8 14.3 %reduce.1 = bf16[2560,128]{1,0:T(8,128)(2,1)S(1)} reduce(bf16[2560,1,128]{2,1,0:T(2,128)(2,1)S(1)} %bitcast.65, bf16[]{:T(256)} %broadcast.28), dimensions={1}, to_apply=%bitcast.50.reduce_sub_computation | reduce | bytes 1310722
  286.1 0.1 reshape.23
  286.2 11.6 %all_to_all.37 = bf16[4,2,40960]{2,1,0:T(2,128)(2,1)S(1)} all-to-all(bf16[4,2,40960]{2,1,0:T(2,128)(2,1)S(1)} %reshape.23), channel_id=1, replica_groups=mesh['dp'=4,'ctx'=32] {'dp'}, dimensions={0} | all-to-all | bytes 1310720 | tf_op jit(solution)/shard_map/all_to_all | solution.py:52
  297.8 0.6 reshape.24
  298.5 0.9 copy.22
  299.4 0.0 all-gather.6.cloned.1.call-update
  299.4 0.0 all-gather.4.cloned.1.call-done
  299.5 92.9 %all-gather.6.cloned.1.call-done = bf16[4,1,4096,640]{2,3,0,1:T(8,128)(2,1)} async-done(((bf16[4,1,128,640]{2,3,0,1:T(8,128)(2,1)}), bf16[4,1,4096,640]{2,3,0,1:T(8,128)(2,1)}) %all-gather.6.cloned.1.call-update) | async-done | bytes 20971536 | tf_op jit(solution)/shard_map/all_gather | solution.py:56
  392.3 12.2 %fusion.2 = f32[256,640]{0,1:T(8,128)S(1)} fusion(bf16[4,4096,256]{2,1,0:T(8,128)(2,1)} %all-gather.4.cloned.1.call-done, bf16[4,1,4096,640]{2,3,0,1:T(8,128)(2,1)} %all-gather.6.cloned.1.call-done), kind=kOutput, calls=%fused_computation.3 | convolution fusion | flops 5368709120 | bytes 30015488 | tf_op jit(solution)/shard_map/rtf,rtd->fd/dot_general | solution.py:53
  404.6 1.1 copy.21
  (4 shorter events, 0.0 us)
Async XLA Ops:
  6.5 292.9 %all-gather.4.cloned.1.call-start = ((), (), s32[]{:S(2)}) async-start(), calls=%async_computation.2 | async-start | bytes 10485760 | tf_op jit(solution)/shard_map/all_gather | solution.py:51
  110.9 9.6 %copy-start.1 = (bf16[1,128,2560]{2,1,0:T(8,128)(2,1)S(1)}, bf16[1,128,2560]{2,1,0:T(8,128)(2,1)}, u32[]{:S(2)}) copy-start(bf16[1,128,2560]{2,1,0:T(8,128)(2,1)} %param.4) | copy-start | bytes 1966084
  113.8 1.6 copy-start
  113.8 12.1 %copy-start.2 = (s32[1,128]{1,0:T(1,128)S(1)}, s32[1,128]{1,0:T(1,128)}, u32[]{:S(2)}) copy-start(s32[1,128]{1,0:T(1,128)} %param.5) | copy-start | bytes 1540
  113.9 278.5 %all-gather.6.cloned.1.call-start = ((), (), s32[]{:S(2)}) async-start(), calls=%async_computation.3 | async-start | bytes 21626880 | tf_op jit(solution)/shard_map/all_gather | solution.py:56
  115.4 91.6 %collective-permute-start.4 = (bf16[128,8192]{1,0:T(8,128)(2,1)S(1)}, bf16[128,8192]{1,0:T(8,128)(2,1)S(1)}, u32[]{:S(2)}, u32[]{:S(2)}) collective-permute-start(bf16[128,8192]{1,0:T(8,128)(2,1)S(1)} %bitcast.57), channel_id=1, source_target_pairs={{0,2},{1,3},{2,4},{3,5},{4,6},{5,7},{6,8},{7,9},{8,10},{9,11},{10,... | collective-permute-start | bytes 6291464 | tf_op jit(solution)/shard_map/ppermute | solution.py:12
  117.8 89.9 %collective-permute-start.1 = (bf16[128,8192]{1,0:T(8,128)(2,1)S(1)}, bf16[128,8192]{1,0:T(8,128)(2,1)S(1)}, u32[]{:S(2)}, u32[]{:S(2)}) collective-permute-start(bf16[128,8192]{1,0:T(8,128)(2,1)S(1)} %bitcast.58), channel_id=1, source_target_pairs={{0,1},{1,2},{2,3},{3,4},{4,5},{5,6},{6,7},{7,8},{8,9},{9,10},{10,1... | collective-permute-start | bytes 6291464 | tf_op jit(solution)/shard_map/ppermute | solution.py:12
  120.5 79.2 %collective-permute-start.5 = (bf16[128,2560]{1,0:T(8,128)(2,1)S(1)}, bf16[128,2560]{1,0:T(8,128)(2,1)S(1)}, u32[]{:S(2)}, u32[]{:S(2)}) collective-permute-start(bf16[128,2560]{1,0:T(8,128)(2,1)S(1)} %bitcast.63), channel_id=1, source_target_pairs={{0,2},{1,3},{2,4},{3,5},{4,6},{5,7},{6,8},{7,9},{8,10},{9,11},{10,... | collective-permute-start | bytes 1966088 | tf_op jit(solution)/shard_map/ppermute | solution.py:12
  122.7 84.0 %collective-permute-start.2 = (bf16[128,2560]{1,0:T(8,128)(2,1)S(1)}, bf16[128,2560]{1,0:T(8,128)(2,1)S(1)}, u32[]{:S(2)}, u32[]{:S(2)}) collective-permute-start(bf16[128,2560]{1,0:T(8,128)(2,1)S(1)} %bitcast.64), channel_id=1, source_target_pairs={{0,1},{1,2},{2,3},{3,4},{4,5},{5,6},{6,7},{7,8},{8,9},{9,10},{10,1... | collective-permute-start | bytes 1966088 | tf_op jit(solution)/shard_map/ppermute | solution.py:12
  125.9 81.1 %collective-permute-start.3 = (bf16[128]{0:T(256)(128)(2,1)S(1)}, bf16[128]{0:T(256)(128)(2,1)S(1)}, u32[]{:S(2)}, u32[]{:S(2)}) collective-permute-start(bf16[128]{0:T(256)(128)(2,1)S(1)} %add_convert_fusion), channel_id=1, source_target_pairs={{0,2},{1,3},{2,4},{3,5},{4,6},{5,7},{6,8},{7,9},{8,10},{9,11},{10,... | collective-permute-start | bytes 776 | tf_op jit(solution)/shard_map/ppermute | solution.py:12
  199.6 8.1 %collective-permute-start = (bf16[128]{0:T(256)(128)(2,1)S(1)}, bf16[128]{0:T(256)(128)(2,1)S(1)}, u32[]{:S(2)}, u32[]{:S(2)}) collective-permute-start(bf16[128]{0:T(256)(128)(2,1)S(1)} %add_convert_fusion), channel_id=1, source_target_pairs={{0,1},{1,2},{2,3},{3,4},{4,5},{5,6},{6,7},{7,8},{8,9},{9,10},{10,1... | collective-permute-start | bytes 776 | tf_op jit(solution)/shard_map/ppermute | solution.py:12
Sparse Core Ops, SparseCore 0:
  114.0 80.6 all-gather.3
  299.5 92.7 all-gather.5
where the time goes:
time: 413 us; the launch traced here: 412 us
  waiting for transfers between devices  168 us (41%)
  blocking collectives  111 us (27%)
  other arithmetic  59.7 us (14%)
  local copies, waits for them, and re-layouts  29.5 us (7%)
  matrix products  15.8 us (4%)
  starting transfers between devices  15.2 us (4%)
  between operations  13.6 us (3%)
    all_gather x1, waiting for transfers between devices, body(): lax.all_gather(split_scaled, 'ctx', axis=1, tiled=True)  92.9 us
    ppermute x6, waiting for transfers between devices, from_behind(): return lax.ppermute(block, axis, route)  74.6 us
    psum x1, blocking collectives, body(): doc_norms = lax.psum(partial_norms, 'ctx')  61.6 us
    unnamed x2, other arithmetic  59.4 us
    all_to_all x1, blocking collectives, body(): lax.all_to_all(hidden, 'ctx', split_axis=2, concat_axis=1, tiled=True)  37.8 us
    unnamed x14, local copies, waits for them, and re-layouts  24.6 us
    ppermute x6, starting transfers between devices, from_behind(): return lax.ppermute(block, axis, route)  15.2 us
    dot_general x1, matrix products, body(): jnp.einsum('rtf,rtd->fd', every_hidden, lax.all_gather(split_scaled, 'ctx...  12.2 us
  transfers between devices with their start and end apart: 8, of which 3 were waited for; matrix products, arithmetic and copies ran while one was open for 5% of the time, Pallas kernels for 0%

commit v1 on v0

v1 whole, which is shorter than its diff:
```python
import functools
import math

import jax
import jax.numpy as jnp
from jax import lax
from jax.experimental import pallas as pl
from jax.experimental.pallas import tpu as pltpu
from jax.sharding import PartitionSpec as P

BLK = 128
TILE = 256
DOCS = 32
STEP = 512


def onehot_docs(ids_ref, base, count):
    ids = jnp.concatenate([ids_ref[j] for j in range(count)], axis=1) + base
    docs = lax.broadcasted_iota(jnp.int32, (4 * DOCS, count * BLK), 0)
    return docs == ids


def gram_kernel(parts, finish, rows_ref, ids_ref, *refs):
    h_refs = refs[: sum(parts)]
    g_ref, init_ref, out_ref, h_buf, g_buf, hot_buf, acc = refs[sum(parts) :]
    k = pl.program_id(0)
    i = pl.program_id(1)
    steps = pl.num_programs(1)
    base = rows_ref[k] * DOCS

    @pl.when((k == 0) & (i == 0))
    def _():
        acc[...] = init_ref[...]

    @pl.when(i == 0)
    def _():
        h_buf[1] = jnp.zeros_like(h_buf[1])
        g_buf[1] = jnp.zeros_like(g_buf[1])
        hot_buf[1] = jnp.zeros_like(hot_buf[1])

    slot = lax.rem(i, 2)
    at = 0
    for row, pieces in enumerate(parts):
        span = steps // pieces
        for piece in range(pieces):

            @pl.when((k == row) & (i // span == piece))
            def _(ref=h_refs[at]):
                h_buf[slot] = ref[...].reshape(TILE, ref.shape[2])

            at += 1
    g_buf[slot] = g_ref[...].reshape(TILE, g_ref.shape[2])
    hot = onehot_docs(ids_ref, base, 2)
    hot_buf[slot] = hot.astype(jnp.bfloat16)

    nt = (((1,), (1,)), ((), ()))
    total = jnp.zeros((1, TILE), jnp.float32)
    own_h = h_buf[slot]
    own_g = g_buf[slot]
    own_hot = hot_buf[slot]
    for other in range(2):
        inner_h = lax.dot_general(h_buf[other], own_h, nt, preferred_element_type=jnp.float32)
        inner_g = lax.dot_general(g_buf[other], own_g, nt, preferred_element_type=jnp.float32)
        same = lax.dot_general(
            hot_buf[other], own_hot, (((0,), (0,)), ((), ())), preferred_element_type=jnp.float32
        )
        weight = jnp.where(slot == other, jnp.float32(1.0), jnp.float32(2.0))
        total += weight * jnp.sum(inner_h * inner_g * same, axis=0, keepdims=True)
    terms = jnp.where(hot, jnp.broadcast_to(total, hot.shape), jnp.float32(0.0))
    acc[...] += terms[:, :BLK] + terms[:, BLK:]

    @pl.when((k == pl.num_programs(0) - 1) & (i == steps - 1))
    def _():
        if finish:
            sums = jnp.sum(acc[...].T, axis=0, keepdims=True)
            out_ref[...] = jnp.broadcast_to(sums[None], out_ref.shape)
        else:
            out_ref[...] = acc[...]


def h_specs(parts, blocks, per_step):
    specs = []
    for row, pieces in enumerate(parts):
        span = blocks // per_step // pieces
        for piece in range(pieces):

            def index(k, i, *_, row=row, piece=piece, span=span):
                here = jnp.clip(i - piece * span, 0, span - 1)
                return (jnp.where(k < row, 0, jnp.where(k > row, span - 1, here)), 0, 0)

            specs.append(pl.BlockSpec((per_step, BLK, TILE), index))
    return specs


def gram(rows, ids, parts, pieces, every_grad, init, finish):
    blocks, row_count, _, width = every_grad.shape
    steps = blocks * BLK // TILE
    per_row = steps
    shape = (row_count * blocks, 1, BLK) if finish else (row_count * DOCS, BLK)
    return pl.pallas_call(
        functools.partial(gram_kernel, parts, finish),
        out_shape=jax.ShapeDtypeStruct(shape, jnp.float32),
        grid_spec=pltpu.PrefetchScalarGridSpec(
            num_scalar_prefetch=1,
            grid=(len(parts), steps),
            in_specs=[
                pl.BlockSpec((2, 1, BLK), lambda k, i, r: (r[k] * per_row + i, 0, 0)),
                *h_specs(parts, blocks, 2),
                pl.BlockSpec((2, None, BLK, width), lambda k, i, r: (i, r[k], 0, 0)),
                pl.BlockSpec((row_count * DOCS, BLK), lambda k, i, r: (0, 0)),
            ],
            out_specs=pl.BlockSpec(shape, lambda k, i, r: (0,) * len(shape)),
            scratch_shapes=[
                pltpu.VMEM((2, TILE, TILE), jnp.bfloat16),
                pltpu.VMEM((2, TILE, width), jnp.bfloat16),
                pltpu.VMEM((2, row_count * DOCS, TILE), jnp.bfloat16),
                pltpu.VMEM((row_count * DOCS, BLK), jnp.float32),
            ],
        ),
        compiler_params=pltpu.CompilerParams(vmem_limit_bytes=32 * 2**20),
        cost_estimate=pl.CostEstimate(
            flops=len(parts) * steps * 2 * TILE * TILE * 2 * (TILE + width),
            bytes_accessed=len(parts) * blocks * BLK * 2 * (TILE + width),
            transcendentals=0,
        ),
        name="gram",
    )(rows, ids, *pieces, every_grad, init)


def product_kernel(parts, bound, rows_ref, ids_ref, norms_ref, *refs):
    h_refs = refs[: sum(parts)]
    g_ref, out_ref, clip, scaled = refs[sum(parts) :]
    k = pl.program_id(0)
    i = pl.program_id(1)
    steps = pl.num_programs(1)

    @pl.when((k == 0) & (i == 0))
    def _():
        out_ref[...] = jnp.zeros_like(out_ref)
        norms = jnp.sum(norms_ref[...], axis=0)
        factor = bound / jnp.maximum(jnp.sqrt(norms), bound) / len(parts)
        clip[...] = jnp.broadcast_to(factor, clip.shape).T

    count = STEP // BLK
    hot = onehot_docs(ids_ref, rows_ref[k] * DOCS, count).astype(jnp.float32)
    factor = lax.dot_general(
        hot,
        clip[...],
        (((0,), (0,)), ((), ())),
        precision=lax.Precision.HIGHEST,
        preferred_element_type=jnp.float32,
    )
    width = g_ref.shape[2]
    for j in range(count):
        for c in range(0, width, BLK):
            scaled[j * BLK : (j + 1) * BLK, c : c + BLK] = (
                g_ref[j, :, c : c + BLK].astype(jnp.float32) * factor[j * BLK : (j + 1) * BLK]
            ).astype(jnp.bfloat16)
    at = 0
    for row, pieces in enumerate(parts):
        span = steps // pieces
        for piece in range(pieces):

            @pl.when((k == row) & (i // span == piece))
            def _(ref=h_refs[at]):
                out_ref[...] += lax.dot_general(
                    ref[...].reshape(STEP, ref.shape[2]),
                    scaled[...],
                    (((0,), (0,)), ((), ())),
                    preferred_element_type=jnp.float32,
                )

            at += 1


def product(rows, ids, norms, parts, pieces, every_grad, bound):
    blocks, row_count, _, width = every_grad.shape
    count = STEP // BLK
    steps = blocks // count
    return pl.pallas_call(
        functools.partial(product_kernel, parts, bound),
        out_shape=jax.ShapeDtypeStruct((TILE, width), jnp.float32),
        grid_spec=pltpu.PrefetchScalarGridSpec(
            num_scalar_prefetch=1,
            grid=(len(parts), steps),
            in_specs=[
                pl.BlockSpec((count, 1, BLK), lambda k, i, r: (r[k] * steps + i, 0, 0)),
                pl.BlockSpec(norms.shape, lambda k, i, r: (0, 0, 0)),
                *h_specs(parts, blocks, count),
                pl.BlockSpec((count, None, BLK, width), lambda k, i, r: (i, r[k], 0, 0)),
            ],
            out_specs=pl.BlockSpec((TILE, width), lambda k, i, r: (0, 0)),
            scratch_shapes=[
                pltpu.VMEM((row_count * DOCS, BLK), jnp.float32),
                pltpu.VMEM((STEP, width), jnp.bfloat16),
            ],
        ),
        compiler_params=pltpu.CompilerParams(vmem_limit_bytes=32 * 2**20),
        cost_estimate=pl.CostEstimate(
            flops=2 * row_count * blocks * BLK * TILE * width,
            bytes_accessed=row_count * blocks * BLK * 2 * (TILE + width),
            transcendentals=0,
        ),
        name="product",
    )(rows, ids, norms, *pieces, every_grad)


def shift(block, distance):
    size = lax.axis_size("dp")
    return lax.ppermute(block, "dp", [(i, (i + distance) % size) for i in range(size)])


def body(hidden, grad_out, segment):
    row_count = lax.axis_size("dp")
    blocks = lax.axis_size("ctx")
    tokens, width_hidden = hidden.shape[1:]
    width_grad = grad_out.shape[2]
    me = lax.axis_index("dp")
    rows = lax.rem(me + jnp.array([0, 3, 1, 2], jnp.int32), row_count)

    quarters = grad_out[0].reshape(tokens, row_count, -1).transpose(1, 0, 2)
    quarters = lax.all_to_all(quarters, "dp", 0, 0, tiled=True)
    every_grad = lax.all_gather(quarters, "ctx", axis=0, tiled=False)

    columns = hidden[0].reshape(tokens, blocks, -1).transpose(1, 0, 2)
    own = lax.all_to_all(columns, "ctx", 0, 0, tiled=True)
    below = shift(own, 1)
    above = shift(own, -1)
    far_low = shift(below[: blocks // 2], 1)
    far_high = shift(above[blocks // 2 :], -1)

    ids, own = lax.optimization_barrier((segment, own))
    ids = jnp.broadcast_to(ids[None], (row_count * blocks, 1, tokens))
    ids = lax.all_to_all(ids, ("dp", "ctx"), 0, 0, tiled=True)

    zero = jnp.zeros((row_count * DOCS, tokens), jnp.float32)
    early = gram(rows[:3], ids, (1, 1, 1), (own, below, above), every_grad, zero, False)
    partial = gram(rows[3:], ids, (2,), (far_low, far_high), every_grad, early, True)
    norms = lax.all_to_all(partial, ("dp", "ctx"), 0, 0, tiled=True)

    bound = math.sqrt(tokens * width_hidden * width_grad)
    return product(
        rows,
        ids,
        norms,
        (1, 1, 1, 2),
        (own, below, above, far_low, far_high),
        every_grad,
        bound,
    )


def solution(mesh):
    in_specs = (P("dp", "ctx", None), P("dp", "ctx", None), P("dp", "ctx"))
    out_specs = P("ctx", "dp")
    return jax.shard_map(body, mesh=mesh, in_specs=in_specs, out_specs=out_specs, check_vma=False)
```

time: 413 us -> 251 us (0.61)
  waiting for transfers between devices: 168 us -> 38.8 us
  Pallas kernels: 0 us -> 95.1 us
  other arithmetic: 59.7 us -> 0.01 us
  blocking collectives: 111 us -> 75.7 us
  matrix products: 15.8 us -> 0 us
  local copies, waits for them, and re-layouts: 29.5 us -> 14.7 us
    pallas_call x0 -> x3, Pallas kernels: none -> 95.1 us  [the longest x2 58.3 us: gram(): pl.pallas_call(functools.partial(gram_kernel, parts, finish), out_shape=j...]
    all_gather x2 -> x1, waiting for transfers between devices: 92.9 us -> 1.02 us  [body(): every_grad = lax.all_gather(quarters, 'ctx', axis=0, tiled=False)]
    psum x1 -> x0, blocking collectives: 61.6 us -> none  [body(): doc_norms = lax.psum(partial_norms, 'ctx')]
    unnamed x2 -> x0, other arithmetic: 59.4 us -> none
    ppermute x6 -> x4, waiting for transfers between devices: 74.6 us -> 37.8 us  [shift(): lax.ppermute(block, 'dp', [(i, (i + distance) % size) for i in range(size)])]
    all_to_all x2 -> x3, blocking collectives: 49.5 us -> 75.7 us  [the longest x1 44.4 us: body(): own = lax.all_to_all(columns, 'ctx', 0, 0, tiled=True)]
    unnamed x14 -> x6, local copies, waits for them, and re-layouts: 24.6 us -> 4.64 us
    dot_general x9 -> x0, matrix products: 15.8 us -> none  [the longest x1 12.2 us: body(): jnp.einsum('rtf,rtd->fd', every_hidden, lax.all_gather(split_scaled, 'ctx...]
  transfers between devices with their start and end apart: 8 -> 6, of which waited for: 3 -> 2; matrix products, arithmetic and copies ran while one was open for 5% -> 5% of each run, Pallas kernels for 0% -> 17%
where the time goes in v1:
time: 251 us; the launch traced here: 249 us
  Pallas kernels  95.1 us (38%)
  blocking collectives  75.7 us (30%)
  waiting for transfers between devices  38.8 us (15%)
  local copies, waits for them, and re-layouts  14.7 us (6%)
  between operations  13.5 us (5%)
  starting transfers between devices  11.1 us (4%)
    pallas_call x2, Pallas kernels, gram(): pl.pallas_call(functools.partial(gram_kernel, parts, finish), out_shape=j...  58.3 us
    all_to_all x1, blocking collectives, body(): own = lax.all_to_all(columns, 'ctx', 0, 0, tiled=True)  44.4 us
    ppermute x4, waiting for transfers between devices, shift(): lax.ppermute(block, 'dp', [(i, (i + distance) % size) for i in range(size)])  37.8 us
    pallas_call x1, Pallas kernels, product(): pl.pallas_call(functools.partial(product_kernel, parts, bound), out_shape...  36.7 us
    all_to_all x1, blocking collectives, body(): norms = lax.all_to_all(partial, ('dp', 'ctx'), 0, 0, tiled=True)  16.5 us
    all_to_all x1, blocking collectives, body(): quarters = lax.all_to_all(quarters, 'dp', 0, 0, tiled=True)  14.8 us
    all_to_all x1, starting transfers between devices, body(): ids = lax.all_to_all(ids, ('dp', 'ctx'), 0, 0, tiled=True)  5.73 us
    ppermute x4, starting transfers between devices, shift(): lax.ppermute(block, 'dp', [(i, (i + distance) % size) for i in range(size)])  5.39 us
  transfers between devices with their start and end apart: 6, of which 2 were waited for; matrix products, arithmetic and copies ran while one was open for 5% of the time, Pallas kernels for 17%

profile of v1, /device:TPU:1, one launch (start us, length us, event | category | flops | bytes accessed | tf_op | source)
XLA Modules:
  0.0 248.8 jit_solution(3278532544147880549)
XLA Ops:
  6.5 0.0 all-gather.3.cloned.1.call-start
  6.5 1.4 copy.13
  7.9 14.8 %all_to_all.20 = bf16[4,128,640]{1,2,0:T(8,128)(2,1)S(1)} all-to-all(bf16[4,128,640]{1,2,0:T(8,128)(2,1)S(1)} %bitcast.14), channel_id=1, replica_groups=mesh['dp'=4,'ctx'=32] {'dp'}, dimensions={0} | all-to-all | bytes 1310720 | tf_op jit(solution)/shard_map/all_to_all | solution.py:222
  22.7 1.1 copy.14
  23.8 0.0 all-gather.3.cloned.1.call-update
  23.8 3.2 %copy.11 = bf16[1,128,8192]{1,2,0:T(8,128)(2,1)S(1)} copy(bf16[1,128,8192]{2,1,0:T(8,128)(2,1)} %param.4) | data formatting | bytes 4194304 | tf_op args[0]
  27.1 2.9 %copy.12 = bf16[128,32,256]{2,0,1:T(8,128)(2,1)} copy(bf16[128,32,256]{0,2,1:T(8,128)(2,1)S(1)} %bitcast.13) | data formatting | bytes 4194304 | tf_op jit(solution)/shard_map/reshape;squeeze | solution.py:225
  30.0 0.0 copy-start
  30.0 0.0 copy-start.1
  30.0 44.4 %all_to_all.21.refs_0_ = bf16[32,128,256]{2,1,0:T(8,128)(2,1)S(1)} all-to-all(bf16[32,128,256]{2,1,0:T(8,128)(2,1)} %bitcast.12), channel_id=1, replica_groups=mesh['dp'=4,'ctx'=32] {'ctx'}, dimensions={0} | all-to-all | bytes 4194304 | tf_op jit(solution)/shard_map/all_to_all | solution.py:226
  74.4 1.2 collective-permute-start
  75.5 1.5 collective-permute-start.2
  77.0 0.0 copy-done
  77.0 0.7 broadcast_in_dim.12
  77.7 5.7 %all-to-all-start.1 = ((s32[128,1,128]{2,1,0:T(1,128)}), s32[128,1,128]{2,1,0:T(1,128)S(1)}, u32[]{:S(2)}, u32[]{:S(2)}) async-start(s32[128,1,128]{2,1,0:T(1,128)} %broadcast_in_dim.12), calls=%async_computation.1 | async-start | bytes 131072 | tf_op jit(solution)/shard_map/all_to_all | solution.py:234
  83.4 0.0 copy-done.1
  83.5 0.6 slice.12.rows_ref
  84.1 37.8 %collective-permute-done.refs_1_ = bf16[32,128,256]{2,1,0:T(8,128)(2,1)} collective-permute-done((bf16[32,128,256]{2,1,0:T(8,128)(2,1)S(1)}, bf16[32,128,256]{2,1,0:T(8,128)(2,1)}, u32[]{:S(2)}, u32[]{:S(2)}) %collective-permute-start) | collective-permute-done | bytes 2097184 | tf_op jit(solution)/shard_map/ppermute | solution.py:210
  121.9 2.3 slice.16
  124.2 0.0 collective-permute-start.1
  124.2 0.0 collective-permute-done.2.refs_2_
  124.2 2.5 slice.17
  126.6 2.7 %collective-permute-start.3 = (bf16[16,128,256]{2,1,0:T(8,128)(2,1)}, bf16[16,128,256]{2,1,0:T(8,128)(2,1)}, u32[]{:S(2)}, u32[]{:S(2)}) collective-permute-start(bf16[16,128,256]{2,1,0:T(8,128)(2,1)} %slice.17), channel_id=1, source_target_pairs={{0,96},{32,0},{64,32},{96,64},{1,97},{33,1},{65,33},{97,65},{2,98}... | collective-permute-start | bytes 3145736 | tf_op jit(solution)/shard_map/ppermute | solution.py:210
  129.4 0.0 all-to-all-done.1.ids_ref
  129.4 1.0 all-gather.3.cloned.1.call-done
  130.4 43.1 %gram.2.refs_3_ = f32[128,128]{1,0:T(8,128)S(1)} custom-call(s32[3]{0:T(128)S(1)} %bitcast.8, s32[128,1,128]{2,1,0:T(1,128)S(1)} %all-to-all-done.1.ids_ref, bf16[32,128,256]{2,1,0:T(8,128)(2,1)S(1)} %all_to_all.21.refs_0_, bf16[32,128,256]{2,1,0:T(8,128)(2,1)} %collective-permute-done.refs_1_, bf16[32,128,256]{2,1,0:T(8,128)(2,1)} %collective-permute-done.2.refs_2_, ...), custom_call_target="tpu_custom_call" | custom-call | flops 11274289152 | bytes 22020096 | tf_op jit(solution)/shard_map/gram/pallas_call | solution.py:100
  173.5 0.0 collective-permute-done.1.refs_0_.refs_3_
  173.5 0.0 collective-permute-done.3.refs_1_.refs_4_
  173.5 15.2 %gram.3 = f32[128,1,128]{2,1,0:T(1,128)S(1)} custom-call(s32[1]{0:T(128)} %slice.12.rows_ref, s32[128,1,128]{2,1,0:T(1,128)S(1)} %all-to-all-done.1.ids_ref, bf16[16,128,256]{2,1,0:T(8,128)(2,1)S(1)} %collective-permute-done.1.refs_0_.refs_3_, bf16[16,128,256]{2,1,0:T(8,128)(2,1)} %collective-permute-done.3.refs_1_.refs_4_, ...), custom_call_target="tpu_custom_call" | custom-call | flops 3758096384 | bytes 7340032 | tf_op jit(solution)/shard_map/gram/pallas_call | solution.py:100
  188.7 16.5 %all_to_all.22.norms_ref = f32[128,1,128]{2,1,0:T(1,128)S(1)} all-to-all(f32[128,1,128]{2,1,0:T(1,128)S(1)} %gram.3), channel_id=1, replica_groups=mesh['dp'=4,'ctx'=32] {'dp','ctx'}, dimensions={0} | all-to-all | bytes 131072 | tf_op jit(solution)/shard_map/all_to_all | solution.py:239
  205.3 36.7 %product.1 = f32[256,640]{1,0:T(8,128)} custom-call(s32[4]{0:T(128)S(1)} %compare_select_fusion.rows_ref, s32[128,1,128]{2,1,0:T(1,128)S(1)} %all-to-all-done.1.ids_ref, f32[128,1,128]{2,1,0:T(1,128)S(1)} %all_to_all.22.norms_ref, bf16[32,128,256]{2,1,0:T(8,128)(2,1)S(1)} %all_to_all.21.refs_0_, bf16[32,128,256]{2,1,0:T(8,128)(2,1)} %collective-permute-done.refs_1_, ...), custom_call_target="tpu_custom_call" | custom-call | flops 5368709120 | bytes 29360128 | tf_op jit(solution)/shard_map/product/pallas_call | solution.py:180
  (2 shorter events, 0.0 us)
Async XLA Ops:
  6.5 123.8 %all-gather.3.cloned.1.call-start = ((), (), s32[]{:S(2)}) async-start(), calls=%async_computation.4 | async-start | bytes 21626880 | tf_op jit(solution)/shard_map/all_gather | solution.py:223
  30.0 47.1 %copy-start = (s32[1,128]{1,0:T(1,128)S(1)}, s32[1,128]{1,0:T(1,128)}, u32[]{:S(2)}) copy-start(s32[1,128]{1,0:T(1,128)} %param.6) | copy-start | bytes 1540
  30.0 53.5 %copy-start.1 = (s32[4]{0:T(128)S(1)}, s32[4]{0:T(128)}, u32[]{:S(2)}) copy-start(s32[4]{0:T(128)} %constant.15.clone) | copy-start | bytes 52
  74.4 47.5 %collective-permute-start = (bf16[32,128,256]{2,1,0:T(8,128)(2,1)S(1)}, bf16[32,128,256]{2,1,0:T(8,128)(2,1)}, u32[]{:S(2)}, u32[]{:S(2)}) collective-permute-start(bf16[32,128,256]{2,1,0:T(8,128)(2,1)S(1)} %all_to_all.21.refs_0_), channel_id=1, source_target_pairs={{0,32},{32,64},{64,96},{96,0},{1,33},{33,65},{65,97},{97,1},{2,34}... | collective-permute-start | bytes 6291464 | tf_op jit(solution)/shard_map/ppermute | solution.py:210
  75.5 48.6 %collective-permute-start.2 = (bf16[32,128,256]{2,1,0:T(8,128)(2,1)S(1)}, bf16[32,128,256]{2,1,0:T(8,128)(2,1)}, u32[]{:S(2)}, u32[]{:S(2)}) collective-permute-start(bf16[32,128,256]{2,1,0:T(8,128)(2,1)S(1)} %all_to_all.21.refs_0_), channel_id=1, source_target_pairs={{0,96},{32,0},{64,32},{96,64},{1,97},{33,1},{65,33},{97,65},{2,98}... | collective-permute-start | bytes 6291464 | tf_op jit(solution)/shard_map/ppermute | solution.py:210
  77.7 51.7 %all-to-all-start.1 = ((s32[128,1,128]{2,1,0:T(1,128)}), s32[128,1,128]{2,1,0:T(1,128)S(1)}, u32[]{:S(2)}, u32[]{:S(2)}) async-start(s32[128,1,128]{2,1,0:T(1,128)} %broadcast_in_dim.12), calls=%async_computation.1 | async-start | bytes 131072 | tf_op jit(solution)/shard_map/all_to_all | solution.py:234
  124.2 49.3 %collective-permute-start.1 = (bf16[16,128,256]{2,1,0:T(8,128)(2,1)}, bf16[16,128,256]{2,1,0:T(8,128)(2,1)S(1)}, u32[]{:S(2)}, u32[]{:S(2)}) collective-permute-start(bf16[16,128,256]{2,1,0:T(8,128)(2,1)} %slice.16), channel_id=1, source_target_pairs={{0,32},{32,64},{64,96},{96,0},{1,33},{33,65},{65,97},{97,1},{2,34}... | collective-permute-start | bytes 3145736 | tf_op jit(solution)/shard_map/ppermute | solution.py:210
  126.6 46.9 %collective-permute-start.3 = (bf16[16,128,256]{2,1,0:T(8,128)(2,1)}, bf16[16,128,256]{2,1,0:T(8,128)(2,1)}, u32[]{:S(2)}, u32[]{:S(2)}) collective-permute-start(bf16[16,128,256]{2,1,0:T(8,128)(2,1)} %slice.17), channel_id=1, source_target_pairs={{0,96},{32,0},{64,32},{96,64},{1,97},{33,1},{65,33},{97,65},{2,98}... | collective-permute-start | bytes 3145736 | tf_op jit(solution)/shard_map/ppermute | solution.py:210
Sparse Core Ops, SparseCore 0:
  24.0 106.3 all-gather.2

commit v2 on v0

v2 whole, which is shorter than its diff:
```python
import functools
import math

import jax
import jax.numpy as jnp
from jax import lax
from jax.experimental import pallas as pl
from jax.experimental.pallas import tpu as pltpu
from jax.sharding import PartitionSpec as P

BLK = 128
TILE = 256
DOCS = 32
GROUP = 2

NT = (((1,), (1,)), ((), ()))


def flat(ref, at, count):
    return ref[at : at + count].reshape(count * BLK, ref.shape[2])


def gram_kernel(nrows, tiles, finish, rows_ref, ids_ref, first_ref, *refs):
    per_row = 6
    row_refs = [refs[k * per_row : (k + 1) * per_row] for k in range(nrows)]
    init_ref, out_ref, h_prev, g_prev, acc = refs[nrows * per_row :]
    step = pl.program_id(0)
    steps = pl.num_programs(0)

    @pl.when(step == 0)
    def _():
        acc[...] = init_ref[...]
        for k in range(nrows):
            h_last, g_last = row_refs[k][4:]
            h_prev[k, 0] = jnp.zeros_like(h_prev[k, 0])
            g_prev[k, 0] = jnp.zeros_like(g_prev[k, 0])
            h_prev[k, 1] = flat(h_last, 0, 2)
            g_prev[k, 1] = flat(g_last, 0, 2)

    place = lax.broadcasted_iota(jnp.int32, (TILE, TILE), 0)
    column = lax.broadcasted_iota(jnp.int32, (TILE, TILE), 1)
    triangle = jnp.where(
        place < column, jnp.float32(2.0), jnp.where(place == column, jnp.float32(1.0), jnp.float32(0.0))
    )
    docs = lax.broadcasted_iota(jnp.int32, (DOCS, TILE), 0)
    for k in range(nrows):
        base = rows_ref[k]
        share = jnp.zeros((DOCS, BLK), jnp.float32)
        for half in range(2):
            h_ref, g_ref = row_refs[k][2 * half : 2 * half + 2]
            old_h = h_prev[k, half]
            old_g = g_prev[k, half]
            for t in range(tiles):
                number = half * steps * tiles + step * tiles + t
                at = base * (2 * steps * tiles * 2) + 2 * number
                ids = jnp.concatenate([ids_ref[at], ids_ref[at + 1]], axis=1)
                first = jnp.concatenate([first_ref[at], first_ref[at + 1]], axis=1) - number * TILE
                own_h = flat(h_ref, 2 * t, 2)
                own_g = flat(g_ref, 2 * t, 2)
                dot = functools.partial(
                    lax.dot_general, dimension_numbers=NT, preferred_element_type=jnp.float32
                )
                pairs = dot(own_h, own_h) * dot(own_g, own_g) * triangle
                pairs = jnp.where(place >= first, pairs, jnp.float32(0.0))
                far = dot(old_h, own_h) * dot(old_g, own_g)
                far = jnp.where(place >= first + TILE, far, jnp.float32(0.0))
                total = jnp.sum(pairs + 2.0 * far, axis=0, keepdims=True)
                terms = jnp.where(docs == ids, jnp.broadcast_to(total, docs.shape), jnp.float32(0.0))
                share += terms[:, :BLK] + terms[:, BLK:]
                old_h, old_g = own_h, own_g
            h_prev[k, half] = old_h
            g_prev[k, half] = old_g
        here = pl.ds(pl.multiple_of(base * DOCS, DOCS), DOCS)
        acc[here, :] += share

    @pl.when(step == steps - 1)
    def _():
        if finish:
            sums = jnp.sum(acc[...].T, axis=0, keepdims=True)
            out_ref[...] = jnp.broadcast_to(sums[None], out_ref.shape)
        else:
            out_ref[...] = acc[...]


def gram(rows, ids, first, tiles, pieces, init, finish):
    blocks, _, _, width = pieces[0][2].shape
    row_docs = init.shape[0]
    steps = blocks // (4 * tiles)
    shape = (ids.shape[0], 1, BLK) if finish else init.shape
    whole = pl.BlockSpec(ids.shape, lambda i, r: (0, 0, 0))
    specs, operands = [], []
    for h_halves, row, grad in pieces:
        low, high = h_halves
        offset = steps if low is high else 0
        specs += [
            pl.BlockSpec((2 * tiles, BLK, TILE), lambda i, r: (i, 0, 0)),
            pl.BlockSpec((2 * tiles, None, BLK, width), lambda i, r, row=row: (i, row, 0, 0)),
            pl.BlockSpec((2 * tiles, BLK, TILE), lambda i, r, offset=offset: (i + offset, 0, 0)),
            pl.BlockSpec((2 * tiles, None, BLK, width), lambda i, r, row=row: (i + steps, row, 0, 0)),
            pl.BlockSpec((2, BLK, TILE), lambda i, r: (steps * tiles - 1, 0, 0)),
            pl.BlockSpec((2, None, BLK, width), lambda i, r, row=row: (steps * tiles - 1, row, 0, 0)),
        ]
        operands += [low, grad, high, grad, low, grad]
    nrows = len(pieces)
    return pl.pallas_call(
        functools.partial(gram_kernel, nrows, tiles, finish),
        out_shape=jax.ShapeDtypeStruct(shape, jnp.float32),
        grid_spec=pltpu.PrefetchScalarGridSpec(
            num_scalar_prefetch=1,
            grid=(steps,),
            in_specs=[whole, whole, *specs, pl.BlockSpec((row_docs, BLK), lambda i, r: (0, 0))],
            out_specs=pl.BlockSpec(shape, lambda i, r: (0,) * len(shape)),
            scratch_shapes=[
                pltpu.VMEM((nrows, 2, TILE, TILE), jnp.bfloat16),
                pltpu.VMEM((nrows, 2, TILE, width), jnp.bfloat16),
                pltpu.VMEM((row_docs, BLK), jnp.float32),
            ],
        ),
        compiler_params=pltpu.CompilerParams(vmem_limit_bytes=32 * 2**20),
        cost_estimate=pl.CostEstimate(
            flops=nrows * blocks * BLK * 4 * TILE * (TILE + width),
            bytes_accessed=nrows * blocks * BLK * 2 * (TILE + width),
            transcendentals=0,
        ),
        name="gram",
    )(rows, ids, first, *operands, init)


def product_kernel(nrows, bound, rows_ref, ids_ref, norms_ref, *refs):
    per_row = 4
    row_refs = [refs[k * per_row : (k + 1) * per_row] for k in range(nrows)]
    out_ref, factor, turned, scaled = refs[nrows * per_row :]
    step = pl.program_id(0)
    steps = pl.num_programs(0)
    groups = factor.shape[0]
    per_group = groups // nrows

    @pl.when(step == 0)
    def _():
        norms = jnp.sum(norms_ref[...], axis=0)
        clip = bound / jnp.maximum(jnp.sqrt(norms), bound) / nrows
        for k in range(nrows):
            span = slice(k * per_group, (k + 1) * per_group)
            ids = ids_ref[span, 0, :] + k * DOCS
            table = jnp.broadcast_to(clip, ids.shape)
            factor[span, :] = jnp.take_along_axis(table, ids, axis=1)

    lines = []
    for k in range(nrows):
        for half in range(2):
            for j in range(GROUP):
                at = rows_ref[k] * per_group + half * (per_group // 2) + step * GROUP + j
                lines.append(factor[pl.ds(at, 1), :])
    used = len(lines)
    lines = jnp.concatenate(lines + [jnp.zeros((BLK - used, BLK), jnp.float32)], axis=0).T
    at = 0
    for k in range(nrows):
        for half in range(2):
            h_ref, g_ref = row_refs[k][2 * half : 2 * half + 2]
            for j in range(GROUP):
                scale = jnp.broadcast_to(lines[:, at : at + 1], (BLK, BLK))
                here = slice(at * BLK, (at + 1) * BLK)
                for c in range(0, g_ref.shape[2], BLK):
                    scaled[here, c : c + BLK] = (
                        g_ref[j, :, c : c + BLK].astype(jnp.float32) * scale
                    ).astype(jnp.bfloat16)
                turned[:, here] = h_ref[j].T
                at += 1
    result = jnp.dot(turned[...], scaled[...], preferred_element_type=jnp.float32)

    @pl.when(step == 0)
    def _():
        out_ref[...] = result

    @pl.when(step > 0)
    def _():
        out_ref[...] += result


def product(rows, ids, norms, pieces, bound):
    blocks, _, _, width = pieces[0][2].shape
    steps = blocks // (2 * GROUP)
    nrows = len(pieces)
    whole = pl.BlockSpec(ids.shape, lambda i, r: (0, 0, 0))
    specs, operands = [], []
    for h_halves, row, grad in pieces:
        low, high = h_halves
        offset = steps if low is high else 0
        specs += [
            pl.BlockSpec((GROUP, BLK, TILE), lambda i, r: (i, 0, 0)),
            pl.BlockSpec((GROUP, None, BLK, width), lambda i, r, row=row: (i, row, 0, 0)),
            pl.BlockSpec((GROUP, BLK, TILE), lambda i, r, offset=offset: (i + offset, 0, 0)),
            pl.BlockSpec((GROUP, None, BLK, width), lambda i, r, row=row: (i + steps, row, 0, 0)),
        ]
        operands += [low, grad, high, grad]
    depth = nrows * 2 * GROUP * BLK
    return pl.pallas_call(
        functools.partial(product_kernel, nrows, bound),
        out_shape=jax.ShapeDtypeStruct((TILE, width), jnp.float32),
        grid_spec=pltpu.PrefetchScalarGridSpec(
            num_scalar_prefetch=1,
            grid=(steps,),
            in_specs=[whole, whole, *specs],
            out_specs=pl.BlockSpec((TILE, width), lambda i, r: (0, 0)),
            scratch_shapes=[
                pltpu.VMEM((nrows * blocks, BLK), jnp.float32),
                pltpu.VMEM((TILE, depth), jnp.bfloat16),
                pltpu.VMEM((depth, width), jnp.bfloat16),
            ],
        ),
        compiler_params=pltpu.CompilerParams(vmem_limit_bytes=32 * 2**20),
        cost_estimate=pl.CostEstimate(
            flops=2 * nrows * blocks * BLK * TILE * width,
            bytes_accessed=nrows * blocks * BLK * 2 * (TILE + width),
            transcendentals=0,
        ),
        name="product",
    )(rows, ids, norms, *operands)


def shift(block, distance):
    size = lax.axis_size("dp")
    return lax.ppermute(block, "dp", [(i, (i + distance) % size) for i in range(size)])


def starts(ids, row_count):
    by_row = ids.reshape(row_count, -1)
    docs = jnp.arange(DOCS, dtype=jnp.int32)
    before = jnp.sum((by_row[:, None, :] < docs[None, :, None]).astype(jnp.int32), axis=2)
    own = by_row[:, None, :] == docs[None, :, None]
    return jnp.sum(jnp.where(own, before[:, :, None], 0), axis=1).reshape(ids.shape)


def body(hidden, grad_out, segment):
    row_count = lax.axis_size("dp")
    blocks = lax.axis_size("ctx")
    tokens, width_hidden = hidden.shape[1:]
    width_grad = grad_out.shape[2]
    me = lax.axis_index("dp")
    rows = lax.rem(me + jnp.array([0, 3, 1, 2], jnp.int32), row_count)

    quarters = grad_out[0].reshape(tokens, row_count, -1).transpose(1, 0, 2)
    send = lambda d: shift(lax.dynamic_index_in_dim(quarters, lax.rem(me + d + 4, 4), 0, False), d)
    mine = [lax.dynamic_index_in_dim(quarters, me, 0, False), send(1), send(-1), send(2)]
    every_grad = lax.all_gather(jnp.stack(mine), "ctx", axis=0, tiled=False)

    columns = hidden[0].reshape(tokens, blocks, -1).transpose(1, 0, 2)
    own = lax.all_to_all(columns, "ctx", 0, 0, tiled=True)
    below = shift(own, 1)
    above = shift(own, -1)
    far_low = shift(below[: blocks // 2], 1)
    far_high = shift(above[blocks // 2 :], -1)

    ids, own = lax.optimization_barrier((segment, own))
    ids = jnp.broadcast_to(ids[None], (row_count * blocks, 1, tokens))
    ids = lax.all_to_all(ids, ("dp", "ctx"), 0, 0, tiled=True)
    first = starts(ids, row_count)

    pieces = [
        ((own, own), 0, every_grad),
        ((below, below), 1, every_grad),
        ((above, above), 2, every_grad),
        ((far_low, far_high), 3, every_grad),
    ]
    zero = jnp.zeros((row_count * DOCS, tokens), jnp.float32)
    early = gram(rows[:3], ids, first, 1, pieces[:3], zero, False)
    partial = gram(rows[3:], ids, first, 2, pieces[3:], early, True)
    norms = lax.all_to_all(partial, ("dp", "ctx"), 0, 0, tiled=True)

    bound = math.sqrt(tokens * width_hidden * width_grad)
    return product(rows, ids, norms, pieces, bound)


def solution(mesh):
    in_specs = (P("dp", "ctx", None), P("dp", "ctx", None), P("dp", "ctx"))
    out_specs = P("ctx", "dp")
    return jax.shard_map(body, mesh=mesh, in_specs=in_specs, out_specs=out_specs, check_vma=False)
```

time: 413 us -> 207 us (0.50)
  waiting for transfers between devices: 168 us -> 49.6 us
  other arithmetic: 59.7 us -> 2.61 us
  blocking collectives: 111 us -> 63.4 us
  Pallas kernels: 0 us -> 45.8 us
  matrix products: 15.8 us -> 0 us
  local copies, waits for them, and re-layouts: 29.5 us -> 14.8 us
    all_gather x2 -> x1, waiting for transfers between devices: 92.9 us -> 0.01 us  [body(): every_grad = lax.all_gather(jnp.stack(mine), 'ctx', axis=0, tiled=False)]
    ppermute x6 -> x7, waiting for transfers between devices: 74.6 us -> 7.65 us  [shift(): lax.ppermute(block, 'dp', [(i, (i + distance) % size) for i in range(size)])]
    psum x1 -> x0, blocking collectives: 61.6 us -> none  [body(): doc_norms = lax.psum(partial_norms, 'ctx')]
    unnamed x2 -> x0, other arithmetic: 59.4 us -> none
    pallas_call x0 -> x3, Pallas kernels: none -> 45.8 us  [the longest x2 28.4 us: gram(): pl.pallas_call(functools.partial(gram_kernel, nrows, tiles, finish), out_...]
    all_to_all x0 -> x1, waiting for transfers between devices: none -> 41.9 us  [body(): ids = lax.all_to_all(ids, ('dp', 'ctx'), 0, 0, tiled=True)]
    unnamed x14 -> x6, local copies, waits for them, and re-layouts: 24.6 us -> 4.64 us
    dot_general x9 -> x0, matrix products: 15.8 us -> none  [the longest x1 12.2 us: body(): jnp.einsum('rtf,rtd->fd', every_hidden, lax.all_gather(split_scaled, 'ctx...]
  transfers between devices with their start and end apart: 8 -> 9, of which waited for: 3 -> 5; matrix products, arithmetic and copies ran while one was open for 5% -> 7% of each run, Pallas kernels for 0% -> 10%
where the time goes in v2:
time: 207 us; the launch traced here: 206 us
  blocking collectives  63.4 us (31%)
  waiting for transfers between devices  49.6 us (24%)
  Pallas kernels  45.8 us (22%)
  starting transfers between devices  16.6 us (8%)
  local copies, waits for them, and re-layouts  14.8 us (7%)
  between operations  13.5 us (7%)
  other arithmetic  2.61 us (1%)
    all_to_all x1, blocking collectives, body(): own = lax.all_to_all(columns, 'ctx', 0, 0, tiled=True)  45.7 us
    all_to_all x1, waiting for transfers between devices, body(): ids = lax.all_to_all(ids, ('dp', 'ctx'), 0, 0, tiled=True)  41.9 us
    pallas_call x2, Pallas kernels, gram(): pl.pallas_call(functools.partial(gram_kernel, nrows, tiles, finish), out_...  28.4 us
    all_to_all x1, blocking collectives, body(): norms = lax.all_to_all(partial, ('dp', 'ctx'), 0, 0, tiled=True)  17.8 us
    pallas_call x1, Pallas kernels, product(): pl.pallas_call(functools.partial(product_kernel, nrows, bound), out_shape...  17.4 us
    ppermute x7, starting transfers between devices, shift(): lax.ppermute(block, 'dp', [(i, (i + distance) % size) for i in range(size)])  10.8 us
    ppermute x7, waiting for transfers between devices, shift(): lax.ppermute(block, 'dp', [(i, (i + distance) % size) for i in range(size)])  7.65 us
    all_to_all x1, starting transfers between devices, body(): ids = lax.all_to_all(ids, ('dp', 'ctx'), 0, 0, tiled=True)  5.78 us
  transfers between devices with their start and end apart: 9, of which 5 were waited for; matrix products, arithmetic and copies ran while one was open for 7% of the time, Pallas kernels for 10%

profile of v2, /device:TPU:1, one launch (start us, length us, event | category | flops | bytes accessed | tf_op | source)
XLA Modules:
  0.0 206.2 jit_solution(12606800426856283744)
XLA Ops:
  6.5 0.0 all-gather.3.cloned.1.call-start
  6.5 1.4 copy.23
  8.0 0.1 constant_dynamic-slice_fusion.3
  8.0 0.2 copy.27
  8.2 3.8 %collective-permute-start.4 = (bf16[128,640]{1,0:T(8,128)(2,1)S(1)}, bf16[128,640]{1,0:T(8,128)(2,1)S(1)}, u32[]{:S(2)}, u32[]{:S(2)}) collective-permute-start(bf16[128,640]{1,0:T(8,128)(2,1)S(1)} %bitcast.41), channel_id=1, source_target_pairs={{0,64},{32,96},{64,0},{96,32},{1,65},{33,97},{65,1},{97,33},{2,66}... | collective-permute-start | bytes 491528 | tf_op jit(solution)/shard_map/ppermute | solution.py:223
  12.0 0.2 copy.26
  12.2 0.8 collective-permute-start.3
  13.0 0.2 copy.25
  13.2 0.8 collective-permute-start.2
  13.9 0.2 copy.24
  14.1 1.6 collective-permute-done.4
  15.7 3.9 %collective-permute-done.3 = bf16[128,640]{1,0:T(8,128)(2,1)S(1)} collective-permute-done((bf16[128,640]{1,0:T(8,128)(2,1)S(1)}, bf16[128,640]{1,0:T(8,128)(2,1)S(1)}, u32[]{:S(2)}, u32[]{:S(2)}) %collective-permute-start.3) | collective-permute-done | bytes 163872 | tf_op jit(solution)/shard_map/ppermute | solution.py:223
  19.6 0.0 collective-permute-done.2
  19.6 0.9 pad_maximum_fusion
  20.5 0.0 all-gather.3.cloned.1.call-update
  20.5 3.2 %copy.21 = bf16[1,128,8192]{1,2,0:T(8,128)(2,1)S(1)} copy(bf16[1,128,8192]{2,1,0:T(8,128)(2,1)} %param.4) | data formatting | bytes 4194304 | tf_op args[0]
  23.8 2.9 %copy.22 = bf16[128,32,256]{2,0,1:T(8,128)(2,1)} copy(bf16[128,32,256]{0,2,1:T(8,128)(2,1)S(1)} %bitcast.35) | data formatting | bytes 4194304 | tf_op jit(solution)/shard_map/reshape;squeeze | solution.py:247
  26.7 0.0 copy-start
  26.7 0.0 copy-start.1
  26.7 45.7 %all_to_all.15.refs_0_.refs_2_.refs_4_ = bf16[32,128,256]{2,1,0:T(8,128)(2,1)S(1)} all-to-all(bf16[32,128,256]{2,1,0:T(8,128)(2,1)} %bitcast.34), channel_id=1, replica_groups=mesh['dp'=4,'ctx'=32] {'ctx'}, dimensions={0} | all-to-all | bytes 4194304 | tf_op jit(solution)/shard_map/all_to_all | solution.py:248
  72.3 1.2 collective-permute-start
  73.5 1.5 collective-permute-start.5
  75.0 0.0 copy-done
  75.0 0.7 broadcast_in_dim.27
  75.7 5.8 %all-to-all-start.1 = ((s32[128,1,128]{2,1,0:T(1,128)}), s32[128,1,128]{2,1,0:T(1,128)S(1)}, u32[]{:S(2)}, u32[]{:S(2)}) async-start(s32[128,1,128]{2,1,0:T(1,128)} %broadcast_in_dim.27), calls=%async_computation.1 | async-start | bytes 131072 | tf_op jit(solution)/shard_map/all_to_all | solution.py:256
  81.5 0.0 copy-done.1
  81.5 0.6 slice.12.rows_ref
  82.1 41.9 %all-to-all-done.1.ids_ref = s32[128,1,128]{2,1,0:T(1,128)S(1)} async-done(((s32[128,1,128]{2,1,0:T(1,128)}), s32[128,1,128]{2,1,0:T(1,128)S(1)}, u32[]{:S(2)}, u32[]{:S(2)}) %all-to-all-start.1) | async-done | bytes 65568 | tf_op jit(solution)/shard_map/all_to_all | solution.py:256
  124.0 0.6 broadcast.15
  124.6 0.8 reduce.3
  125.4 0.4 convert_reduce_fusion
  125.8 0.5 select_reduce_fusion
  126.3 0.1 reshape.15.first_ref
  126.4 0.0 collective-permute-done.refs_6_.refs_8_.refs_10_.refs_4_
  126.4 2.3 %slice.16 = bf16[16,128,256]{2,1,0:T(8,128)(2,1)} slice(bf16[32,128,256]{2,1,0:T(8,128)(2,1)} %collective-permute-done.refs_6_.refs_8_.refs_10_.refs_4_), slice={[0:16], [0:128], [0:256]} | slice | bytes 2097152 | tf_op jit(solution)/shard_map/slice | solution.py:251
  128.7 1.0 collective-permute-start.1
  129.7 0.0 collective-permute-done.5.refs_12_.refs_14_.refs_16_.refs_8_.refs_10_
  129.7 2.3 %slice.17 = bf16[16,128,256]{2,1,0:T(8,128)(2,1)} slice(bf16[32,128,256]{2,1,0:T(8,128)(2,1)} %collective-permute-done.5.refs_12_.refs_14_.refs_16_.refs_8_.refs_10_), slice={[16:32], [0:128], [0:256]} | slice | bytes 2097152 | tf_op jit(solution)/shard_map/slice | solution.py:252
  132.0 1.6 collective-permute-start.6
  133.6 0.0 all-gather.3.cloned.1.call-done
  133.6 20.2 %gram.2.refs_6_ = f32[128,128]{1,0:T(8,128)S(1)} custom-call(s32[3]{0:T(128)S(1)} %bitcast.13, s32[128,1,128]{2,1,0:T(1,128)S(1)} %all-to-all-done.1.ids_ref, s32[128,1,128]{2,1,0:T(1,128)S(1)} %reshape.15.first_ref, bf16[32,128,256]{2,1,0:T(8,128)(2,1)S(1)} %all_to_all.15.refs_0_.refs_2_.refs_4_, bf16[32,4,128,640]{3,2,1,0:T(8,128)(2,1)} %bitcast.14, ...), custom_call_target="tpu_custom_call" | custom-call | flops 11274289152 | bytes 22020096 | tf_op jit(solution)/shard_map/gram/pallas_call | solution.py:105
  153.8 0.3 collective-permute-done.1.refs_0_.refs_4_.refs_12_
  154.1 1.9 collective-permute-done.6.refs_2_.refs_14_
  156.0 8.2 %gram.3 = f32[128,1,128]{2,1,0:T(1,128)S(1)} custom-call(s32[1]{0:T(128)} %slice.12.rows_ref, s32[128,1,128]{2,1,0:T(1,128)S(1)} %all-to-all-done.1.ids_ref, s32[128,1,128]{2,1,0:T(1,128)S(1)} %reshape.15.first_ref, bf16[16,128,256]{2,1,0:T(8,128)(2,1)S(1)} %collective-permute-done.1.refs_0_.refs_4_.refs_12_, bf16[32,4,128,640]{3,2,1,0:T(8,128)(2,1)} %bitcast.23, ...), custom_call_target="tpu_custom_call" | custom-call | flops 3758096384 | bytes 7340032 | tf_op jit(solution)/shard_map/gram/pallas_call | solution.py:105
  164.2 17.8 %all_to_all.16.norms_ref = f32[128,1,128]{2,1,0:T(1,128)S(1)} all-to-all(f32[128,1,128]{2,1,0:T(1,128)S(1)} %gram.3), channel_id=1, replica_groups=mesh['dp'=4,'ctx'=32] {'dp','ctx'}, dimensions={0} | all-to-all | bytes 131072 | tf_op jit(solution)/shard_map/all_to_all | solution.py:268
  182.0 17.4 %product.1 = f32[256,640]{1,0:T(8,128)} custom-call(s32[4]{0:T(128)S(1)} %compare_select_fusion.rows_ref, s32[128,1,128]{2,1,0:T(1,128)S(1)} %all-to-all-done.1.ids_ref, f32[128,1,128]{2,1,0:T(1,128)S(1)} %all_to_all.16.norms_ref, bf16[32,128,256]{2,1,0:T(8,128)(2,1)S(1)} %all_to_all.15.refs_0_.refs_2_.refs_4_, bf16[32,4,128,640]{3,2,1,0:T(8,128)(2,1)} %bitcast.26, ...), custom_call_target="tpu_custom_call" | custom-call | flops 5368709120 | bytes 29360128 | tf_op jit(solution)/shard_map/product/pallas_call | solution.py:197
  (3 shorter events, 0.0 us)
Async XLA Ops:
  6.5 127.1 %all-gather.3.cloned.1.call-start = ((), (), s32[]{:S(2)}) async-start(), calls=%async_computation.3 | async-start | bytes 21626880 | tf_op jit(solution)/shard_map/all_gather | solution.py:245
  8.2 7.5 %collective-permute-start.4 = (bf16[128,640]{1,0:T(8,128)(2,1)S(1)}, bf16[128,640]{1,0:T(8,128)(2,1)S(1)}, u32[]{:S(2)}, u32[]{:S(2)}) collective-permute-start(bf16[128,640]{1,0:T(8,128)(2,1)S(1)} %bitcast.41), channel_id=1, source_target_pairs={{0,64},{32,96},{64,0},{96,32},{1,65},{33,97},{65,1},{97,33},{2,66}... | collective-permute-start | bytes 491528 | tf_op jit(solution)/shard_map/ppermute | solution.py:223
  12.2 7.4 %collective-permute-start.3 = (bf16[128,640]{1,0:T(8,128)(2,1)S(1)}, bf16[128,640]{1,0:T(8,128)(2,1)S(1)}, u32[]{:S(2)}, u32[]{:S(2)}) collective-permute-start(bf16[128,640]{1,0:T(8,128)(2,1)S(1)} %bitcast.42), channel_id=1, source_target_pairs={{0,96},{32,0},{64,32},{96,64},{1,97},{33,1},{65,33},{97,65},{2,98}... | collective-permute-start | bytes 491528 | tf_op jit(solution)/shard_map/ppermute | solution.py:223
  13.2 6.4 %collective-permute-start.2 = (bf16[128,640]{1,0:T(8,128)(2,1)S(1)}, bf16[128,640]{1,0:T(8,128)(2,1)S(1)}, u32[]{:S(2)}, u32[]{:S(2)}) collective-permute-start(bf16[128,640]{1,0:T(8,128)(2,1)S(1)} %bitcast.43), channel_id=1, source_target_pairs={{0,32},{32,64},{64,96},{96,0},{1,33},{33,65},{65,97},{97,1},{2,34}... | collective-permute-start | bytes 491528 | tf_op jit(solution)/shard_map/ppermute | solution.py:223
  26.7 48.4 %copy-start = (s32[1,128]{1,0:T(1,128)S(1)}, s32[1,128]{1,0:T(1,128)}, u32[]{:S(2)}) copy-start(s32[1,128]{1,0:T(1,128)} %param.6) | copy-start | bytes 1540
  26.7 54.8 %copy-start.1 = (s32[4]{0:T(128)S(1)}, s32[4]{0:T(128)}, u32[]{:S(2)}) copy-start(s32[4]{0:T(128)} %constant.42.clone) | copy-start | bytes 52
  72.3 54.0 %collective-permute-start = (bf16[32,128,256]{2,1,0:T(8,128)(2,1)S(1)}, bf16[32,128,256]{2,1,0:T(8,128)(2,1)}, u32[]{:S(2)}, u32[]{:S(2)}) collective-permute-start(bf16[32,128,256]{2,1,0:T(8,128)(2,1)S(1)} %all_to_all.15.refs_0_.refs_2_.refs_4_), channel_id=1, source_target_pairs={{0,32},{32,64},{64,96},{96,0},{1,33},{33,65},{65,97},{97,1},{2,34}... | collective-permute-start | bytes 6291464 | tf_op jit(solution)/shard_map/ppermute | solution.py:223
  73.5 56.2 %collective-permute-start.5 = (bf16[32,128,256]{2,1,0:T(8,128)(2,1)S(1)}, bf16[32,128,256]{2,1,0:T(8,128)(2,1)}, u32[]{:S(2)}, u32[]{:S(2)}) collective-permute-start(bf16[32,128,256]{2,1,0:T(8,128)(2,1)S(1)} %all_to_all.15.refs_0_.refs_2_.refs_4_), channel_id=1, source_target_pairs={{0,96},{32,0},{64,32},{96,64},{1,97},{33,1},{65,33},{97,65},{2,98}... | collective-permute-start | bytes 6291464 | tf_op jit(solution)/shard_map/ppermute | solution.py:223
  75.7 48.3 %all-to-all-start.1 = ((s32[128,1,128]{2,1,0:T(1,128)}), s32[128,1,128]{2,1,0:T(1,128)S(1)}, u32[]{:S(2)}, u32[]{:S(2)}) async-start(s32[128,1,128]{2,1,0:T(1,128)} %broadcast_in_dim.27), calls=%async_computation.1 | async-start | bytes 131072 | tf_op jit(solution)/shard_map/all_to_all | solution.py:256
  128.7 25.4 %collective-permute-start.1 = (bf16[16,128,256]{2,1,0:T(8,128)(2,1)}, bf16[16,128,256]{2,1,0:T(8,128)(2,1)S(1)}, u32[]{:S(2)}, u32[]{:S(2)}) collective-permute-start(bf16[16,128,256]{2,1,0:T(8,128)(2,1)} %slice.16), channel_id=1, source_target_pairs={{0,32},{32,64},{64,96},{96,0},{1,33},{33,65},{65,97},{97,1},{2,34}... | collective-permute-start | bytes 3145736 | tf_op jit(solution)/shard_map/ppermute | solution.py:223
  132.0 24.0 %collective-permute-start.6 = (bf16[16,128,256]{2,1,0:T(8,128)(2,1)}, bf16[16,128,256]{2,1,0:T(8,128)(2,1)}, u32[]{:S(2)}, u32[]{:S(2)}) collective-permute-start(bf16[16,128,256]{2,1,0:T(8,128)(2,1)} %slice.17), channel_id=1, source_target_pairs={{0,96},{32,0},{64,32},{96,64},{1,97},{33,1},{65,33},{97,65},{2,98}... | collective-permute-start | bytes 3145736 | tf_op jit(solution)/shard_map/ppermute | solution.py:223
Sparse Core Ops, SparseCore 0:
  20.6 107.6 all-gather.2

commit v3 on v2

v3 whole, which is shorter than its diff:
```python
import functools
import math

import jax
import jax.numpy as jnp
from jax import lax
from jax.experimental import pallas as pl
from jax.experimental.pallas import tpu as pltpu
from jax.sharding import PartitionSpec as P

BLK = 128
TILE = 256
DOCS = 32
GROUP = 4

NT = (((1,), (1,)), ((), ()))


def flat(ref, at, count):
    return ref[at : at + count].reshape(count * BLK, ref.shape[2])


def flat_pair(refs, at, count):
    return jnp.concatenate([flat(ref, at, count) for ref in refs], axis=1)


def gram_kernel(nrows, tiles, rows_ref, ids_ref, first_ref, *refs):
    per_row = 9
    row_refs = [refs[k * per_row : (k + 1) * per_row] for k in range(nrows)]
    out_ref, h_prev, g_prev, acc = refs[nrows * per_row :]
    step = pl.program_id(0)
    steps = pl.num_programs(0)

    @pl.when(step == 0)
    def _():
        acc[...] = jnp.zeros_like(acc)
        for k in range(nrows):
            g_last = row_refs[k][8]
            h_prev[k, 0] = jnp.zeros_like(h_prev[k, 0])
            g_prev[k, 0] = jnp.zeros_like(g_prev[k, 0])
            h_prev[k, 1] = flat_pair(row_refs[k][6:8], 0, 2)
            g_prev[k, 1] = flat(g_last, 0, 2)

    place = lax.broadcasted_iota(jnp.int32, (TILE, TILE), 0)
    column = lax.broadcasted_iota(jnp.int32, (TILE, TILE), 1)
    triangle = jnp.where(
        place < column, jnp.float32(2.0), jnp.where(place == column, jnp.float32(1.0), jnp.float32(0.0))
    )
    docs = lax.broadcasted_iota(jnp.int32, (DOCS, TILE), 0)
    for k in range(nrows):
        base = rows_ref[k]
        share = jnp.zeros((DOCS, BLK), jnp.float32)
        for half in range(2):
            h_refs = row_refs[k][3 * half : 3 * half + 2]
            g_ref = row_refs[k][3 * half + 2]
            old_h = h_prev[k, half]
            old_g = g_prev[k, half]
            for t in range(tiles):
                number = half * steps * tiles + step * tiles + t
                at = base * (2 * steps * tiles * 2) + 2 * number
                ids = jnp.concatenate([ids_ref[at], ids_ref[at + 1]], axis=1)
                first = jnp.concatenate([first_ref[at], first_ref[at + 1]], axis=1) - number * TILE
                own_h = flat_pair(h_refs, 2 * t, 2)
                own_g = flat(g_ref, 2 * t, 2)
                dot = functools.partial(
                    lax.dot_general, dimension_numbers=NT, preferred_element_type=jnp.float32
                )
                pairs = dot(own_h, own_h) * dot(own_g, own_g) * triangle
                pairs = jnp.where(place >= first, pairs, jnp.float32(0.0))
                far = dot(old_h, own_h) * dot(old_g, own_g)
                far = jnp.where(place >= first + TILE, far, jnp.float32(0.0))
                total = jnp.sum(pairs + 2.0 * far, axis=0, keepdims=True)
                terms = jnp.where(docs == ids, jnp.broadcast_to(total, docs.shape), jnp.float32(0.0))
                share += terms[:, :BLK] + terms[:, BLK:]
                old_h, old_g = own_h, own_g
            h_prev[k, half] = old_h
            g_prev[k, half] = old_g
        here = pl.ds(pl.multiple_of(base * DOCS, DOCS), DOCS)
        acc[here, :] += share

    @pl.when(step == steps - 1)
    def _():
        sums = jnp.sum(acc[...].T, axis=0, keepdims=True)
        out_ref[...] = jnp.broadcast_to(sums[None], out_ref.shape)


def row_specs(count, steps, width, row):
    specs = []
    for offset in (0, steps):
        for _ in range(2):
            specs.append(pl.BlockSpec((count, BLK, BLK), lambda i, r, o=offset: (i + o, 0, 0)))
        specs.append(
            pl.BlockSpec((count, None, BLK, width), lambda i, r, o=offset: (i + o, row, 0, 0))
        )
    return specs


def gram(rows, ids, first, tiles, pieces):
    blocks, _, _, width = pieces[0][3].shape
    steps = blocks // (4 * tiles)
    shape = (ids.shape[0], 1, BLK)
    whole = pl.BlockSpec(ids.shape, lambda i, r: (0, 0, 0))
    last = steps * tiles - 1
    specs, operands = [], []
    for left, right, row, grad in pieces:
        specs += row_specs(2 * tiles, steps, width, row)
        specs += [pl.BlockSpec((2, BLK, BLK), lambda i, r: (last, 0, 0))] * 2
        specs += [pl.BlockSpec((2, None, BLK, width), lambda i, r, row=row: (last, row, 0, 0))]
        operands += [left, right, grad] * 3
    nrows = len(pieces)
    return pl.pallas_call(
        functools.partial(gram_kernel, nrows, tiles),
        out_shape=jax.ShapeDtypeStruct(shape, jnp.float32),
        grid_spec=pltpu.PrefetchScalarGridSpec(
            num_scalar_prefetch=1,
            grid=(steps,),
            in_specs=[whole, whole, *specs],
            out_specs=pl.BlockSpec(shape, lambda i, r: (0, 0, 0)),
            scratch_shapes=[
                pltpu.VMEM((nrows, 2, TILE, TILE), jnp.bfloat16),
                pltpu.VMEM((nrows, 2, TILE, width), jnp.bfloat16),
                pltpu.VMEM((nrows * DOCS, BLK), jnp.float32),
            ],
        ),
        compiler_params=pltpu.CompilerParams(vmem_limit_bytes=32 * 2**20),
        cost_estimate=pl.CostEstimate(
            flops=nrows * blocks * BLK * 4 * TILE * (TILE + width),
            bytes_accessed=nrows * blocks * BLK * 2 * (TILE + width),
            transcendentals=0,
        ),
        name="gram",
    )(rows, ids, first, *operands)


def product_kernel(nrows, bound, rows_ref, ids_ref, norms_ref, *refs):
    per_row = 6
    row_refs = [refs[k * per_row : (k + 1) * per_row] for k in range(nrows)]
    out_ref, factor, scaled = refs[nrows * per_row :]
    step = pl.program_id(0)
    steps = pl.num_programs(0)
    groups = factor.shape[0]
    per_group = groups // nrows

    @pl.when(step == 0)
    def _():
        norms = jnp.sum(norms_ref[...], axis=0)
        clip = bound / jnp.maximum(jnp.sqrt(norms), bound) / nrows
        for k in range(nrows):
            span = slice(k * per_group, (k + 1) * per_group)
            ids = ids_ref[span, 0, :] + k * DOCS
            table = jnp.broadcast_to(clip, ids.shape)
            factor[span, :] = jnp.take_along_axis(table, ids, axis=1)

    lines = []
    for k in range(nrows):
        for half in range(2):
            for j in range(GROUP):
                at = rows_ref[k] * per_group + half * (per_group // 2) + step * GROUP + j
                lines.append(factor[pl.ds(at, 1), :])
    used = len(lines)
    lines = jnp.concatenate(lines + [jnp.zeros((BLK - used, BLK), jnp.float32)], axis=0).T
    at = 0
    result = None
    for k in range(nrows):
        for half in range(2):
            h_refs = row_refs[k][3 * half : 3 * half + 2]
            g_ref = row_refs[k][3 * half + 2]
            begin = at * BLK
            for j in range(GROUP):
                scale = jnp.broadcast_to(lines[:, at : at + 1], (BLK, BLK))
                here = slice(at * BLK, (at + 1) * BLK)
                for c in range(0, g_ref.shape[2], BLK):
                    scaled[here, c : c + BLK] = (
                        g_ref[j, :, c : c + BLK].astype(jnp.float32) * scale
                    ).astype(jnp.bfloat16)
                at += 1
            share = lax.dot_general(
                flat_pair(h_refs, 0, GROUP),
                scaled[begin : at * BLK, :],
                (((0,), (0,)), ((), ())),
                preferred_element_type=jnp.float32,
            )
            result = share if result is None else result + share

    @pl.when(step == 0)
    def _():
        out_ref[...] = result

    @pl.when(step > 0)
    def _():
        out_ref[...] += result


def product(rows, ids, norms, pieces, bound):
    blocks, _, _, width = pieces[0][3].shape
    steps = blocks // (2 * GROUP)
    nrows = len(pieces)
    whole = pl.BlockSpec(ids.shape, lambda i, r: (0, 0, 0))
    specs, operands = [], []
    for left, right, row, grad in pieces:
        specs += row_specs(GROUP, steps, width, row)
        operands += [left, right, grad] * 2
    return pl.pallas_call(
        functools.partial(product_kernel, nrows, bound),
        out_shape=jax.ShapeDtypeStruct((TILE, width), jnp.float32),
        grid_spec=pltpu.PrefetchScalarGridSpec(
            num_scalar_prefetch=1,
            grid=(steps,),
            in_specs=[whole, whole, *specs],
            out_specs=pl.BlockSpec((TILE, width), lambda i, r: (0, 0)),
            scratch_shapes=[
                pltpu.VMEM((nrows * blocks, BLK), jnp.float32),
                pltpu.VMEM((nrows * 2 * GROUP * BLK, width), jnp.bfloat16),
            ],
        ),
        compiler_params=pltpu.CompilerParams(vmem_limit_bytes=32 * 2**20),
        cost_estimate=pl.CostEstimate(
            flops=2 * nrows * blocks * BLK * TILE * width,
            bytes_accessed=nrows * blocks * BLK * 2 * (TILE + width),
            transcendentals=0,
        ),
        name="product",
    )(rows, ids, norms, *operands)


def quarters_kernel(rows_ref, *refs):
    ins, outs = refs[: len(refs) // 2], refs[len(refs) // 2 :]
    for in_ref, out_ref in zip(ins, outs):
        out_ref[...] = in_ref[...]


def quarters(targets, grad):
    tokens, width = grad.shape
    count = targets.shape[0]
    part = width // count
    return pl.pallas_call(
        quarters_kernel,
        out_shape=[jax.ShapeDtypeStruct((tokens, part), grad.dtype)] * count,
        grid_spec=pltpu.PrefetchScalarGridSpec(
            num_scalar_prefetch=1,
            grid=(1,),
            in_specs=[pl.BlockSpec((tokens, part), lambda i, r, k=k: (0, r[k])) for k in range(count)],
            out_specs=[pl.BlockSpec((tokens, part), lambda i, r: (0, 0))] * count,
        ),
        name="quarters",
    )(targets, *[grad] * count)


def columns_kernel(in_ref, left_ref, right_ref):
    for j in range(left_ref.shape[0]):
        left_ref[j] = in_ref[:, 2 * j * BLK : (2 * j + 1) * BLK]
        right_ref[j] = in_ref[:, (2 * j + 1) * BLK : (2 * j + 2) * BLK]


def columns(hidden, blocks, steps=4):
    tokens, width = hidden.shape
    count = blocks // steps
    half = pl.BlockSpec((count, tokens, BLK), lambda i: (i, 0, 0))
    return pl.pallas_call(
        columns_kernel,
        out_shape=[jax.ShapeDtypeStruct((blocks, tokens, BLK), hidden.dtype)] * 2,
        grid=(steps,),
        in_specs=[pl.BlockSpec((tokens, width // steps), lambda i: (0, i))],
        out_specs=[half, half],
        name="columns",
    )(hidden)


def shift(block, distance):
    size = lax.axis_size("dp")
    return lax.ppermute(block, "dp", [(i, (i + distance) % size) for i in range(size)])


def starts(ids, row_count):
    by_row = ids.reshape(row_count, -1)
    docs = jnp.arange(DOCS, dtype=jnp.int32)
    before = jnp.sum((by_row[:, None, :] < docs[None, :, None]).astype(jnp.int32), axis=2)
    own = by_row[:, None, :] == docs[None, :, None]
    return jnp.sum(jnp.where(own, before[:, :, None], 0), axis=1).reshape(ids.shape)


def body(hidden, grad_out, segment):
    row_count = lax.axis_size("dp")
    blocks = lax.axis_size("ctx")
    tokens, width_hidden = hidden.shape[1:]
    width_grad = grad_out.shape[2]
    me = lax.axis_index("dp")
    rows = lax.rem(me + jnp.array([0, 3, 1, 2], jnp.int32), row_count)

    keep, up, down, across = quarters(lax.rem(me + jnp.array([0, 1, 3, 2], jnp.int32), row_count), grad_out[0])
    received = [keep, shift(up, 1), shift(down, -1), shift(across, 2)]

    left, right = columns(hidden[0], blocks)
    left, right, *received = lax.optimization_barrier((left, right, *received))

    every_grad = lax.all_gather(jnp.stack(received), "ctx", axis=0, tiled=False)

    left = lax.all_to_all(left, "ctx", 0, 0, tiled=True)
    left_below, left_above = shift(left, 1), shift(left, -1)
    right, left_ready = lax.optimization_barrier((right, left))
    right = lax.all_to_all(right, "ctx", 0, 0, tiled=True)
    right_below, right_above = shift(right, 1), shift(right, -1)
    left_far = shift(left_below, 1)
    right_far = shift(right_above, -1)

    ids, right_ready = lax.optimization_barrier((segment, right))
    ids = jnp.broadcast_to(ids[None], (row_count * blocks, 1, tokens))
    ids = lax.all_to_all(ids, ("dp", "ctx"), 0, 0, tiled=True)
    first = starts(ids, row_count)

    pieces = [
        (left, right, 0, every_grad),
        (left_below, right_below, 1, every_grad),
        (left_above, right_above, 2, every_grad),
        (left_far, right_far, 3, every_grad),
    ]
    partial = gram(rows, ids, first, 1, pieces)
    norms = lax.all_to_all(partial, ("dp", "ctx"), 0, 0, tiled=True)

    bound = math.sqrt(tokens * width_hidden * width_grad)
    return product(rows, ids, norms, pieces, bound)


def solution(mesh):
    in_specs = (P("dp", "ctx", None), P("dp", "ctx", None), P("dp", "ctx"))
    out_specs = P("ctx", "dp")
    return jax.shard_map(body, mesh=mesh, in_specs=in_specs, out_specs=out_specs, check_vma=False)
```

time: 207 us -> 223 us (1.077)
  waiting for transfers between devices: 49.6 us -> 86.8 us
  blocking collectives: 63.4 us -> 48.4 us
  local copies, waits for them, and re-layouts: 14.8 us -> 1.33 us
  starting transfers between devices: 16.6 us -> 21.6 us
    all_to_all x0 -> x1, waiting for transfers between devices: none -> 22.7 us  [body(): right = lax.all_to_all(right, 'ctx', 0, 0, tiled=True)]
    ppermute x7 -> x9, waiting for transfers between devices: 7.65 us -> 24.6 us  [shift(): lax.ppermute(block, 'dp', [(i, (i + distance) % size) for i in range(size)])]
    all_to_all x1, blocking collectives: 45.7 us -> 32.9 us  [body(): left = lax.all_to_all(left, 'ctx', 0, 0, tiled=True)]
    all_to_all x0 -> x1, starting transfers between devices: none -> 5.29 us  [body(): right = lax.all_to_all(right, 'ctx', 0, 0, tiled=True)]
    slice x3 -> x0, local copies, waits for them, and re-layouts: 5.15 us -> none  [the longest x1 2.29 us: body(): far_high = shift(above[blocks // 2:], -1)]
    unnamed x6 -> x8, local copies, waits for them, and re-layouts: 4.64 us -> 0.02 us
    pallas_call x2 -> x3, Pallas kernels: 28.4 us -> 32.6 us  [the longest x1 26.1 us: gram(): pl.pallas_call(functools.partial(gram_kernel, nrows, tiles), out_shape=ja...]
    another operation x6 -> x0, local copies, waits for them, and re-layouts: 3.61 us -> none  [the longest x1 2.91 us: body(): columns = hidden[0].reshape(tokens, blocks, -1).transpose(1, 0, 2)]
  transfers between devices with their start and end apart: 9 -> 12, of which waited for: 5 -> 5; matrix products, arithmetic and copies ran while one was open for 7% -> 1% of each run, Pallas kernels for 10% -> 2%
where the time goes in v3:
time: 223 us
  waiting for transfers between devices  86.8 us (39%)
  blocking collectives  48.4 us (22%)
  Pallas kernels  47.2 us (21%)
  starting transfers between devices  21.6 us (10%)
  between operations  13.5 us (6%)
  other arithmetic  3.84 us (2%)
    all_to_all x1, waiting for transfers between devices, body(): ids = lax.all_to_all(ids, ('dp', 'ctx'), 0, 0, tiled=True)  39.5 us
    all_to_all x1, blocking collectives, body(): left = lax.all_to_all(left, 'ctx', 0, 0, tiled=True)  32.9 us
    pallas_call x1, Pallas kernels, gram(): pl.pallas_call(functools.partial(gram_kernel, nrows, tiles), out_shape=ja...  26.1 us
    ppermute x9, waiting for transfers between devices, shift(): lax.ppermute(block, 'dp', [(i, (i + distance) % size) for i in range(size)])  24.6 us
    all_to_all x1, waiting for transfers between devices, body(): right = lax.all_to_all(right, 'ctx', 0, 0, tiled=True)  22.7 us
    all_to_all x1, blocking collectives, body(): norms = lax.all_to_all(partial, ('dp', 'ctx'), 0, 0, tiled=True)  15.4 us
    pallas_call x1, Pallas kernels, product(): pl.pallas_call(functools.partial(product_kernel, nrows, bound), out_shape...  14.6 us
    ppermute x9, starting transfers between devices, shift(): lax.ppermute(block, 'dp', [(i, (i + distance) % size) for i in range(size)])  9.39 us
  transfers between devices with their start and end apart: 12, of which 5 were waited for; matrix products, arithmetic and copies ran while one was open for 1% of the time, Pallas kernels for 2%

profile of v3, /device:TPU:1, one launch (start us, length us, event | category | flops | bytes accessed | tf_op | source)
XLA Modules:
  0.0 222.7 jit_solution(16657149719119997039)
XLA Ops:
  6.5 0.0 all-gather.3.cloned.1.call-start
  6.5 1.2 compare_select_fusion.rows_ref
  7.7 2.7 %quarters.1 = (bf16[128,640]{1,0:T(8,128)(2,1)}, bf16[128,640]{1,0:T(8,128)(2,1)}, bf16[128,640]{1,0:T(8,128)(2,1)}, bf16[128,640]{1,0:T(8,128)(2,1)}) custom-call(s32[4]{0:T(128)} %compare_select_fusion.rows_ref, bf16[128,2560]{1,0:T(8,128)(2,1)} %bitcast.28, bf16[128,2560]{1,0:T(8,128)(2,1)} %bitcast.29, bf16[128,2560]{1,0:T(8,128)(2,1)} %bitcast.30, ...), custom_call_target="tpu_custom_call" | custom-call | tf_op jit(solution)/shard_map/quarters/pallas_call | solution.py:236
  10.4 0.0 copy-start.1
  10.4 2.1 collective-permute-start
  12.5 1.5 collective-permute-start.1
  14.0 1.6 collective-permute-start.2
  15.6 3.9 %columns.1 = (bf16[32,128,128]{2,1,0:T(8,128)(2,1)}, bf16[32,128,128]{2,1,0:T(8,128)(2,1)}) custom-call(bf16[128,8192]{1,0:T(8,128)(2,1)} %bitcast.32), custom_call_target="tpu_custom_call" | custom-call | tf_op jit(solution)/shard_map/columns/pallas_call | solution.py:259
  19.5 0.0 copy-start
  19.5 0.0 collective-permute-done
  19.5 0.0 collective-permute-done.1
  19.5 2.9 %collective-permute-done.2 = bf16[128,640]{1,0:T(8,128)(2,1)S(1)} collective-permute-done((bf16[128,640]{1,0:T(8,128)(2,1)}, bf16[128,640]{1,0:T(8,128)(2,1)S(1)}, u32[]{:S(2)}, u32[]{:S(2)}) %collective-permute-start.2) | collective-permute-done | bytes 163872 | tf_op jit(solution)/shard_map/ppermute | solution.py:271
  22.5 0.0 copy-done.1
  22.5 0.9 pad_maximum_fusion
  23.4 0.0 all-gather.3.cloned.1.call-update
  23.4 0.0 copy-done
  23.4 0.0 copy-start.2
  23.5 0.0 copy-start.3
  23.5 32.9 %all_to_all.20.refs_0_.refs_3_.refs_6_ = bf16[32,128,128]{2,1,0:T(8,128)(2,1)S(1)} all-to-all(bf16[32,128,128]{2,1,0:T(8,128)(2,1)S(1)} %copy-done), channel_id=1, replica_groups=mesh['dp'=4,'ctx'=32] {'ctx'}, dimensions={0} | all-to-all | bytes 2097152 | tf_op jit(solution)/shard_map/all_to_all | solution.py:298
  56.4 5.3 %all-to-all-start.1 = ((bf16[32,128,128]{2,1,0:T(8,128)(2,1)}), bf16[32,128,128]{2,1,0:T(8,128)(2,1)S(1)}, u32[]{:S(2)}, u32[]{:S(2)}) async-start(bf16[32,128,128]{2,1,0:T(8,128)(2,1)} %get-tuple-element.27), calls=%async_computation.1 | async-start | bytes 2097152 | tf_op jit(solution)/shard_map/all_to_all | solution.py:301
  61.7 0.7 collective-permute-start.3
  62.5 22.7 %all-to-all-done.1.refs_1_.refs_4_.refs_7_ = bf16[32,128,128]{2,1,0:T(8,128)(2,1)S(1)} async-done(((bf16[32,128,128]{2,1,0:T(8,128)(2,1)}), bf16[32,128,128]{2,1,0:T(8,128)(2,1)S(1)}, u32[]{:S(2)}, u32[]{:S(2)}) %all-to-all-start.1) | async-done | bytes 1048608 | tf_op jit(solution)/shard_map/all_to_all | solution.py:301
  85.1 0.0 collective-permute-start.6
  85.1 0.0 collective-permute-start.5
  85.1 1.5 collective-permute-start.4
  86.6 1.0 collective-permute-done.3.refs_9_.refs_12_.refs_15_.refs_6_
  87.6 0.4 collective-permute-start.7
  88.0 20.6 %collective-permute-done.6.refs_19_.refs_22_.refs_25_.refs_13_.refs_16_ = bf16[32,128,128]{2,1,0:T(8,128)(2,1)} collective-permute-done((bf16[32,128,128]{2,1,0:T(8,128)(2,1)S(1)}, bf16[32,128,128]{2,1,0:T(8,128)(2,1)}, u32[]{:S(2)}, u32[]{:S(2)}) %collective-permute-start.6) | collective-permute-done | bytes 1048608 | tf_op jit(solution)/shard_map/ppermute | solution.py:271
  108.7 1.5 collective-permute-start.8
  110.2 0.0 copy-done.2
  110.2 0.6 broadcast_in_dim.24
  110.8 6.9 %all-to-all-start.2 = ((s32[128,1,128]{2,1,0:T(1,128)}), s32[128,1,128]{2,1,0:T(1,128)S(1)}, u32[]{:S(2)}, u32[]{:S(2)}) async-start(s32[128,1,128]{2,1,0:T(1,128)} %broadcast_in_dim.24), calls=%async_computation.2 | async-start | bytes 131072 | tf_op jit(solution)/shard_map/all_to_all | solution.py:308
  117.7 0.0 copy-done.3
  117.8 39.5 %all-to-all-done.2.ids_ref = s32[128,1,128]{2,1,0:T(1,128)S(1)} async-done(((s32[128,1,128]{2,1,0:T(1,128)}), s32[128,1,128]{2,1,0:T(1,128)S(1)}, u32[]{:S(2)}, u32[]{:S(2)}) %all-to-all-start.2) | async-done | bytes 65568 | tf_op jit(solution)/shard_map/all_to_all | solution.py:308
  157.3 0.5 broadcast.15
  157.8 0.8 reduce.3
  158.7 0.4 convert_reduce_fusion
  159.1 0.5 select_reduce_fusion
  159.6 0.1 reshape.8.first_ref
  159.7 0.0 collective-permute-done.5.refs_18_.refs_21_.refs_24_.refs_12_.refs_15_
  159.7 0.0 collective-permute-done.4.refs_10_.refs_13_.refs_16_.refs_7_
  159.7 0.0 collective-permute-done.7.refs_27_.refs_30_.refs_33_.refs_18_.refs_21_
  159.7 0.0 collective-permute-done.8.refs_28_.refs_31_.refs_34_.refs_19_.refs_22_
  159.7 0.0 all-gather.3.cloned.1.call-done
  159.7 26.1 %gram.1 = f32[128,1,128]{2,1,0:T(1,128)S(1)} custom-call(s32[4]{0:T(128)S(1)} %compare_select_fusion.2.rows_ref, s32[128,1,128]{2,1,0:T(1,128)S(1)} %all-to-all-done.2.ids_ref, s32[128,1,128]{2,1,0:T(1,128)S(1)} %reshape.8.first_ref, bf16[32,128,128]{2,1,0:T(8,128)(2,1)S(1)} %all_to_all.20.refs_0_.refs_3_.refs_6_, ...), custom_call_target="tpu_custom_call" | custom-call | flops 15032385536 | bytes 29360128 | tf_op jit(solution)/shard_map/gram/pallas_call | solution.py:111
  185.8 15.4 %all_to_all.21.norms_ref = f32[128,1,128]{2,1,0:T(1,128)S(1)} all-to-all(f32[128,1,128]{2,1,0:T(1,128)S(1)} %gram.1), channel_id=1, replica_groups=mesh['dp'=4,'ctx'=32] {'dp','ctx'}, dimensions={0} | all-to-all | bytes 131072 | tf_op jit(solution)/shard_map/all_to_all | solution.py:318
  201.2 14.6 %product.1 = f32[256,640]{1,0:T(8,128)} custom-call(s32[4]{0:T(128)S(1)} %compare_select_fusion.2.rows_ref, s32[128,1,128]{2,1,0:T(1,128)S(1)} %all-to-all-done.2.ids_ref, f32[128,1,128]{2,1,0:T(1,128)S(1)} %all_to_all.21.norms_ref, bf16[32,128,128]{2,1,0:T(8,128)(2,1)S(1)} %all_to_all.20.refs_0_.refs_3_.refs_6_, ...), custom_call_target="tpu_custom_call" | custom-call | flops 5368709120 | bytes 29360128 | tf_op jit(solution)/shard_map/product/pallas_call | solution.py:203
  (2 shorter events, 0.0 us)
Async XLA Ops:
  6.5 153.2 %all-gather.3.cloned.1.call-start = ((), (), s32[]{:S(2)}) async-start(), calls=%async_computation.4 | async-start | bytes 21626880 | tf_op jit(solution)/shard_map/all_gather | solution.py:296
  10.4 12.1 %copy-start.1 = (bf16[128,640]{1,0:T(8,128)(2,1)S(1)}, bf16[128,640]{1,0:T(8,128)(2,1)}, u32[]{:S(2)}) copy-start(bf16[128,640]{1,0:T(8,128)(2,1)} %get-tuple-element.29) | copy-start | bytes 491524
  10.4 9.1 %collective-permute-start = (bf16[128,640]{1,0:T(8,128)(2,1)}, bf16[128,640]{1,0:T(8,128)(2,1)S(1)}, u32[]{:S(2)}, u32[]{:S(2)}) collective-permute-start(bf16[128,640]{1,0:T(8,128)(2,1)} %get-tuple-element.22), channel_id=1, source_target_pairs={{0,32},{32,64},{64,96},{96,0},{1,33},{33,65},{65,97},{97,1},{2,34}... | collective-permute-start | bytes 491528 | tf_op jit(solution)/shard_map/ppermute | solution.py:271
  12.5 7.0 %collective-permute-start.1 = (bf16[128,640]{1,0:T(8,128)(2,1)}, bf16[128,640]{1,0:T(8,128)(2,1)S(1)}, u32[]{:S(2)}, u32[]{:S(2)}) collective-permute-start(bf16[128,640]{1,0:T(8,128)(2,1)} %get-tuple-element.23), channel_id=1, source_target_pairs={{0,96},{32,0},{64,32},{96,64},{1,97},{33,1},{65,33},{97,65},{2,98}... | collective-permute-start | bytes 491528 | tf_op jit(solution)/shard_map/ppermute | solution.py:271
  14.0 8.4 %collective-permute-start.2 = (bf16[128,640]{1,0:T(8,128)(2,1)}, bf16[128,640]{1,0:T(8,128)(2,1)S(1)}, u32[]{:S(2)}, u32[]{:S(2)}) collective-permute-start(bf16[128,640]{1,0:T(8,128)(2,1)} %get-tuple-element.24), channel_id=1, source_target_pairs={{0,64},{32,96},{64,0},{96,32},{1,65},{33,97},{65,1},{97,33},{2,66}... | collective-permute-start | bytes 491528 | tf_op jit(solution)/shard_map/ppermute | solution.py:271
  19.5 3.9 %copy-start = (bf16[32,128,128]{2,1,0:T(8,128)(2,1)S(1)}, bf16[32,128,128]{2,1,0:T(8,128)(2,1)}, u32[]{:S(2)}) copy-start(bf16[32,128,128]{2,1,0:T(8,128)(2,1)} %get-tuple-element.26) | copy-start | bytes 3145732
  23.4 86.7 %copy-start.2 = (s32[1,128]{1,0:T(1,128)S(1)}, s32[1,128]{1,0:T(1,128)}, u32[]{:S(2)}) copy-start(s32[1,128]{1,0:T(1,128)} %param.7) | copy-start | bytes 1540
  23.5 94.3 %copy-start.3 = (s32[4]{0:T(128)S(1)}, s32[4]{0:T(128)}, u32[]{:S(2)}) copy-start(s32[4]{0:T(128)} %constant.18.clone) | copy-start | bytes 52
  56.4 28.7 %all-to-all-start.1 = ((bf16[32,128,128]{2,1,0:T(8,128)(2,1)}), bf16[32,128,128]{2,1,0:T(8,128)(2,1)S(1)}, u32[]{:S(2)}, u32[]{:S(2)}) async-start(bf16[32,128,128]{2,1,0:T(8,128)(2,1)} %get-tuple-element.27), calls=%async_computation.1 | async-start | bytes 2097152 | tf_op jit(solution)/shard_map/all_to_all | solution.py:301
  61.7 25.9 %collective-permute-start.3 = (bf16[32,128,128]{2,1,0:T(8,128)(2,1)S(1)}, bf16[32,128,128]{2,1,0:T(8,128)(2,1)S(1)}, u32[]{:S(2)}, u32[]{:S(2)}) collective-permute-start(bf16[32,128,128]{2,1,0:T(8,128)(2,1)S(1)} %all_to_all.20.refs_0_.refs_3_.refs_6_), channel_id=1, source_target_pairs={{0,32},{32,64},{64,96},{96,0},{1,33},{33,65},{65,97},{97,1},{2,34}... | collective-permute-start | bytes 3145736 | tf_op jit(solution)/shard_map/ppermute | solution.py:271
  85.1 23.6 %collective-permute-start.6 = (bf16[32,128,128]{2,1,0:T(8,128)(2,1)S(1)}, bf16[32,128,128]{2,1,0:T(8,128)(2,1)}, u32[]{:S(2)}, u32[]{:S(2)}) collective-permute-start(bf16[32,128,128]{2,1,0:T(8,128)(2,1)S(1)} %all-to-all-done.1.refs_1_.refs_4_.refs_7_), channel_id=1, source_target_pairs={{0,96},{32,0},{64,32},{96,64},{1,97},{33,1},{65,33},{97,65},{2,98}... | collective-permute-start | bytes 3145736 | tf_op jit(solution)/shard_map/ppermute | solution.py:271
  85.1 74.5 %collective-permute-start.5 = (bf16[32,128,128]{2,1,0:T(8,128)(2,1)S(1)}, bf16[32,128,128]{2,1,0:T(8,128)(2,1)}, u32[]{:S(2)}, u32[]{:S(2)}) collective-permute-start(bf16[32,128,128]{2,1,0:T(8,128)(2,1)S(1)} %all_to_all.20.refs_0_.refs_3_.refs_6_), channel_id=1, source_target_pairs={{0,96},{32,0},{64,32},{96,64},{1,97},{33,1},{65,33},{97,65},{2,98}... | collective-permute-start | bytes 3145736 | tf_op jit(solution)/shard_map/ppermute | solution.py:271
  85.1 74.6 %collective-permute-start.4 = (bf16[32,128,128]{2,1,0:T(8,128)(2,1)S(1)}, bf16[32,128,128]{2,1,0:T(8,128)(2,1)}, u32[]{:S(2)}, u32[]{:S(2)}) collective-permute-start(bf16[32,128,128]{2,1,0:T(8,128)(2,1)S(1)} %all-to-all-done.1.refs_1_.refs_4_.refs_7_), channel_id=1, source_target_pairs={{0,32},{32,64},{64,96},{96,0},{1,33},{33,65},{65,97},{97,1},{2,34}... | collective-permute-start | bytes 3145736 | tf_op jit(solution)/shard_map/ppermute | solution.py:271
  87.6 72.1 %collective-permute-start.7 = (bf16[32,128,128]{2,1,0:T(8,128)(2,1)S(1)}, bf16[32,128,128]{2,1,0:T(8,128)(2,1)}, u32[]{:S(2)}, u32[]{:S(2)}) collective-permute-start(bf16[32,128,128]{2,1,0:T(8,128)(2,1)S(1)} %collective-permute-done.3.refs_9_.refs_12_.refs_15_.refs_6_), channel_id=1, source_target_pairs={{0,32},{32,64},{64,96},{96,0},{1,33},{33,65},{65,97},{97,1},{2,34}... | collective-permute-start | bytes 3145736 | tf_op jit(solution)/shard_map/ppermute | solution.py:271
  108.7 51.0 %collective-permute-start.8 = (bf16[32,128,128]{2,1,0:T(8,128)(2,1)}, bf16[32,128,128]{2,1,0:T(8,128)(2,1)}, u32[]{:S(2)}, u32[]{:S(2)}) collective-permute-start(bf16[32,128,128]{2,1,0:T(8,128)(2,1)} %collective-permute-done.6.refs_19_.refs_22_.refs_25_.refs_13_.refs_16_), channel_id=1, source_target_pairs={{0,96},{32,0},{64,32},{96,64},{1,97},{33,1},{65,33},{97,65},{2,98}... | collective-permute-start | bytes 3145736 | tf_op jit(solution)/shard_map/ppermute | solution.py:271
  110.8 46.5 %all-to-all-start.2 = ((s32[128,1,128]{2,1,0:T(1,128)}), s32[128,1,128]{2,1,0:T(1,128)S(1)}, u32[]{:S(2)}, u32[]{:S(2)}) async-start(s32[128,1,128]{2,1,0:T(1,128)} %broadcast_in_dim.24), calls=%async_computation.2 | async-start | bytes 131072 | tf_op jit(solution)/shard_map/all_to_all | solution.py:308
Sparse Core Ops, SparseCore 0:
  23.6 98.0 all-gather.2

commit v4 on v3

v4 whole, which is shorter than its diff:
```python
import functools
import math

import jax
import jax.numpy as jnp
from jax import lax
from jax.experimental import pallas as pl
from jax.experimental.pallas import tpu as pltpu
from jax.sharding import PartitionSpec as P

BLK = 128
TILE = 256
DOCS = 32
GROUP = 2

NT = (((1,), (1,)), ((), ()))


def flat(ref, at, count):
    return ref[at : at + count].reshape(count * BLK, ref.shape[2])


def flat_pair(refs, at, count):
    return jnp.concatenate([flat(ref, at, count) for ref in refs], axis=1)


def gram_kernel(kinds, tiles, finish, rows_ref, ids_ref, first_ref, *refs):
    per_row = 9
    nrows = len(kinds)
    row_refs = [refs[k * per_row : (k + 1) * per_row] for k in range(nrows)]
    init_ref, out_ref, h_prev, g_prev, acc = refs[nrows * per_row :]
    step = pl.program_id(0)
    steps = pl.num_programs(0)

    @pl.when(step == 0)
    def _():
        acc[...] = init_ref[...]
        for k in range(nrows):
            h_prev[k, 0] = jnp.zeros_like(h_prev[k, 0])
            g_prev[k, 0] = jnp.zeros_like(g_prev[k, 0])
            h_prev[k, 1] = flat_pair(row_refs[k][6:8], 0, 2)
            g_prev[k, 1] = flat(row_refs[k][8], 0, 2)

    place = lax.broadcasted_iota(jnp.int32, (TILE, TILE), 0)
    column = lax.broadcasted_iota(jnp.int32, (TILE, TILE), 1)
    triangle = jnp.where(
        place < column, jnp.float32(2.0), jnp.where(place == column, jnp.float32(1.0), jnp.float32(0.0))
    )
    docs = lax.broadcasted_iota(jnp.int32, (DOCS, TILE), 0)
    dot = functools.partial(lax.dot_general, dimension_numbers=NT, preferred_element_type=jnp.float32)
    for k, row in enumerate(kinds):
        share = jnp.zeros((DOCS, BLK), jnp.float32)
        line = slice(row, row + 1)
        for half in range(2):
            h_refs = row_refs[k][3 * half : 3 * half + 2]
            g_ref = row_refs[k][3 * half + 2]
            old_h = h_prev[k, half]
            old_g = g_prev[k, half]
            for t in range(tiles):
                number = half * steps * tiles + step * tiles + t
                at = 2 * number
                ids = jnp.concatenate([ids_ref[at, line], ids_ref[at + 1, line]], axis=1)
                first = jnp.concatenate([first_ref[at, line], first_ref[at + 1, line]], axis=1)
                first = first - number * TILE
                own_h = flat_pair(h_refs, 2 * t, 2)
                own_g = flat(g_ref, 2 * t, 2)
                pairs = dot(own_h, own_h) * dot(own_g, own_g) * triangle
                pairs = jnp.where(place >= first, pairs, jnp.float32(0.0))
                far = dot(old_h, own_h) * dot(old_g, own_g)
                far = jnp.where(place >= first + TILE, far, jnp.float32(0.0))
                total = jnp.sum(pairs + 2.0 * far, axis=0, keepdims=True)
                terms = jnp.where(docs == ids, jnp.broadcast_to(total, docs.shape), jnp.float32(0.0))
                share += terms[:, :BLK] + terms[:, BLK:]
                old_h, old_g = own_h, own_g
            h_prev[k, half] = old_h
            g_prev[k, half] = old_g
        here = pl.ds(pl.multiple_of(rows_ref[row] * DOCS, DOCS), DOCS)
        acc[here, :] += share

    @pl.when(step == steps - 1)
    def _():
        if finish:
            sums = jnp.sum(acc[...].T, axis=0, keepdims=True)
            out_ref[...] = jnp.broadcast_to(sums[None], out_ref.shape)
        else:
            out_ref[...] = acc[...]


def row_specs(count, steps, width, row):
    specs = []
    for offset in (0, steps):
        for _ in range(2):
            specs.append(pl.BlockSpec((count, BLK, BLK), lambda i, r, o=offset: (i + o, 0, 0)))
        specs.append(
            pl.BlockSpec((count, None, BLK, width), lambda i, r, o=offset: (i + o, row, 0, 0))
        )
    return specs


def gram(rows, ids, first, tiles, pieces, init, devices):
    blocks, _, _, width = pieces[0][3].shape
    steps = blocks // (4 * tiles)
    shape = (devices, 1, BLK) if devices else init.shape
    whole = pl.BlockSpec(ids.shape, lambda i, r: (0, 0, 0))
    last = steps * tiles - 1
    specs, operands = [], []
    for left, right, _, grad, place in pieces:
        specs += row_specs(2 * tiles, steps, width, place)
        specs += [pl.BlockSpec((2, BLK, BLK), lambda i, r: (last, 0, 0))] * 2
        specs += [pl.BlockSpec((2, None, BLK, width), lambda i, r, p=place: (last, p, 0, 0))]
        operands += [left, right, grad] * 3
    nrows = len(pieces)
    return pl.pallas_call(
        functools.partial(gram_kernel, [piece[2] for piece in pieces], tiles, bool(devices)),
        out_shape=jax.ShapeDtypeStruct(shape, jnp.float32),
        grid_spec=pltpu.PrefetchScalarGridSpec(
            num_scalar_prefetch=1,
            grid=(steps,),
            in_specs=[whole, whole, *specs, pl.BlockSpec(init.shape, lambda i, r: (0, 0))],
            out_specs=pl.BlockSpec(shape, lambda i, r: (0,) * len(shape)),
            scratch_shapes=[
                pltpu.VMEM((nrows, 2, TILE, TILE), jnp.bfloat16),
                pltpu.VMEM((nrows, 2, TILE, width), jnp.bfloat16),
                pltpu.VMEM(init.shape, jnp.float32),
            ],
        ),
        compiler_params=pltpu.CompilerParams(vmem_limit_bytes=50 * 2**20),
        cost_estimate=pl.CostEstimate(
            flops=nrows * blocks * BLK * 4 * TILE * (TILE + width),
            bytes_accessed=nrows * blocks * BLK * 2 * (TILE + width),
            transcendentals=0,
        ),
        name="gram",
    )(rows, ids, first, *operands, init)


def product_kernel(nrows, bound, rows_ref, ids_ref, norms_ref, *refs):
    per_row = 6
    row_refs = [refs[k * per_row : (k + 1) * per_row] for k in range(nrows)]
    out_ref, factor, scaled = refs[nrows * per_row :]
    step = pl.program_id(0)
    steps = pl.num_programs(0)
    blocks = ids_ref.shape[0]

    @pl.when(step == 0)
    def _():
        norms = jnp.sum(norms_ref[...], axis=0)
        clip = bound / jnp.maximum(jnp.sqrt(norms), bound) / nrows
        for k in range(nrows):
            ids = ids_ref[:, k, :] + rows_ref[k] * DOCS
            table = jnp.broadcast_to(clip, ids.shape)
            factor[k] = jnp.take_along_axis(table, ids, axis=1)

    lines = []
    for k in range(nrows):
        for half in range(2):
            for j in range(GROUP):
                at = half * (blocks // 2) + step * GROUP + j
                lines.append(factor[k, pl.ds(at, 1), :])
    used = len(lines)
    lines = jnp.concatenate(lines + [jnp.zeros((BLK - used, BLK), jnp.float32)], axis=0).T
    at = 0
    result = None
    for k in range(nrows):
        for half in range(2):
            h_refs = row_refs[k][3 * half : 3 * half + 2]
            g_ref = row_refs[k][3 * half + 2]
            begin = at * BLK
            for j in range(GROUP):
                scale = jnp.broadcast_to(lines[:, at : at + 1], (BLK, BLK))
                here = slice(at * BLK, (at + 1) * BLK)
                for c in range(0, g_ref.shape[2], BLK):
                    scaled[here, c : c + BLK] = (
                        g_ref[j, :, c : c + BLK].astype(jnp.float32) * scale
                    ).astype(jnp.bfloat16)
                at += 1
            share = lax.dot_general(
                flat_pair(h_refs, 0, GROUP),
                scaled[begin : at * BLK, :],
                (((0,), (0,)), ((), ())),
                preferred_element_type=jnp.float32,
            )
            result = share if result is None else result + share

    @pl.when(step == 0)
    def _():
        out_ref[...] = result

    @pl.when(step > 0)
    def _():
        out_ref[...] += result


def product(rows, ids, norms, pieces, bound):
    blocks, _, _, width = pieces[0][3].shape
    steps = blocks // (2 * GROUP)
    nrows = len(pieces)
    whole = pl.BlockSpec(ids.shape, lambda i, r: (0, 0, 0))
    specs, operands = [], []
    for left, right, _, grad, place in pieces:
        specs += row_specs(GROUP, steps, width, place)
        operands += [left, right, grad] * 2
    return pl.pallas_call(
        functools.partial(product_kernel, nrows, bound),
        out_shape=jax.ShapeDtypeStruct((TILE, width), jnp.float32),
        grid_spec=pltpu.PrefetchScalarGridSpec(
            num_scalar_prefetch=1,
            grid=(steps,),
            in_specs=[whole, pl.BlockSpec(norms.shape, lambda i, r: (0, 0, 0)), *specs],
            out_specs=pl.BlockSpec((TILE, width), lambda i, r: (0, 0)),
            scratch_shapes=[
                pltpu.VMEM((nrows, blocks, BLK), jnp.float32),
                pltpu.VMEM((nrows * 2 * GROUP * BLK, width), jnp.bfloat16),
            ],
        ),
        compiler_params=pltpu.CompilerParams(vmem_limit_bytes=24 * 2**20),
        cost_estimate=pl.CostEstimate(
            flops=2 * nrows * blocks * BLK * TILE * width,
            bytes_accessed=nrows * blocks * BLK * 2 * (TILE + width),
            transcendentals=0,
        ),
        name="product",
    )(rows, ids, norms, *operands)


def quarters_kernel(me_ref, ids_ref, *refs):
    ins, outs = refs[: len(refs) // 2], refs[len(refs) // 2 :]
    tokens = ins[0].shape[0]
    for in_ref, out_ref in zip(ins, outs):
        out_ref[:tokens, :] = in_ref[...]
        ids = ids_ref[...].astype(jnp.float32).astype(jnp.bfloat16)
        out_ref[tokens:, :BLK] = jnp.broadcast_to(ids, (16, BLK))
        out_ref[tokens:, BLK:] = jnp.zeros((16, out_ref.shape[1] - BLK), jnp.bfloat16)


def quarters(me, offsets, grad, ids):
    tokens, width = grad.shape
    count = len(offsets)
    part = width // count
    return pl.pallas_call(
        quarters_kernel,
        out_shape=[jax.ShapeDtypeStruct((tokens + 16, part), grad.dtype)] * count,
        grid_spec=pltpu.PrefetchScalarGridSpec(
            num_scalar_prefetch=1,
            grid=(1,),
            in_specs=[pl.BlockSpec(ids.shape, lambda i, m: (0, 0))]
            + [
                pl.BlockSpec((tokens, part), lambda i, m, o=o: (0, lax.rem(m[0] + o, count)))
                for o in offsets
            ],
            out_specs=[pl.BlockSpec((tokens + 16, part), lambda i, m: (0, 0))] * count,
        ),
        name="quarters",
    )(me, ids, *[grad] * count)


def columns_kernel(in_ref, left_ref, right_ref):
    for j in range(left_ref.shape[0]):
        left_ref[j] = in_ref[:, 2 * j * BLK : (2 * j + 1) * BLK]
        right_ref[j] = in_ref[:, (2 * j + 1) * BLK : (2 * j + 2) * BLK]


def columns(hidden, blocks, steps=4):
    tokens, width = hidden.shape
    count = blocks // steps
    half = pl.BlockSpec((count, tokens, BLK), lambda i: (i, 0, 0))
    return pl.pallas_call(
        columns_kernel,
        out_shape=[jax.ShapeDtypeStruct((blocks, tokens, BLK), hidden.dtype)] * 2,
        grid=(steps,),
        in_specs=[pl.BlockSpec((tokens, width // steps), lambda i: (0, i))],
        out_specs=[half, half],
        name="columns",
    )(hidden)


def shift(block, distance):
    size = lax.axis_size("dp")
    return lax.ppermute(block, "dp", [(i, (i + distance) % size) for i in range(size)])


def starts(ids):
    docs = jnp.arange(DOCS, dtype=jnp.int32)
    before = jnp.sum((ids[None] < docs[:, None, None, None]).astype(jnp.int32), axis=(1, 3))
    own = ids[None] == docs[:, None, None, None]
    return jnp.sum(jnp.where(own, before[:, None, :, None], 0), axis=0)


def body(hidden, grad_out, segment):
    row_count = lax.axis_size("dp")
    blocks = lax.axis_size("ctx")
    tokens, width_hidden = hidden.shape[1:]
    width_grad = grad_out.shape[2]
    me = lax.axis_index("dp")

    keep, up, down, across = quarters(me[None], (0, 1, 3, 2), grad_out[0], segment)
    received = [keep, shift(up, 1), shift(down, -1), shift(across, 2)]

    left, right = columns(hidden[0], blocks)
    left, right, *received = lax.optimization_barrier((left, right, *received))

    grads = jnp.stack([part[:tokens] for part in received])
    every_grad = lax.all_gather(grads, "ctx", axis=0, tiled=False)

    left = lax.all_to_all(left, "ctx", 0, 0, tiled=True)
    left_below, left_above = lax.optimization_barrier((shift(left, 1), shift(left, -1)))
    right, left_ready = lax.optimization_barrier((right, left))
    right = lax.all_to_all(right, "ctx", 0, 0, tiled=True)
    right_below, right_above = lax.optimization_barrier((shift(right, 1), shift(right, -1)))
    left_far = shift(left_below, 1)
    right_far = shift(right_above, -1)

    ids = jnp.stack([part[tokens, :BLK] for part in received]).astype(jnp.int32)
    ids, right_ready = lax.optimization_barrier((ids, right))
    ids = jnp.broadcast_to(ids[None], (blocks, row_count, tokens))
    ids = lax.all_to_all(ids, "ctx", 0, 0, tiled=True)
    first = starts(ids)

    rows = lax.rem(me + jnp.array([0, 3, 1, 2], jnp.int32), row_count)
    pieces = [
        (left, right, 0, every_grad, 0),
        (left_below, right_below, 1, every_grad, 1),
        (left_above, right_above, 2, every_grad, 2),
        (left_far, right_far, 3, every_grad, 3),
    ]
    zero = jnp.zeros((row_count * DOCS, BLK), jnp.float32)
    early = gram(rows, ids, first, 1, pieces[:3], zero, 0)
    partial = gram(rows, ids, first, 2, pieces[3:], early, row_count * blocks)
    norms = lax.all_to_all(partial, ("dp", "ctx"), 0, 0, tiled=True)

    bound = math.sqrt(tokens * width_hidden * width_grad)
    return product(rows, ids, norms, pieces, bound)


def solution(mesh):
    in_specs = (P("dp", "ctx", None), P("dp", "ctx", None), P("dp", "ctx"))
    out_specs = P("ctx", "dp")
    return jax.shard_map(body, mesh=mesh, in_specs=in_specs, out_specs=out_specs, check_vma=False)
```

time: 223 us -> 195 us (0.87)
  waiting for transfers between devices: 86.8 us -> 50.5 us
  local copies, waits for them, and re-layouts: 1.33 us -> 9.13 us
  Pallas kernels: 47.2 us -> 50.3 us
    all_to_all x1, waiting for transfers between devices: 39.5 us -> 7.5 us  [body(): ids = lax.all_to_all(ids, 'ctx', 0, 0, tiled=True)]
    ppermute x9, waiting for transfers between devices: 24.6 us -> 8.98 us  [shift(): lax.ppermute(block, 'dp', [(i, (i + distance) % size) for i in range(size)])]
    all_gather x1, waiting for transfers between devices: 0.02 us -> 12.2 us  [body(): every_grad = lax.all_gather(grads, 'ctx', axis=0, tiled=False)]
    unnamed x8 -> x16, local copies, waits for them, and re-layouts: 0.02 us -> 6.99 us
    pallas_call x2 -> x3, Pallas kernels: 28.7 us -> 30.7 us  [the longest x2 28.7 us: gram(): pl.pallas_call(functools.partial(gram_kernel, [piece[2] for piece in piec...]
  transfers between devices with their start and end apart: 12 -> 12, of which waited for: 5 -> 6; matrix products, arithmetic and copies ran while one was open for 1% -> 2% of each run, Pallas kernels for 2% -> 12%
where the time goes in v4:
time: 195 us; the launch traced here: 194 us
  waiting for transfers between devices  50.5 us (26%)
  Pallas kernels  50.3 us (26%)
  blocking collectives  47.5 us (24%)
  starting transfers between devices  19.6 us (10%)
  between operations  13.6 us (7%)
  local copies, waits for them, and re-layouts  9.13 us (5%)
  other arithmetic  3.63 us (2%)
    all_to_all x1, blocking collectives, body(): left = lax.all_to_all(left, 'ctx', 0, 0, tiled=True)  32.9 us
    pallas_call x2, Pallas kernels, gram(): pl.pallas_call(functools.partial(gram_kernel, [piece[2] for piece in piec...  28.7 us
    all_to_all x1, waiting for transfers between devices, body(): right = lax.all_to_all(right, 'ctx', 0, 0, tiled=True)  21.8 us
    pallas_call x1, Pallas kernels, product(): pl.pallas_call(functools.partial(product_kernel, nrows, bound), out_shape...  15.6 us
    all_to_all x1, blocking collectives, body(): norms = lax.all_to_all(partial, ('dp', 'ctx'), 0, 0, tiled=True)  14.6 us
    all_gather x1, waiting for transfers between devices, body(): every_grad = lax.all_gather(grads, 'ctx', axis=0, tiled=False)  12.2 us
    ppermute x9, waiting for transfers between devices, shift(): lax.ppermute(block, 'dp', [(i, (i + distance) % size) for i in range(size)])  8.98 us
    ppermute x9, starting transfers between devices, shift(): lax.ppermute(block, 'dp', [(i, (i + distance) % size) for i in range(size)])  8.77 us
  transfers between devices with their start and end apart: 12, of which 6 were waited for; matrix products, arithmetic and copies ran while one was open for 2% of the time, Pallas kernels for 12%

profile of v4, /device:TPU:1, one launch (start us, length us, event | category | flops | bytes accessed | tf_op | source)
XLA Modules:
  0.0 194.2 jit_solution(5164490993849005530)
XLA Ops:
  6.5 0.0 all-gather.3.cloned.1.call-start
  6.5 2.1 %quarters.1 = (bf16[144,640]{1,0:T(8,128)(2,1)}, bf16[144,640]{1,0:T(8,128)(2,1)}, bf16[144,640]{1,0:T(8,128)(2,1)}, bf16[144,640]{1,0:T(8,128)(2,1)}) custom-call(s32[1]{0:T(128)} %bitcast.1.me_ref, s32[1,128]{1,0:T(1,128)} %ids_ref.1, bf16[128,2560]{1,0:T(8,128)(2,1)} %bitcast.32, bf16[128,2560]{1,0:T(8,128)(2,1)} %bitcast.33, bf16[128,2560]{1,0:T(8,128)(2,1)} %bitcast.34, ...), custom_call_target="tpu_custom_call" | custom-call | tf_op jit(solution)/shard_map/quarters/pallas_call | solution.py:240
  8.6 2.1 %collective-permute-start = (bf16[144,640]{1,0:T(8,128)(2,1)}, bf16[144,640]{1,0:T(8,128)(2,1)S(1)}, u32[]{:S(2)}, u32[]{:S(2)}) collective-permute-start(bf16[144,640]{1,0:T(8,128)(2,1)} %get-tuple-element.26), channel_id=1, source_target_pairs={{0,32},{32,64},{64,96},{96,0},{1,33},{33,65},{65,97},{97,1},{2,34}... | collective-permute-start | bytes 552968 | tf_op jit(solution)/shard_map/ppermute | solution.py:279
  10.7 1.5 collective-permute-start.1
  12.2 1.6 collective-permute-start.2
  13.8 3.9 %columns.1 = (bf16[32,128,128]{2,1,0:T(8,128)(2,1)}, bf16[32,128,128]{2,1,0:T(8,128)(2,1)}) custom-call(bf16[128,8192]{1,0:T(8,128)(2,1)} %bitcast.36), custom_call_target="tpu_custom_call" | custom-call | tf_op jit(solution)/shard_map/columns/pallas_call | solution.py:267
  17.7 0.0 collective-permute-done
  17.7 0.0 collective-permute-done.1
  17.7 0.0 copy-start.5
  17.8 3.8 %collective-permute-done.2 = bf16[144,640]{1,0:T(8,128)(2,1)S(1)} collective-permute-done((bf16[144,640]{1,0:T(8,128)(2,1)}, bf16[144,640]{1,0:T(8,128)(2,1)S(1)}, u32[]{:S(2)}, u32[]{:S(2)}) %collective-permute-start.2) | collective-permute-done | bytes 184352 | tf_op jit(solution)/shard_map/ppermute | solution.py:279
  21.6 0.0 copy-done.4
  21.7 0.9 pad_maximum_fusion
  22.6 0.0 copy-done.5
  22.6 0.0 copy-done.6
  22.6 0.0 all-gather.3.cloned.1.call-update
  22.6 0.0 copy-done.3
  22.6 0.0 copy-start.7
  22.6 32.9 %all_to_all.20.refs_0_.refs_3_.refs_6_ = bf16[32,128,128]{2,1,0:T(8,128)(2,1)S(1)} all-to-all(bf16[32,128,128]{2,1,0:T(8,128)(2,1)S(1)} %copy-done.3), channel_id=1, replica_groups=mesh['dp'=4,'ctx'=32] {'ctx'}, dimensions={0} | all-to-all | bytes 2097152 | tf_op jit(solution)/shard_map/all_to_all | solution.py:305
  55.6 5.3 %all-to-all-start.1 = ((bf16[32,128,128]{2,1,0:T(8,128)(2,1)}), bf16[32,128,128]{2,1,0:T(8,128)(2,1)S(1)}, u32[]{:S(2)}, u32[]{:S(2)}) async-start(bf16[32,128,128]{2,1,0:T(8,128)(2,1)} %get-tuple-element.35), calls=%async_computation.1 | async-start | bytes 2097152 | tf_op jit(solution)/shard_map/all_to_all | solution.py:308
  60.9 0.8 collective-permute-start.4
  61.7 0.7 collective-permute-start.3
  62.4 21.8 %all-to-all-done.1.refs_1_.refs_4_.refs_7_ = bf16[32,128,128]{2,1,0:T(8,128)(2,1)S(1)} async-done(((bf16[32,128,128]{2,1,0:T(8,128)(2,1)}), bf16[32,128,128]{2,1,0:T(8,128)(2,1)S(1)}, u32[]{:S(2)}, u32[]{:S(2)}) %all-to-all-start.1) | async-done | bytes 1048608 | tf_op jit(solution)/shard_map/all_to_all | solution.py:308
  84.2 0.0 collective-permute-start.7
  84.2 1.5 collective-permute-start.6
  85.7 0.7 slice.26
  86.4 0.7 slice.27
  87.1 0.6 broadcast_in_dim.30
  87.7 5.6 %all-to-all-start.2 = ((s32[32,4,128]{2,1,0:T(4,128)}), s32[32,4,128]{2,1,0:T(4,128)S(1)}, u32[]{:S(2)}, u32[]{:S(2)}) async-start(s32[32,4,128]{2,1,0:T(4,128)} %broadcast_in_dim.30), calls=%async_computation.2 | async-start | bytes 131072 | tf_op jit(solution)/shard_map/all_to_all | solution.py:316
  93.3 0.0 copy-done.7
  93.3 0.0 collective-permute-done.4.refs_18_.refs_21_.refs_24_.refs_12_.refs_15_
  93.3 0.0 copy-start.1
  93.3 0.0 collective-permute-done.3.refs_9_.refs_12_.refs_15_.refs_6_
  93.3 0.3 collective-permute-start.5
  93.6 7.5 %all-to-all-done.2.ids_ref = s32[32,4,128]{2,1,0:T(4,128)S(1)} async-done(((s32[32,4,128]{2,1,0:T(4,128)}), s32[32,4,128]{2,1,0:T(4,128)S(1)}, u32[]{:S(2)}, u32[]{:S(2)}) %all-to-all-start.2) | async-done | bytes 65568 | tf_op jit(solution)/shard_map/all_to_all | solution.py:316
  101.1 2.4 %convert_reduce_fusion = s32[32,4]{1,0:T(8,128)S(1)} fusion(s32[32,4,128]{2,0,1:T(8,128)S(1)} %copy.5), kind=kLoop, calls=%fused_computation.1 | loop fusion | flops 1572736 | bytes 66048 | tf_op jit(solution)/shard_map/reduce_sum | solution.py:284
  103.5 0.3 select_reduce_fusion
  103.8 4.0 %collective-permute-done.7.refs_19_.refs_22_.refs_25_.refs_13_.refs_16_ = bf16[32,128,128]{2,1,0:T(8,128)(2,1)} collective-permute-done((bf16[32,128,128]{2,1,0:T(8,128)(2,1)S(1)}, bf16[32,128,128]{2,1,0:T(8,128)(2,1)}, u32[]{:S(2)}, u32[]{:S(2)}) %collective-permute-start.7) | collective-permute-done | bytes 1048608 | tf_op jit(solution)/shard_map/ppermute | solution.py:279
  107.8 1.2 collective-permute-done.6.refs_10_.refs_13_.refs_16_.refs_7_
  109.0 0.3 collective-permute-start.8
  109.3 12.2 %all-gather.3.cloned.1.call-done = bf16[128,128,640]{2,1,0:T(8,128)(2,1)} async-done(((bf16[4,128,640]{2,1,0:T(8,128)(2,1)}), bf16[128,128,640]{2,1,0:T(8,128)(2,1)}) %all-gather.3.cloned.1.call-update) | async-done | bytes 20971536 | tf_op jit(solution)/shard_map/all_gather | solution.py:303
  121.5 0.0 copy-done.1
  121.5 20.3 %gram.2.refs_9_ = f32[128,128]{1,0:T(8,128)S(1)} custom-call(s32[4]{0:T(128)S(1)} %compare_select_fusion.rows_ref, s32[32,4,128]{2,1,0:T(4,128)S(1)} %all-to-all-done.2.ids_ref, s32[32,4,128]{2,1,0:T(4,128)S(1)} %copy.7.first_ref, bf16[32,128,128]{2,1,0:T(8,128)(2,1)S(1)} %all_to_all.20.refs_0_.refs_3_.refs_6_, ...), custom_call_target="tpu_custom_call" | custom-call | flops 11274289152 | bytes 22020096 | tf_op jit(solution)/shard_map/gram/pallas_call | solution.py:113
  141.8 0.0 collective-permute-done.5.refs_0_.refs_3_.refs_6_.refs_18_.refs_21_
  141.9 0.0 collective-permute-done.8.refs_1_.refs_4_.refs_7_.refs_19_.refs_22_
  141.9 8.4 %gram.3 = f32[128,1,128]{2,1,0:T(1,128)S(1)} custom-call(s32[4]{0:T(128)S(1)} %compare_select_fusion.rows_ref, s32[32,4,128]{2,1,0:T(4,128)S(1)} %all-to-all-done.2.ids_ref, s32[32,4,128]{2,1,0:T(4,128)S(1)} %copy.7.first_ref, bf16[32,128,128]{2,1,0:T(8,128)(2,1)} %collective-permute-done.5.refs_0_.refs_3_.refs_6_.refs_18_.refs_21_, ...), custom_call_target="tpu_custom_call" | custom-call | flops 3758096384 | bytes 7340032 | tf_op jit(solution)/shard_map/gram/pallas_call | solution.py:113
  150.2 14.6 %all_to_all.21.norms_ref = f32[128,1,128]{2,1,0:T(1,128)S(1)} all-to-all(f32[128,1,128]{2,1,0:T(1,128)S(1)} %gram.3), channel_id=1, replica_groups=mesh['dp'=4,'ctx'=32] {'dp','ctx'}, dimensions={0} | all-to-all | bytes 131072 | tf_op jit(solution)/shard_map/all_to_all | solution.py:329
  164.8 7.0 %copy-done = bf16[128,128,640]{2,1,0:T(8,128)(2,1)S(1)} copy-done((bf16[128,128,640]{2,1,0:T(8,128)(2,1)S(1)}, bf16[128,128,640]{2,1,0:T(8,128)(2,1)}, u32[]{:S(2)}) %copy-start) | copy-done | bytes 20971544
  171.7 15.6 %product.1 = f32[256,640]{1,0:T(8,128)} custom-call(s32[4]{0:T(128)S(1)} %compare_select_fusion.rows_ref, s32[32,4,128]{2,1,0:T(4,128)S(1)} %all-to-all-done.2.ids_ref, f32[128,1,128]{2,1,0:T(1,128)S(1)} %all_to_all.21.norms_ref, bf16[32,128,128]{2,1,0:T(8,128)(2,1)S(1)} %all_to_all.20.refs_0_.refs_3_.refs_6_, ...), custom_call_target="tpu_custom_call" | custom-call | flops 5368709120 | bytes 29360128 | tf_op jit(solution)/shard_map/product/pallas_call | solution.py:203
  (15 shorter events, 0.2 us)
Async XLA Ops:
  6.5 115.0 %all-gather.3.cloned.1.call-start = ((), (), s32[]{:S(2)}) async-start(), calls=%async_computation.4 | async-start | bytes 21626880 | tf_op jit(solution)/shard_map/all_gather | solution.py:303
  8.6 13.0 %copy-start.4 = (bf16[144,640]{1,0:T(8,128)(2,1)S(1)}, bf16[144,640]{1,0:T(8,128)(2,1)}, u32[]{:S(2)}) copy-start(bf16[144,640]{1,0:T(8,128)(2,1)} %get-tuple-element.29) | copy-start | bytes 552964
  8.6 9.1 %collective-permute-start = (bf16[144,640]{1,0:T(8,128)(2,1)}, bf16[144,640]{1,0:T(8,128)(2,1)S(1)}, u32[]{:S(2)}, u32[]{:S(2)}) collective-permute-start(bf16[144,640]{1,0:T(8,128)(2,1)} %get-tuple-element.26), channel_id=1, source_target_pairs={{0,32},{32,64},{64,96},{96,0},{1,33},{33,65},{65,97},{97,1},{2,34}... | collective-permute-start | bytes 552968 | tf_op jit(solution)/shard_map/ppermute | solution.py:279
  10.7 7.0 %collective-permute-start.1 = (bf16[144,640]{1,0:T(8,128)(2,1)}, bf16[144,640]{1,0:T(8,128)(2,1)S(1)}, u32[]{:S(2)}, u32[]{:S(2)}) collective-permute-start(bf16[144,640]{1,0:T(8,128)(2,1)} %get-tuple-element.27), channel_id=1, source_target_pairs={{0,96},{32,0},{64,32},{96,64},{1,97},{33,1},{65,33},{97,65},{2,98}... | collective-permute-start | bytes 552968 | tf_op jit(solution)/shard_map/ppermute | solution.py:279
  12.2 9.3 %collective-permute-start.2 = (bf16[144,640]{1,0:T(8,128)(2,1)}, bf16[144,640]{1,0:T(8,128)(2,1)S(1)}, u32[]{:S(2)}, u32[]{:S(2)}) collective-permute-start(bf16[144,640]{1,0:T(8,128)(2,1)} %get-tuple-element.28), channel_id=1, source_target_pairs={{0,64},{32,96},{64,0},{96,32},{1,65},{33,97},{65,1},{97,33},{2,66}... | collective-permute-start | bytes 552968 | tf_op jit(solution)/shard_map/ppermute | solution.py:279
  17.7 4.9 %copy-start.3 = (bf16[32,128,128]{2,1,0:T(8,128)(2,1)S(1)}, bf16[32,128,128]{2,1,0:T(8,128)(2,1)}, u32[]{:S(2)}) copy-start(bf16[32,128,128]{2,1,0:T(8,128)(2,1)} %get-tuple-element.34) | copy-start | bytes 3145732
  17.7 4.8 %copy-start.5 = (bf16[144,640]{1,0:T(8,128)(2,1)}, bf16[144,640]{1,0:T(8,128)(2,1)S(1)}, u32[]{:S(2)}) copy-start(bf16[144,640]{1,0:T(8,128)(2,1)S(1)} %collective-permute-done.1) | copy-start | bytes 552964
  21.6 1.0 copy-start.6
  22.6 70.6 %copy-start.7 = (s32[4]{0:T(128)S(1)}, s32[4]{0:T(128)}, u32[]{:S(2)}) copy-start(s32[4]{0:T(128)} %constant.16.clone) | copy-start | bytes 52
  55.6 28.7 %all-to-all-start.1 = ((bf16[32,128,128]{2,1,0:T(8,128)(2,1)}), bf16[32,128,128]{2,1,0:T(8,128)(2,1)S(1)}, u32[]{:S(2)}, u32[]{:S(2)}) async-start(bf16[32,128,128]{2,1,0:T(8,128)(2,1)} %get-tuple-element.35), calls=%async_computation.1 | async-start | bytes 2097152 | tf_op jit(solution)/shard_map/all_to_all | solution.py:308
  60.9 32.5 %collective-permute-start.4 = (bf16[32,128,128]{2,1,0:T(8,128)(2,1)S(1)}, bf16[32,128,128]{2,1,0:T(8,128)(2,1)S(1)}, u32[]{:S(2)}, u32[]{:S(2)}) collective-permute-start(bf16[32,128,128]{2,1,0:T(8,128)(2,1)S(1)} %all_to_all.20.refs_0_.refs_3_.refs_6_), channel_id=1, source_target_pairs={{0,96},{32,0},{64,32},{96,64},{1,97},{33,1},{65,33},{97,65},{2,98}... | collective-permute-start | bytes 3145736 | tf_op jit(solution)/shard_map/ppermute | solution.py:279
  61.7 31.7 %collective-permute-start.3 = (bf16[32,128,128]{2,1,0:T(8,128)(2,1)S(1)}, bf16[32,128,128]{2,1,0:T(8,128)(2,1)}, u32[]{:S(2)}, u32[]{:S(2)}) collective-permute-start(bf16[32,128,128]{2,1,0:T(8,128)(2,1)S(1)} %all_to_all.20.refs_0_.refs_3_.refs_6_), channel_id=1, source_target_pairs={{0,32},{32,64},{64,96},{96,0},{1,33},{33,65},{65,97},{97,1},{2,34}... | collective-permute-start | bytes 3145736 | tf_op jit(solution)/shard_map/ppermute | solution.py:279
  84.2 23.6 %collective-permute-start.7 = (bf16[32,128,128]{2,1,0:T(8,128)(2,1)S(1)}, bf16[32,128,128]{2,1,0:T(8,128)(2,1)}, u32[]{:S(2)}, u32[]{:S(2)}) collective-permute-start(bf16[32,128,128]{2,1,0:T(8,128)(2,1)S(1)} %all-to-all-done.1.refs_1_.refs_4_.refs_7_), channel_id=1, source_target_pairs={{0,96},{32,0},{64,32},{96,64},{1,97},{33,1},{65,33},{97,65},{2,98}... | collective-permute-start | bytes 3145736 | tf_op jit(solution)/shard_map/ppermute | solution.py:279
  84.2 24.8 %collective-permute-start.6 = (bf16[32,128,128]{2,1,0:T(8,128)(2,1)S(1)}, bf16[32,128,128]{2,1,0:T(8,128)(2,1)}, u32[]{:S(2)}, u32[]{:S(2)}) collective-permute-start(bf16[32,128,128]{2,1,0:T(8,128)(2,1)S(1)} %all-to-all-done.1.refs_1_.refs_4_.refs_7_), channel_id=1, source_target_pairs={{0,32},{32,64},{64,96},{96,0},{1,33},{33,65},{65,97},{97,1},{2,34}... | collective-permute-start | bytes 3145736 | tf_op jit(solution)/shard_map/ppermute | solution.py:279
  87.7 13.4 %all-to-all-start.2 = ((s32[32,4,128]{2,1,0:T(4,128)}), s32[32,4,128]{2,1,0:T(4,128)S(1)}, u32[]{:S(2)}, u32[]{:S(2)}) async-start(s32[32,4,128]{2,1,0:T(4,128)} %broadcast_in_dim.30), calls=%async_computation.2 | async-start | bytes 131072 | tf_op jit(solution)/shard_map/all_to_all | solution.py:316
  93.3 28.2 %copy-start.1 = (bf16[32,128,128]{2,1,0:T(8,128)(2,1)}, bf16[32,128,128]{2,1,0:T(8,128)(2,1)S(1)}, u32[]{:S(2)}) copy-start(bf16[32,128,128]{2,1,0:T(8,128)(2,1)S(1)} %collective-permute-done.4.refs_18_.refs_21_.refs_24_.refs_12_.refs_15_) | copy-start | bytes 3145732
  93.3 48.5 %collective-permute-start.5 = (bf16[32,128,128]{2,1,0:T(8,128)(2,1)}, bf16[32,128,128]{2,1,0:T(8,128)(2,1)}, u32[]{:S(2)}, u32[]{:S(2)}) collective-permute-start(bf16[32,128,128]{2,1,0:T(8,128)(2,1)} %collective-permute-done.3.refs_9_.refs_12_.refs_15_.refs_6_), channel_id=1, source_target_pairs={{0,32},{32,64},{64,96},{96,0},{1,33},{33,65},{65,97},{97,1},{2,34}... | collective-permute-start | bytes 3145736 | tf_op jit(solution)/shard_map/ppermute | solution.py:279
  109.0 32.9 %collective-permute-start.8 = (bf16[32,128,128]{2,1,0:T(8,128)(2,1)}, bf16[32,128,128]{2,1,0:T(8,128)(2,1)}, u32[]{:S(2)}, u32[]{:S(2)}) collective-permute-start(bf16[32,128,128]{2,1,0:T(8,128)(2,1)} %collective-permute-done.7.refs_19_.refs_22_.refs_25_.refs_13_.refs_16_), channel_id=1, source_target_pairs={{0,96},{32,0},{64,32},{96,64},{1,97},{33,1},{65,33},{97,65},{2,98}... | collective-permute-start | bytes 3145736 | tf_op jit(solution)/shard_map/ppermute | solution.py:279
  141.8 22.9 %copy-start.2 = (bf16[32,128,128]{2,1,0:T(8,128)(2,1)S(1)}, bf16[32,128,128]{2,1,0:T(8,128)(2,1)}, u32[]{:S(2)}) copy-start(bf16[32,128,128]{2,1,0:T(8,128)(2,1)} %copy-done.1) | copy-start | bytes 3145732
  164.8 7.0 %copy-start = (bf16[128,128,640]{2,1,0:T(8,128)(2,1)S(1)}, bf16[128,128,640]{2,1,0:T(8,128)(2,1)}, u32[]{:S(2)}) copy-start(bf16[128,128,640]{2,1,0:T(8,128)(2,1)} %all-gather.3.cloned.1.call-done) | copy-start | bytes 62914564
Sparse Core Ops, SparseCore 0:
  22.7 98.7 all-gather.2

commit v5 on v4

v5 whole, which is shorter than its diff:
```python
import functools
import math

import jax
import jax.numpy as jnp
from jax import lax
from jax.experimental import pallas as pl
from jax.experimental.pallas import tpu as pltpu
from jax.sharding import PartitionSpec as P

BLK = 128
TILE = 256
DOCS = 32
GROUP = 4

NT = (((1,), (1,)), ((), ()))
TN = (((0,), (0,)), ((), ()))


def flat(block):
    return block.reshape(block.shape[0] * block.shape[1], block.shape[2])


def columns_of(refs, at, count):
    return jnp.concatenate([flat(ref[pl.ds(at, count)]) for ref in refs], axis=1)


def gram_kernel(kinds, tiles, finish, rows_ref, ids_ref, first_ref, *refs):
    nrows = len(kinds)
    h_refs = [refs[2 * k : 2 * k + 2] for k in range(nrows)]
    g_ref, init_ref, out_ref, g_prev, acc = refs[2 * nrows :]
    step = pl.program_id(0)

    @pl.when(step == 0)
    def _():
        acc[...] = init_ref[...]
        g_prev[...] = jnp.zeros_like(g_prev)

    place = lax.broadcasted_iota(jnp.int32, (TILE, TILE), 0)
    column = lax.broadcasted_iota(jnp.int32, (TILE, TILE), 1)
    triangle = jnp.where(
        place < column, jnp.float32(2.0), jnp.where(place == column, jnp.float32(1.0), jnp.float32(0.0))
    )
    docs = lax.broadcasted_iota(jnp.int32, (DOCS, TILE), 0)
    dot = functools.partial(lax.dot_general, dimension_numbers=NT, preferred_element_type=jnp.float32)
    for k, row in enumerate(kinds):
        share = jnp.zeros((DOCS, BLK), jnp.float32)
        line = slice(row, row + 1)
        old_h = columns_of(h_refs[k], jnp.maximum(2 * step * tiles - 2, 0), 2)
        old_g = g_prev[k]
        for t in range(tiles):
            number = step * tiles + t
            at = 2 * number
            ids = jnp.concatenate([ids_ref[at, line], ids_ref[at + 1, line]], axis=1)
            first = jnp.concatenate([first_ref[at, line], first_ref[at + 1, line]], axis=1)
            first = first - number * TILE
            own_h = columns_of(h_refs[k], at, 2)
            own_g = flat(g_ref[2 * t : 2 * t + 2, k])
            pairs = dot(own_h, own_h) * dot(own_g, own_g) * triangle
            pairs = jnp.where(place >= first, pairs, jnp.float32(0.0))
            far = dot(old_h, own_h) * dot(old_g, own_g)
            far = jnp.where(place >= first + TILE, far, jnp.float32(0.0))
            total = jnp.sum(pairs + 2.0 * far, axis=0, keepdims=True)
            terms = jnp.where(docs == ids, jnp.broadcast_to(total, docs.shape), jnp.float32(0.0))
            share += terms[:, :BLK] + terms[:, BLK:]
            old_h, old_g = own_h, own_g
        g_prev[k] = old_g
        here = pl.ds(pl.multiple_of(rows_ref[row] * DOCS, DOCS), DOCS)
        acc[here, :] += share

    @pl.when(step == pl.num_programs(0) - 1)
    def _():
        if finish:
            sums = jnp.sum(acc[...].T, axis=0, keepdims=True)
            out_ref[...] = jnp.broadcast_to(sums[None], out_ref.shape)
        else:
            out_ref[...] = acc[...]


def gram(rows, ids, first, tiles, kinds, hidden, grad, init, devices):
    blocks, _, _, width = grad.shape
    nrows = len(kinds)
    count = 2 * tiles
    shape = (devices, 1, BLK) if devices else init.shape
    whole = pl.BlockSpec(ids.shape, lambda i, r: (0, 0, 0))
    place = kinds[0] // nrows
    return pl.pallas_call(
        functools.partial(gram_kernel, kinds, tiles, bool(devices)),
        out_shape=jax.ShapeDtypeStruct(shape, jnp.float32),
        grid_spec=pltpu.PrefetchScalarGridSpec(
            num_scalar_prefetch=1,
            grid=(blocks // count,),
            in_specs=[
                whole,
                whole,
                *[pl.BlockSpec(memory_space=pltpu.VMEM)] * (2 * nrows),
                pl.BlockSpec((count, nrows, BLK, width), lambda i, r: (i, place, 0, 0)),
                pl.BlockSpec(init.shape, lambda i, r: (0, 0)),
            ],
            out_specs=pl.BlockSpec(shape, lambda i, r: (0,) * len(shape)),
            scratch_shapes=[
                pltpu.VMEM((nrows, TILE, width), jnp.bfloat16),
                pltpu.VMEM(init.shape, jnp.float32),
            ],
        ),
        compiler_params=pltpu.CompilerParams(vmem_limit_bytes=40 * 2**20),
        cost_estimate=pl.CostEstimate(
            flops=nrows * blocks * BLK * 4 * TILE * (TILE + width),
            bytes_accessed=nrows * blocks * BLK * 2 * (TILE + width),
            transcendentals=0,
        ),
        name="gram",
    )(rows, ids, first, *[half for pair in hidden for half in pair], grad, init)


def product_kernel(nrows, bound, rows_ref, ids_ref, norms_ref, *refs):
    h_refs = [refs[2 * k : 2 * k + 2] for k in range(nrows)]
    g_ref, out_ref, factor, scaled = refs[2 * nrows :]
    step = pl.program_id(0)

    @pl.when(step == 0)
    def _():
        norms = jnp.sum(norms_ref[...], axis=0)
        clip = bound / jnp.maximum(jnp.sqrt(norms), bound) / nrows
        for k in range(nrows):
            ids = ids_ref[:, k, :] + rows_ref[k] * DOCS
            table = jnp.broadcast_to(clip, ids.shape)
            factor[k] = jnp.take_along_axis(table, ids, axis=1)

    lines = [factor[k, pl.ds(step * GROUP + j, 1), :] for k in range(nrows) for j in range(GROUP)]
    used = len(lines)
    lines = jnp.concatenate(lines + [jnp.zeros((BLK - used, BLK), jnp.float32)], axis=0).T
    result = None
    for k in range(nrows):
        for j in range(GROUP):
            at = k * GROUP + j
            scale = jnp.broadcast_to(lines[:, at : at + 1], (BLK, BLK))
            for c in range(0, g_ref.shape[3], BLK):
                scaled[at * BLK : (at + 1) * BLK, c : c + BLK] = (
                    g_ref[j, k, :, c : c + BLK].astype(jnp.float32) * scale
                ).astype(jnp.bfloat16)
        share = lax.dot_general(
            columns_of(h_refs[k], step * GROUP, GROUP),
            scaled[k * GROUP * BLK : (k + 1) * GROUP * BLK, :],
            TN,
            preferred_element_type=jnp.float32,
        )
        result = share if result is None else result + share

    @pl.when(step == 0)
    def _():
        out_ref[...] = result

    @pl.when(step > 0)
    def _():
        out_ref[...] += result


def product(rows, ids, norms, hidden, grad, bound):
    blocks, nrows, _, width = grad.shape
    return pl.pallas_call(
        functools.partial(product_kernel, nrows, bound),
        out_shape=jax.ShapeDtypeStruct((TILE, width), jnp.float32),
        grid_spec=pltpu.PrefetchScalarGridSpec(
            num_scalar_prefetch=1,
            grid=(blocks // GROUP,),
            in_specs=[
                pl.BlockSpec(ids.shape, lambda i, r: (0, 0, 0)),
                pl.BlockSpec(norms.shape, lambda i, r: (0, 0, 0)),
                *[pl.BlockSpec(memory_space=pltpu.VMEM)] * (2 * nrows),
                pl.BlockSpec((GROUP, nrows, BLK, width), lambda i, r: (i, 0, 0, 0)),
            ],
            out_specs=pl.BlockSpec((TILE, width), lambda i, r: (0, 0)),
            scratch_shapes=[
                pltpu.VMEM((nrows, blocks, BLK), jnp.float32),
                pltpu.VMEM((nrows * GROUP * BLK, width), jnp.bfloat16),
            ],
        ),
        compiler_params=pltpu.CompilerParams(vmem_limit_bytes=40 * 2**20),
        cost_estimate=pl.CostEstimate(
            flops=2 * nrows * blocks * BLK * TILE * width,
            bytes_accessed=nrows * blocks * BLK * 2 * (TILE + width),
            transcendentals=0,
        ),
        name="product",
    )(rows, ids, norms, *[half for pair in hidden for half in pair], grad)


def quarters_kernel(me_ref, ids_ref, *refs):
    ins, outs = refs[: len(refs) // 2], refs[len(refs) // 2 :]
    tokens = ins[0].shape[0]
    for in_ref, out_ref in zip(ins, outs):
        out_ref[:tokens, :] = in_ref[...]
        ids = ids_ref[...].astype(jnp.float32).astype(jnp.bfloat16)
        out_ref[tokens:, :BLK] = jnp.broadcast_to(ids, (16, BLK))
        out_ref[tokens:, BLK:] = jnp.zeros((16, out_ref.shape[1] - BLK), jnp.bfloat16)


def quarters(me, offsets, grad, ids):
    tokens, width = grad.shape
    count = len(offsets)
    part = width // count
    return pl.pallas_call(
        quarters_kernel,
        out_shape=[jax.ShapeDtypeStruct((tokens + 16, part), grad.dtype)] * count,
        grid_spec=pltpu.PrefetchScalarGridSpec(
            num_scalar_prefetch=1,
            grid=(1,),
            in_specs=[pl.BlockSpec(ids.shape, lambda i, m: (0, 0))]
            + [
                pl.BlockSpec((tokens, part), lambda i, m, o=o: (0, lax.rem(m[0] + o, count)))
                for o in offsets
            ],
            out_specs=[pl.BlockSpec((tokens + 16, part), lambda i, m: (0, 0))] * count,
        ),
        name="quarters",
    )(me, ids, *[grad] * count)


def columns_kernel(in_ref, left_ref, right_ref):
    for j in range(left_ref.shape[0]):
        left_ref[j] = in_ref[:, 2 * j * BLK : (2 * j + 1) * BLK]
        right_ref[j] = in_ref[:, (2 * j + 1) * BLK : (2 * j + 2) * BLK]


def columns(hidden, blocks, steps=4):
    tokens, width = hidden.shape
    count = blocks // steps
    half = pl.BlockSpec((count, tokens, BLK), lambda i: (i, 0, 0))
    return pl.pallas_call(
        columns_kernel,
        out_shape=[jax.ShapeDtypeStruct((blocks, tokens, BLK), hidden.dtype)] * 2,
        grid=(steps,),
        in_specs=[pl.BlockSpec((tokens, width // steps), lambda i: (0, i))],
        out_specs=[half, half],
        name="columns",
    )(hidden)


def shift(block, distance):
    size = lax.axis_size("dp")
    return lax.ppermute(block, "dp", [(i, (i + distance) % size) for i in range(size)])


def starts(ids):
    docs = jnp.arange(DOCS, dtype=jnp.int32)
    before = jnp.sum((ids[None] < docs[:, None, None, None]).astype(jnp.int32), axis=(1, 3))
    own = ids[None] == docs[:, None, None, None]
    return jnp.sum(jnp.where(own, before[:, None, :, None], 0), axis=0)


def body(hidden, grad_out, segment):
    row_count = lax.axis_size("dp")
    blocks = lax.axis_size("ctx")
    tokens, width_hidden = hidden.shape[1:]
    width_grad = grad_out.shape[2]
    me = lax.axis_index("dp")

    keep, up, down, across = quarters(me[None], (0, 1, 3, 2), grad_out[0], segment)
    received = [keep, shift(up, 1), shift(down, -1), shift(across, 2)]

    left, right = columns(hidden[0], blocks)
    left, right, *received = lax.optimization_barrier((left, right, *received))

    grads = jnp.stack([part[:tokens] for part in received])
    every_grad = lax.all_gather(grads, "ctx", axis=0, tiled=False)

    left = lax.all_to_all(left, "ctx", 0, 0, tiled=True)
    left_below, left_above = lax.optimization_barrier((shift(left, 1), shift(left, -1)))
    right, left_ready = lax.optimization_barrier((right, left))
    right = lax.all_to_all(right, "ctx", 0, 0, tiled=True)
    right_below, right_above = lax.optimization_barrier((shift(right, 1), shift(right, -1)))
    left_far = shift(left_below, 1)
    right_far = shift(right_above, -1)

    ids = jnp.stack([part[tokens, :BLK] for part in received]).astype(jnp.int32)
    ids, right_ready = lax.optimization_barrier((ids, right))
    ids = jnp.broadcast_to(ids[None], (blocks, row_count, tokens))
    ids = lax.all_to_all(ids, "ctx", 0, 0, tiled=True)
    first = starts(ids)

    rows = lax.rem(me + jnp.array([0, 3, 1, 2], jnp.int32), row_count)
    pairs = [
        (left, right),
        (left_below, right_below),
        (left_above, right_above),
        (left_far, right_far),
    ]
    zero = jnp.zeros((row_count * DOCS, BLK), jnp.float32)
    early = gram(rows, ids, first, 2, (0, 1, 2), pairs[:3], every_grad, zero, 0)
    partial = gram(rows, ids, first, 4, (3,), pairs[3:], every_grad, early, row_count * blocks)
    norms = lax.all_to_all(partial, ("dp", "ctx"), 0, 0, tiled=True)

    bound = math.sqrt(tokens * width_hidden * width_grad)
    return product(rows, ids, norms, pairs, every_grad, bound)


def solution(mesh):
    in_specs = (P("dp", "ctx", None), P("dp", "ctx", None), P("dp", "ctx"))
    out_specs = P("ctx", "dp")
    return jax.shard_map(body, mesh=mesh, in_specs=in_specs, out_specs=out_specs, check_vma=False)
```

time: 195 us -> 190 us (0.974)
  local copies, waits for them, and re-layouts: 9.13 us -> 6.66 us
    unnamed x16 -> x22, local copies, waits for them, and re-layouts: 6.99 us -> 4.61 us
where the time goes in v5:
time: 190 us; the launch traced here: 189 us
  Pallas kernels  50 us (26%)
  waiting for transfers between devices  48.6 us (26%)
  blocking collectives  47.5 us (25%)
  starting transfers between devices  19.5 us (10%)
  between operations  13.6 us (7%)
  local copies, waits for them, and re-layouts  6.66 us (4%)
  other arithmetic  3.63 us (2%)
    all_to_all x1, blocking collectives, body(): left = lax.all_to_all(left, 'ctx', 0, 0, tiled=True)  32.9 us
    pallas_call x2, Pallas kernels, gram(): pl.pallas_call(functools.partial(gram_kernel, kinds, tiles, bool(devices)...  27.6 us
    all_to_all x1, waiting for transfers between devices, body(): right = lax.all_to_all(right, 'ctx', 0, 0, tiled=True)  21.8 us
    pallas_call x1, Pallas kernels, product(): pl.pallas_call(functools.partial(product_kernel, nrows, bound), out_shape...  16.5 us
    all_to_all x1, blocking collectives, body(): norms = lax.all_to_all(partial, ('dp', 'ctx'), 0, 0, tiled=True)  14.5 us
    all_gather x1, waiting for transfers between devices, body(): every_grad = lax.all_gather(grads, 'ctx', axis=0, tiled=False)  12.2 us
    ppermute x9, starting transfers between devices, shift(): lax.ppermute(block, 'dp', [(i, (i + distance) % size) for i in range(size)])  8.7 us
    ppermute x9, waiting for transfers between devices, shift(): lax.ppermute(block, 'dp', [(i, (i + distance) % size) for i in range(size)])  7.98 us
  transfers between devices with their start and end apart: 12, of which 6 were waited for; matrix products, arithmetic and copies ran while one was open for 2% of the time, Pallas kernels for 12%

profile of v5, /device:TPU:1, one launch (start us, length us, event | category | flops | bytes accessed | tf_op | source)
XLA Modules:
  0.0 189.5 jit_solution(8524542292946923008)
XLA Ops:
  6.5 0.0 all-gather.3.cloned.1.call-start
  6.5 2.1 %quarters.1 = (bf16[144,640]{1,0:T(8,128)(2,1)}, bf16[144,640]{1,0:T(8,128)(2,1)}, bf16[144,640]{1,0:T(8,128)(2,1)}, bf16[144,640]{1,0:T(8,128)(2,1)}) custom-call(s32[1]{0:T(128)} %bitcast.1.me_ref, s32[1,128]{1,0:T(1,128)} %ids_ref.1, bf16[128,2560]{1,0:T(8,128)(2,1)} %bitcast.15, bf16[128,2560]{1,0:T(8,128)(2,1)} %bitcast.16, bf16[128,2560]{1,0:T(8,128)(2,1)} %bitcast.17, ...), custom_call_target="tpu_custom_call" | custom-call | tf_op jit(solution)/shard_map/quarters/pallas_call | solution.py:203
  8.6 2.1 %collective-permute-start = (bf16[144,640]{1,0:T(8,128)(2,1)}, bf16[144,640]{1,0:T(8,128)(2,1)S(1)}, u32[]{:S(2)}, u32[]{:S(2)}) collective-permute-start(bf16[144,640]{1,0:T(8,128)(2,1)} %get-tuple-element.26), channel_id=1, source_target_pairs={{0,32},{32,64},{64,96},{96,0},{1,33},{33,65},{65,97},{97,1},{2,34}... | collective-permute-start | bytes 552968 | tf_op jit(solution)/shard_map/ppermute | solution.py:242
  10.7 1.5 collective-permute-start.1
  12.2 1.6 collective-permute-start.2
  13.8 3.9 %columns.1 = (bf16[32,128,128]{2,1,0:T(8,128)(2,1)}, bf16[32,128,128]{2,1,0:T(8,128)(2,1)}) custom-call(bf16[128,8192]{1,0:T(8,128)(2,1)} %bitcast.19), custom_call_target="tpu_custom_call" | custom-call | tf_op jit(solution)/shard_map/columns/pallas_call | solution.py:230
  17.7 0.0 collective-permute-done
  17.7 0.0 collective-permute-done.1
  17.7 0.0 copy-start.8
  17.7 3.8 %collective-permute-done.2 = bf16[144,640]{1,0:T(8,128)(2,1)S(1)} collective-permute-done((bf16[144,640]{1,0:T(8,128)(2,1)}, bf16[144,640]{1,0:T(8,128)(2,1)S(1)}, u32[]{:S(2)}, u32[]{:S(2)}) %collective-permute-start.2) | collective-permute-done | bytes 184352 | tf_op jit(solution)/shard_map/ppermute | solution.py:242
  21.5 0.0 copy-done.7
  21.6 0.9 pad_maximum_fusion
  22.6 0.0 copy-done.8
  22.6 0.0 all-gather.3.cloned.1.call-update
  22.6 0.0 copy-start.10
  22.6 32.9 %all_to_all.20.refs_0_ = bf16[32,128,128]{2,1,0:T(8,128)(2,1)S(1)} all-to-all(bf16[32,128,128]{2,1,0:T(8,128)(2,1)S(1)} %copy-done.6), channel_id=1, replica_groups=mesh['dp'=4,'ctx'=32] {'ctx'}, dimensions={0} | all-to-all | bytes 2097152 | tf_op jit(solution)/shard_map/all_to_all | solution.py:268
  55.6 5.3 %all-to-all-start.1 = ((bf16[32,128,128]{2,1,0:T(8,128)(2,1)}), bf16[32,128,128]{2,1,0:T(8,128)(2,1)S(1)}, u32[]{:S(2)}, u32[]{:S(2)}) async-start(bf16[32,128,128]{2,1,0:T(8,128)(2,1)} %get-tuple-element.35), calls=%async_computation.1 | async-start | bytes 2097152 | tf_op jit(solution)/shard_map/all_to_all | solution.py:271
  60.8 0.8 collective-permute-start.4
  61.7 0.7 collective-permute-start.3
  62.4 21.8 %all-to-all-done.1.refs_1_ = bf16[32,128,128]{2,1,0:T(8,128)(2,1)S(1)} async-done(((bf16[32,128,128]{2,1,0:T(8,128)(2,1)}), bf16[32,128,128]{2,1,0:T(8,128)(2,1)S(1)}, u32[]{:S(2)}, u32[]{:S(2)}) %all-to-all-start.1) | async-done | bytes 1048608 | tf_op jit(solution)/shard_map/all_to_all | solution.py:271
  84.2 0.0 collective-permute-start.7
  84.2 1.5 collective-permute-start.6
  85.7 1.1 copy-done
  86.8 0.6 slice.26
  87.4 0.6 slice.27
  88.0 0.6 broadcast_in_dim.30
  88.7 5.6 %all-to-all-start.2 = ((s32[32,4,128]{2,1,0:T(4,128)}), s32[32,4,128]{2,1,0:T(4,128)S(1)}, u32[]{:S(2)}, u32[]{:S(2)}) async-start(s32[32,4,128]{2,1,0:T(4,128)} %broadcast_in_dim.30), calls=%async_computation.2 | async-start | bytes 131072 | tf_op jit(solution)/shard_map/all_to_all | solution.py:279
  94.2 0.0 copy-done.10
  94.3 0.0 collective-permute-done.4.refs_4_
  94.3 1.1 copy-done.3
  95.4 0.0 collective-permute-done.3.refs_2_
  95.4 0.2 collective-permute-start.5
  95.6 6.6 %all-to-all-done.2.ids_ref = s32[32,4,128]{2,1,0:T(4,128)S(1)} async-done(((s32[32,4,128]{2,1,0:T(4,128)}), s32[32,4,128]{2,1,0:T(4,128)S(1)}, u32[]{:S(2)}, u32[]{:S(2)}) %all-to-all-start.2) | async-done | bytes 65568 | tf_op jit(solution)/shard_map/all_to_all | solution.py:279
  102.1 2.4 %convert_reduce_fusion = s32[32,4]{1,0:T(8,128)S(1)} fusion(s32[32,4,128]{2,0,1:T(8,128)S(1)} %copy.5), kind=kLoop, calls=%fused_computation.1 | loop fusion | flops 1572736 | bytes 66048 | tf_op jit(solution)/shard_map/reduce_sum | solution.py:247
  104.5 0.3 select_reduce_fusion
  104.9 2.9 %collective-permute-done.7.refs_5_ = bf16[32,128,128]{2,1,0:T(8,128)(2,1)} collective-permute-done((bf16[32,128,128]{2,1,0:T(8,128)(2,1)S(1)}, bf16[32,128,128]{2,1,0:T(8,128)(2,1)}, u32[]{:S(2)}, u32[]{:S(2)}) %collective-permute-start.7) | collective-permute-done | bytes 1048608 | tf_op jit(solution)/shard_map/ppermute | solution.py:242
  107.8 1.2 collective-permute-done.6.refs_3_
  109.0 0.3 collective-permute-start.8
  109.3 12.2 %all-gather.3.cloned.1.call-done = bf16[128,128,640]{2,1,0:T(8,128)(2,1)} async-done(((bf16[4,128,640]{2,1,0:T(8,128)(2,1)}), bf16[128,128,640]{2,1,0:T(8,128)(2,1)}) %all-gather.3.cloned.1.call-update) | async-done | bytes 20971536 | tf_op jit(solution)/shard_map/all_gather | solution.py:266
  121.5 1.2 copy-done.1
  122.7 1.2 copy-done.4
  123.9 19.7 %gram.2.refs_3_ = f32[128,128]{1,0:T(8,128)S(1)} custom-call(s32[4]{0:T(128)S(1)} %compare_select_fusion.rows_ref, s32[32,4,128]{2,1,0:T(4,128)S(1)} %all-to-all-done.2.ids_ref, s32[32,4,128]{2,1,0:T(4,128)S(1)} %copy.7.first_ref, bf16[32,128,128]{2,1,0:T(8,128)(2,1)S(1)} %all_to_all.20.refs_0_, bf16[32,128,128]{2,1,0:T(8,128)(2,1)S(1)} %copy-done.1, ...), custom_call_target="tpu_custom_call" | custom-call | flops 11274289152 | bytes 22020096 | tf_op jit(solution)/shard_map/gram/pallas_call | solution.py:87
  143.6 0.0 collective-permute-done.5.refs_0_.refs_6_
  143.6 0.0 collective-permute-done.8.refs_1_.refs_7_
  143.6 7.9 %gram.3 = f32[128,1,128]{2,1,0:T(1,128)S(1)} custom-call(s32[4]{0:T(128)S(1)} %compare_select_fusion.rows_ref, s32[32,4,128]{2,1,0:T(4,128)S(1)} %all-to-all-done.2.ids_ref, s32[32,4,128]{2,1,0:T(4,128)S(1)} %copy.7.first_ref, bf16[32,128,128]{2,1,0:T(8,128)(2,1)S(1)} %collective-permute-done.5.refs_0_.refs_6_, ...), custom_call_target="tpu_custom_call" | custom-call | flops 3758096384 | bytes 7340032 | tf_op jit(solution)/shard_map/gram/pallas_call | solution.py:87
  151.6 14.5 %all_to_all.21.norms_ref = f32[128,1,128]{2,1,0:T(1,128)S(1)} all-to-all(f32[128,1,128]{2,1,0:T(1,128)S(1)} %gram.3), channel_id=1, replica_groups=mesh['dp'=4,'ctx'=32] {'dp','ctx'}, dimensions={0} | all-to-all | bytes 131072 | tf_op jit(solution)/shard_map/all_to_all | solution.py:292
  166.1 0.0 copy-done.5
  166.1 16.5 %product.1 = f32[256,640]{1,0:T(8,128)} custom-call(s32[4]{0:T(128)S(1)} %compare_select_fusion.rows_ref, s32[32,4,128]{2,1,0:T(4,128)S(1)} %all-to-all-done.2.ids_ref, f32[128,1,128]{2,1,0:T(1,128)S(1)} %all_to_all.21.norms_ref, bf16[32,128,128]{2,1,0:T(8,128)(2,1)S(1)} %all_to_all.20.refs_0_, bf16[32,128,128]{2,1,0:T(8,128)(2,1)S(1)} %copy-done.2, ...), custom_call_target="tpu_custom_call" | custom-call | flops 5368709120 | bytes 29360128 | tf_op jit(solution)/shard_map/product/pallas_call | solution.py:161
  (21 shorter events, 0.2 us)
Async XLA Ops:
  6.5 114.9 %all-gather.3.cloned.1.call-start = ((), (), s32[]{:S(2)}) async-start(), calls=%async_computation.4 | async-start | bytes 21626880 | tf_op jit(solution)/shard_map/all_gather | solution.py:266
  8.6 13.0 %copy-start.7 = (bf16[144,640]{1,0:T(8,128)(2,1)S(1)}, bf16[144,640]{1,0:T(8,128)(2,1)}, u32[]{:S(2)}) copy-start(bf16[144,640]{1,0:T(8,128)(2,1)} %get-tuple-element.29) | copy-start | bytes 552964
  8.6 9.1 %collective-permute-start = (bf16[144,640]{1,0:T(8,128)(2,1)}, bf16[144,640]{1,0:T(8,128)(2,1)S(1)}, u32[]{:S(2)}, u32[]{:S(2)}) collective-permute-start(bf16[144,640]{1,0:T(8,128)(2,1)} %get-tuple-element.26), channel_id=1, source_target_pairs={{0,32},{32,64},{64,96},{96,0},{1,33},{33,65},{65,97},{97,1},{2,34}... | collective-permute-start | bytes 552968 | tf_op jit(solution)/shard_map/ppermute | solution.py:242
  10.7 7.0 %collective-permute-start.1 = (bf16[144,640]{1,0:T(8,128)(2,1)}, bf16[144,640]{1,0:T(8,128)(2,1)S(1)}, u32[]{:S(2)}, u32[]{:S(2)}) collective-permute-start(bf16[144,640]{1,0:T(8,128)(2,1)} %get-tuple-element.27), channel_id=1, source_target_pairs={{0,96},{32,0},{64,32},{96,64},{1,97},{33,1},{65,33},{97,65},{2,98}... | collective-permute-start | bytes 552968 | tf_op jit(solution)/shard_map/ppermute | solution.py:242
  12.2 9.3 %collective-permute-start.2 = (bf16[144,640]{1,0:T(8,128)(2,1)}, bf16[144,640]{1,0:T(8,128)(2,1)S(1)}, u32[]{:S(2)}, u32[]{:S(2)}) collective-permute-start(bf16[144,640]{1,0:T(8,128)(2,1)} %get-tuple-element.28), channel_id=1, source_target_pairs={{0,64},{32,96},{64,0},{96,32},{1,65},{33,97},{65,1},{97,33},{2,66}... | collective-permute-start | bytes 552968 | tf_op jit(solution)/shard_map/ppermute | solution.py:242
  17.7 4.9 %copy-start.6 = (bf16[32,128,128]{2,1,0:T(8,128)(2,1)S(1)}, bf16[32,128,128]{2,1,0:T(8,128)(2,1)}, u32[]{:S(2)}) copy-start(bf16[32,128,128]{2,1,0:T(8,128)(2,1)} %get-tuple-element.34) | copy-start | bytes 3145732
  17.7 4.9 %copy-start.8 = (bf16[144,640]{1,0:T(8,128)(2,1)}, bf16[144,640]{1,0:T(8,128)(2,1)S(1)}, u32[]{:S(2)}) copy-start(bf16[144,640]{1,0:T(8,128)(2,1)S(1)} %collective-permute-done.1) | copy-start | bytes 552964
  21.5 1.0 copy-start.9
  22.6 71.6 %copy-start.10 = (s32[4]{0:T(128)S(1)}, s32[4]{0:T(128)}, u32[]{:S(2)}) copy-start(s32[4]{0:T(128)} %constant.16.clone) | copy-start | bytes 52
  55.6 28.7 %all-to-all-start.1 = ((bf16[32,128,128]{2,1,0:T(8,128)(2,1)}), bf16[32,128,128]{2,1,0:T(8,128)(2,1)S(1)}, u32[]{:S(2)}, u32[]{:S(2)}) async-start(bf16[32,128,128]{2,1,0:T(8,128)(2,1)} %get-tuple-element.35), calls=%async_computation.1 | async-start | bytes 2097152 | tf_op jit(solution)/shard_map/all_to_all | solution.py:271
  60.8 33.4 %collective-permute-start.4 = (bf16[32,128,128]{2,1,0:T(8,128)(2,1)S(1)}, bf16[32,128,128]{2,1,0:T(8,128)(2,1)S(1)}, u32[]{:S(2)}, u32[]{:S(2)}) collective-permute-start(bf16[32,128,128]{2,1,0:T(8,128)(2,1)S(1)} %all_to_all.20.refs_0_), channel_id=1, source_target_pairs={{0,96},{32,0},{64,32},{96,64},{1,97},{33,1},{65,33},{97,65},{2,98}... | collective-permute-start | bytes 3145736 | tf_op jit(solution)/shard_map/ppermute | solution.py:242
  61.7 33.7 %collective-permute-start.3 = (bf16[32,128,128]{2,1,0:T(8,128)(2,1)S(1)}, bf16[32,128,128]{2,1,0:T(8,128)(2,1)}, u32[]{:S(2)}, u32[]{:S(2)}) collective-permute-start(bf16[32,128,128]{2,1,0:T(8,128)(2,1)S(1)} %all_to_all.20.refs_0_), channel_id=1, source_target_pairs={{0,32},{32,64},{64,96},{96,0},{1,33},{33,65},{65,97},{97,1},{2,34}... | collective-permute-start | bytes 3145736 | tf_op jit(solution)/shard_map/ppermute | solution.py:242
  84.2 23.6 %collective-permute-start.7 = (bf16[32,128,128]{2,1,0:T(8,128)(2,1)S(1)}, bf16[32,128,128]{2,1,0:T(8,128)(2,1)}, u32[]{:S(2)}, u32[]{:S(2)}) collective-permute-start(bf16[32,128,128]{2,1,0:T(8,128)(2,1)S(1)} %all-to-all-done.1.refs_1_), channel_id=1, source_target_pairs={{0,96},{32,0},{64,32},{96,64},{1,97},{33,1},{65,33},{97,65},{2,98}... | collective-permute-start | bytes 3145736 | tf_op jit(solution)/shard_map/ppermute | solution.py:242
  84.2 24.8 %collective-permute-start.6 = (bf16[32,128,128]{2,1,0:T(8,128)(2,1)S(1)}, bf16[32,128,128]{2,1,0:T(8,128)(2,1)}, u32[]{:S(2)}, u32[]{:S(2)}) collective-permute-start(bf16[32,128,128]{2,1,0:T(8,128)(2,1)S(1)} %all-to-all-done.1.refs_1_), channel_id=1, source_target_pairs={{0,32},{32,64},{64,96},{96,0},{1,33},{33,65},{65,97},{97,1},{2,34}... | collective-permute-start | bytes 3145736 | tf_op jit(solution)/shard_map/ppermute | solution.py:242
  85.7 1.1 copy-start
  88.7 13.5 %all-to-all-start.2 = ((s32[32,4,128]{2,1,0:T(4,128)}), s32[32,4,128]{2,1,0:T(4,128)S(1)}, u32[]{:S(2)}, u32[]{:S(2)}) async-start(s32[32,4,128]{2,1,0:T(4,128)} %broadcast_in_dim.30), calls=%async_computation.2 | async-start | bytes 131072 | tf_op jit(solution)/shard_map/all_to_all | solution.py:279
  94.3 1.1 copy-start.3
  95.4 48.3 %collective-permute-start.5 = (bf16[32,128,128]{2,1,0:T(8,128)(2,1)}, bf16[32,128,128]{2,1,0:T(8,128)(2,1)S(1)}, u32[]{:S(2)}, u32[]{:S(2)}) collective-permute-start(bf16[32,128,128]{2,1,0:T(8,128)(2,1)} %collective-permute-done.3.refs_2_), channel_id=1, source_target_pairs={{0,32},{32,64},{64,96},{96,0},{1,33},{33,65},{65,97},{97,1},{2,34}... | collective-permute-start | bytes 3145736 | tf_op jit(solution)/shard_map/ppermute | solution.py:242
  109.0 34.6 %collective-permute-start.8 = (bf16[32,128,128]{2,1,0:T(8,128)(2,1)}, bf16[32,128,128]{2,1,0:T(8,128)(2,1)S(1)}, u32[]{:S(2)}, u32[]{:S(2)}) collective-permute-start(bf16[32,128,128]{2,1,0:T(8,128)(2,1)} %collective-permute-done.7.refs_5_), channel_id=1, source_target_pairs={{0,96},{32,0},{64,32},{96,64},{1,97},{33,1},{65,33},{97,65},{2,98}... | collective-permute-start | bytes 3145736 | tf_op jit(solution)/shard_map/ppermute | solution.py:242
  121.5 1.2 copy-start.1
  122.7 1.2 copy-start.4
  143.6 22.5 %copy-start.2 = (bf16[32,128,128]{2,1,0:T(8,128)(2,1)S(1)}, bf16[32,128,128]{2,1,0:T(8,128)(2,1)}, u32[]{:S(2)}) copy-start(bf16[32,128,128]{2,1,0:T(8,128)(2,1)} %copy-done) | copy-start | bytes 3145732
  143.6 22.5 %copy-start.5 = (bf16[32,128,128]{2,1,0:T(8,128)(2,1)S(1)}, bf16[32,128,128]{2,1,0:T(8,128)(2,1)}, u32[]{:S(2)}) copy-start(bf16[32,128,128]{2,1,0:T(8,128)(2,1)} %copy-done.3) | copy-start | bytes 3145732
Sparse Core Ops, SparseCore 0:
  22.7 98.7 all-gather.2

commit v6 on v5

v6 whole, which is shorter than its diff:
```python
import functools
import math

import jax
import jax.numpy as jnp
from jax import lax
from jax.experimental import pallas as pl
from jax.experimental.pallas import tpu as pltpu
from jax.sharding import PartitionSpec as P

BLK = 128
TILE = 256
DOCS = 32
DEPTH = 8
HALVES = 2
PARTS = 4
AHEAD = 3

NT = (((1,), (1,)), ((), ()))
TN = (((0,), (0,)), ((), ()))


def flat(block):
    return block.reshape(block.shape[0] * block.shape[1], block.shape[2])


def columns_of(refs, at, count):
    return jnp.concatenate([flat(ref[pl.ds(at, count)]) for ref in refs], axis=1)


def gram_dot(left, right):
    return lax.dot_general(left, right, NT, preferred_element_type=jnp.float32)


def places():
    spot = lax.broadcasted_iota(jnp.int32, (TILE, TILE), 0)
    column = lax.broadcasted_iota(jnp.int32, (TILE, TILE), 1)
    return spot, column


def pair_products(old, own):
    spot, column = places()
    return jnp.where(spot <= column, gram_dot(own, own), gram_dot(old, own))


def counted(pairs, first):
    spot, column = places()
    weight = jnp.where(spot == column, jnp.float32(1.0), jnp.float32(2.0))
    begin = jnp.where(spot <= column, first, first + TILE)
    return jnp.where(spot >= begin, pairs * weight, jnp.float32(0.0))


def line_of(ref, at, row):
    line = slice(row, row + 1)
    return jnp.concatenate([ref[at, line], ref[at + 1, line]], axis=1)


def doc_sums(terms, ids):
    docs = lax.broadcasted_iota(jnp.int32, (DOCS, TILE), 0)
    total = jnp.sum(terms, axis=0, keepdims=True)
    parts = jnp.where(docs == ids, jnp.broadcast_to(total, docs.shape), jnp.float32(0.0))
    return parts[:, :BLK] + parts[:, BLK:]


def hidden_kernel(kinds, first_ref, *refs):
    nrows = len(kinds)
    per_row = 2 * HALVES
    out_ref = refs[per_row * nrows]
    tiles = out_ref.shape[1]
    step = pl.program_id(0)
    for k, row in enumerate(kinds):
        row_refs = refs[per_row * k : per_row * (k + 1)]
        old = columns_of(row_refs[HALVES:], 0, 2)
        for t in range(tiles):
            number = step * tiles + t
            first = line_of(first_ref, 2 * number, row) - number * TILE
            own = columns_of(row_refs[:HALVES], 2 * t, 2)
            out_ref[k, t] = counted(pair_products(old, own), first)
            old = own


def hidden_gram(first, kinds, hidden):
    pieces = [piece for row in hidden for piece in row]
    blocks = pieces[0].shape[0]
    count = blocks // PARTS
    tiles = count // 2
    nrows = len(kinds)
    own = pl.BlockSpec((count, BLK, BLK), lambda i: (i, 0, 0))
    old = pl.BlockSpec((2, BLK, BLK), lambda i: (jnp.maximum(i * tiles - 1, 0), 0, 0))
    return pl.pallas_call(
        functools.partial(hidden_kernel, kinds),
        out_shape=pltpu.HBM((nrows, blocks // 2, TILE, TILE), jnp.float32),
        grid=(PARTS,),
        in_specs=[
            pl.BlockSpec(first.shape, lambda i: (0, 0, 0)),
            *[spec for _ in kinds for spec in [own] * HALVES + [old] * HALVES],
        ],
        out_specs=pl.BlockSpec((nrows, tiles, TILE, TILE), lambda i: (0, i, 0, 0)),
        compiler_params=pltpu.CompilerParams(vmem_limit_bytes=24 * 2**20),
        cost_estimate=pl.CostEstimate(
            flops=nrows * blocks * BLK * 4 * TILE * TILE,
            bytes_accessed=nrows * blocks * BLK * TILE * 6,
            transcendentals=0,
        ),
        name="hidden_gram",
    )(first, *[piece for row in hidden for piece in [*row, *row]])


def early_kernel(kinds, rows_ref, ids_ref, pairs_hbm, g_hbm, out_ref, g_ref, pairs_ref, pair_sems, sems):
    nrows = len(kinds)
    blocks, every = g_ref.shape[:2]
    count = blocks // PARTS
    tiles = count // 2

    def copy(n):
        here = pl.ds(lax.rem(n, PARTS) * count, count)
        row = n // PARTS
        return pltpu.make_async_copy(g_hbm.at[here, row], g_ref.at[here, row], sems.at[n])

    def pair_copy(n):
        here = pl.ds(lax.rem(n, PARTS) * tiles, tiles)
        slot = lax.rem(n, AHEAD + 1)
        return pltpu.make_async_copy(pairs_hbm.at[n // PARTS, here], pairs_ref.at[slot], pair_sems.at[n])

    for n in range(AHEAD):
        copy(n).start()
        pair_copy(n).start()
    out_ref[...] = jnp.zeros_like(out_ref)
    for k, row in enumerate(kinds):

        @pl.loop(0, PARTS)
        def _(c, k=k, row=row):
            n = k * PARTS + c
            copy(n).wait()
            pair_copy(n).wait()

            @pl.when(n + AHEAD < every * PARTS)
            def _():
                copy(n + AHEAD).start()

            @pl.when(n + AHEAD < nrows * PARTS)
            def _():
                pair_copy(n + AHEAD).start()

            slot = lax.rem(n, AHEAD + 1)
            share = jnp.zeros((DOCS, BLK), jnp.float32)
            old = flat(g_ref[pl.ds(jnp.maximum(c * count - 2, 0), 2), row])
            for t in range(tiles):
                at = c * count + 2 * t
                own = flat(g_ref[pl.ds(at, 2), row])
                terms = pairs_ref[slot, t] * pair_products(old, own)
                share += doc_sums(terms, line_of(ids_ref, at, row))
                old = own
            here = pl.ds(pl.multiple_of(rows_ref[row] * DOCS, DOCS), DOCS)
            out_ref[here, :] += share

    for n in range(nrows * PARTS, every * PARTS):
        copy(n).wait()
        if n + AHEAD < every * PARTS:
            copy(n + AHEAD).start()


def late_kernel(row, rows_ref, ids_ref, first_ref, *refs):
    h_refs = refs[:HALVES]
    g_ref, init_ref, out_ref, acc = refs[HALVES:]
    count = g_ref.shape[0] // PARTS
    acc[...] = init_ref[...]

    @pl.loop(0, PARTS)
    def _(c):
        share = jnp.zeros((DOCS, BLK), jnp.float32)
        before = jnp.maximum(c * count - 2, 0)
        old_h = columns_of(h_refs, before, 2)
        old_g = flat(g_ref[pl.ds(before, 2), row])
        for t in range(count // 2):
            at = c * count + 2 * t
            first = line_of(first_ref, at, row) - at * BLK
            own_h = columns_of(h_refs, at, 2)
            own_g = flat(g_ref[pl.ds(at, 2), row])
            terms = counted(pair_products(old_h, own_h) * pair_products(old_g, own_g), first)
            share += doc_sums(terms, line_of(ids_ref, at, row))
            old_h, old_g = own_h, own_g
        here = pl.ds(pl.multiple_of(rows_ref[row] * DOCS, DOCS), DOCS)
        acc[here, :] += share

    sums = jnp.sum(acc[...].T, axis=0, keepdims=True)
    out_ref[...] = jnp.broadcast_to(sums[None], out_ref.shape)


def in_vmem(count):
    return [pl.BlockSpec(memory_space=pltpu.VMEM)] * count


def in_hbm(count):
    return [pl.BlockSpec(memory_space=pltpu.HBM)] * count


def keep_in(space, array):
    return pltpu.with_memory_space_constraint(array, space)


def gram_cost(nrows, grad):
    blocks, _, _, width = grad.shape
    return pl.CostEstimate(
        flops=nrows * blocks * BLK * 4 * TILE * (TILE + width),
        bytes_accessed=grad.size * 2,
        transcendentals=0,
    )


def gram_early(rows, ids, kinds, pairs, grad):
    every = grad.shape[1]
    tiles = pairs.shape[1] // PARTS
    return pl.pallas_call(
        functools.partial(early_kernel, kinds),
        out_shape=[
            jax.ShapeDtypeStruct((every * DOCS, BLK), jnp.float32),
            pltpu.VMEM(grad.shape, grad.dtype),
        ],
        grid_spec=pltpu.PrefetchScalarGridSpec(
            num_scalar_prefetch=1,
            grid=(),
            in_specs=[*in_vmem(1), *in_hbm(2)],
            out_specs=in_vmem(2),
            scratch_shapes=[
                pltpu.VMEM((AHEAD + 1, tiles, TILE, TILE), jnp.float32),
                pltpu.SemaphoreType.DMA((len(kinds) * PARTS,)),
                pltpu.SemaphoreType.DMA((every * PARTS,)),
            ],
        ),
        compiler_params=pltpu.CompilerParams(vmem_limit_bytes=8 * 2**20),
        cost_estimate=gram_cost(len(kinds), grad),
        name="gram",
    )(rows, ids, keep_in(pltpu.HBM, pairs), keep_in(pltpu.HBM, grad))


def gram_late(rows, ids, first, row, hidden, grad, init, devices):
    return pl.pallas_call(
        functools.partial(late_kernel, row),
        out_shape=jax.ShapeDtypeStruct((devices, 1, BLK), jnp.float32),
        grid_spec=pltpu.PrefetchScalarGridSpec(
            num_scalar_prefetch=1,
            grid=(),
            in_specs=in_vmem(2 + len(hidden) + 2),
            out_specs=pl.BlockSpec(memory_space=pltpu.VMEM),
            scratch_shapes=[pltpu.VMEM(init.shape, jnp.float32)],
        ),
        compiler_params=pltpu.CompilerParams(vmem_limit_bytes=4 * 2**20),
        cost_estimate=gram_cost(1, grad),
        name="gram_late",
    )(rows, ids, first, *hidden, keep_in(pltpu.VMEM, grad), init)


def product_kernel(nrows, bound, rows_ref, ids_ref, norms_ref, *refs):
    pieces = refs[: HALVES * nrows]
    g_ref, out_ref, h_ref, h_sems, factor, scaled = refs[HALVES * nrows :]
    blocks = g_ref.shape[0]
    steps = blocks // DEPTH

    def hidden_copies(k):
        return [
            pltpu.make_async_copy(pieces[n], h_ref.at[n], h_sems.at[n])
            for n in range(HALVES * k, HALVES * (k + 1))
        ]

    for piece in hidden_copies(0):
        piece.start()
    norms = jnp.sum(norms_ref[...], axis=0)
    clip = bound / jnp.maximum(jnp.sqrt(norms), bound) / nrows
    for k in range(nrows):
        ids = ids_ref[:, k, :] + rows_ref[k] * DOCS
        table = jnp.broadcast_to(clip, ids.shape)
        factor[k] = jnp.take_along_axis(table, ids, axis=1)

    def scale(n, slot):
        k, begin = n // steps, n % steps * DEPTH
        lines = jnp.concatenate([factor[k, begin : begin + DEPTH, :]] * (BLK // DEPTH), axis=0).T
        for j in range(DEPTH):
            factors = jnp.broadcast_to(lines[:, j : j + 1], (BLK, BLK))
            for c in range(0, g_ref.shape[3], BLK):
                grad = g_ref[begin + j, k, :, c : c + BLK].astype(jnp.float32)
                scaled[slot, j * BLK : (j + 1) * BLK, c : c + BLK] = (grad * factors).astype(jnp.bfloat16)

    scale(0, 0)
    for n in range(nrows * steps):
        k, begin = n // steps, n % steps * DEPTH
        if begin == 0:
            for piece in hidden_copies(k):
                piece.wait()
            if k + 1 < nrows:
                for piece in hidden_copies(k + 1):
                    piece.start()
        if n + 1 < nrows * steps:
            scale(n + 1, (n + 1) % 2)
        share = lax.dot_general(
            columns_of([h_ref.at[HALVES * k + q] for q in range(HALVES)], begin, DEPTH),
            scaled[n % 2],
            TN,
            preferred_element_type=jnp.float32,
        )
        if n == 0:
            out_ref[...] = share
        else:
            out_ref[...] += share


def product(rows, ids, norms, hidden, grad, bound):
    blocks, nrows, _, width = grad.shape
    pieces = [piece for row in hidden for piece in row]
    return pl.pallas_call(
        functools.partial(product_kernel, nrows, bound),
        out_shape=jax.ShapeDtypeStruct((TILE, width), jnp.float32),
        grid_spec=pltpu.PrefetchScalarGridSpec(
            num_scalar_prefetch=1,
            grid=(),
            in_specs=[*in_vmem(2), *in_hbm(len(pieces)), *in_vmem(1)],
            out_specs=pl.BlockSpec(memory_space=pltpu.VMEM),
            scratch_shapes=[
                pltpu.VMEM((len(pieces), *pieces[0].shape), grad.dtype),
                pltpu.SemaphoreType.DMA((len(pieces),)),
                pltpu.VMEM((nrows, blocks, BLK), jnp.float32),
                pltpu.VMEM((2, DEPTH * BLK, width), jnp.bfloat16),
            ],
        ),
        compiler_params=pltpu.CompilerParams(vmem_limit_bytes=14 * 2**20),
        cost_estimate=pl.CostEstimate(
            flops=2 * nrows * blocks * BLK * TILE * width,
            bytes_accessed=nrows * blocks * BLK * 2 * (TILE + width),
            transcendentals=0,
        ),
        name="product",
    )(rows, ids, norms, *pieces, keep_in(pltpu.VMEM, grad))


def quarters_kernel(me_ref, ids_ref, *refs):
    ins, outs = refs[: len(refs) // 2], refs[len(refs) // 2 :]
    tokens = ins[0].shape[0]
    for in_ref, out_ref in zip(ins, outs):
        out_ref[:tokens, :] = in_ref[...]
        ids = ids_ref[...].astype(jnp.float32).astype(jnp.bfloat16)
        out_ref[tokens:, :BLK] = jnp.broadcast_to(ids, (16, BLK))
        out_ref[tokens:, BLK:] = jnp.zeros((16, out_ref.shape[1] - BLK), jnp.bfloat16)


def quarters(me, offsets, grad, ids):
    tokens, width = grad.shape
    count = len(offsets)
    part = width // count
    return pl.pallas_call(
        quarters_kernel,
        out_shape=[jax.ShapeDtypeStruct((tokens + 16, part), grad.dtype)] * count,
        grid_spec=pltpu.PrefetchScalarGridSpec(
            num_scalar_prefetch=1,
            grid=(1,),
            in_specs=[pl.BlockSpec(ids.shape, lambda i, m: (0, 0))]
            + [
                pl.BlockSpec((tokens, part), lambda i, m, o=o: (0, lax.rem(m[0] + o, count)))
                for o in offsets
            ],
            out_specs=[pl.BlockSpec((tokens + 16, part), lambda i, m: (0, 0))] * count,
        ),
        name="quarters",
    )(me, ids, *[grad] * count)


def columns_kernel(in_ref, *out_refs):
    for j in range(out_refs[0].shape[0]):
        for q, out_ref in enumerate(out_refs):
            at = (j * HALVES + q) * BLK
            out_ref[j] = in_ref[:, at : at + BLK]


def columns(hidden, blocks, steps=4):
    tokens, width = hidden.shape
    count = blocks // steps
    return pl.pallas_call(
        columns_kernel,
        out_shape=[jax.ShapeDtypeStruct((blocks, tokens, BLK), hidden.dtype)] * HALVES,
        grid=(steps,),
        in_specs=[pl.BlockSpec((tokens, width // steps), lambda i: (0, i))],
        out_specs=[pl.BlockSpec((count, tokens, BLK), lambda i: (i, 0, 0))] * HALVES,
        name="columns",
    )(hidden)


def shift(block, distance):
    size = lax.axis_size("dp")
    return lax.ppermute(block, "dp", [(i, (i + distance) % size) for i in range(size)])


def starts(ids):
    docs = jnp.arange(DOCS, dtype=jnp.int32)
    before = jnp.sum((ids[None] < docs[:, None, None, None]).astype(jnp.int32), axis=(1, 3))
    own = ids[None] == docs[:, None, None, None]
    return jnp.sum(jnp.where(own, before[:, None, :, None], 0), axis=0)


def body(hidden, grad_out, segment):
    row_count = lax.axis_size("dp")
    blocks = lax.axis_size("ctx")
    tokens, width_hidden = hidden.shape[1:]
    width_grad = grad_out.shape[2]
    me = lax.axis_index("dp")

    keep, up, down, across = quarters(me[None], (0, 1, 3, 2), grad_out[0], segment)
    across = shift(across, 2)
    received = [keep, shift(up, 1), shift(down, -1), across]

    chunks = columns(hidden[0], blocks)
    chunks, received = lax.optimization_barrier((chunks, received))

    every_grad = jnp.stack([part[:tokens] for part in received])
    every_grad = lax.all_gather(every_grad, "ctx", axis=0, tiled=False)

    hidden_rows = [[], [], [], []]
    ready = None
    for q, chunk in enumerate(chunks):
        if ready is not None:
            chunk, ready = lax.optimization_barrier((chunk, ready))
        own = lax.all_to_all(chunk, "ctx", 0, 0, tiled=True)
        ready = own
        below, above = lax.optimization_barrier((shift(own, 1), shift(own, -1)))
        far = shift(below, 1) if q < HALVES // 2 else shift(above, -1)
        for row, piece in zip(hidden_rows, (own, below, above, far)):
            row.append(piece)

    ids = jnp.stack([part[tokens, :BLK] for part in received]).astype(jnp.int32)
    ids, ready = lax.optimization_barrier((ids, ready))
    ids = jnp.broadcast_to(ids[None], (blocks, row_count, tokens))
    ids = lax.all_to_all(ids, "ctx", 0, 0, tiled=True)
    first = starts(ids)

    rows = lax.rem(me + jnp.array([0, 3, 1, 2], jnp.int32), row_count)
    kinds = (0, 1, 2)
    pairs = hidden_gram(first, kinds, hidden_rows[:3])
    early, grads = gram_early(rows, ids, kinds, pairs, every_grad)
    devices = row_count * blocks
    partial = gram_late(rows, ids, first, 3, hidden_rows[3], grads, early, devices)
    norms = lax.all_to_all(partial, ("dp", "ctx"), 0, 0, tiled=True)

    bound = math.sqrt(tokens * width_hidden * width_grad)
    return product(rows, ids, norms, hidden_rows, grads, bound)


def solution(mesh):
    in_specs = (P("dp", "ctx", None), P("dp", "ctx", None), P("dp", "ctx"))
    out_specs = P("ctx", "dp")
    return jax.shard_map(body, mesh=mesh, in_specs=in_specs, out_specs=out_specs, check_vma=False)
```

time: 190 us -> 180 us (0.947)
  waiting for transfers between devices: 48.6 us -> 38.3 us
  local copies, waits for them, and re-layouts: 6.66 us -> 0.8 us
  starting transfers between devices: 19.5 us -> 24 us
  blocking collectives: 47.5 us -> 49.7 us
    all_gather x1, waiting for transfers between devices: 12.2 us -> 0.86 us  [body(): every_grad = lax.all_gather(every_grad, 'ctx', axis=0, tiled=False)]
    pallas_call x1, Pallas kernels: 16.5 us -> 10.5 us  [product(): pl.pallas_call(functools.partial(product_kernel, nrows, bound), out_shape...]
    pallas_call x2 -> x3, Pallas kernels: 27.6 us -> 33 us  [the longest x1 16.2 us: gram_early(): pl.pallas_call(functools.partial(early_kernel, kinds), out_shape=[jax.Sha...]
    unnamed x22 -> x10, local copies, waits for them, and re-layouts: 4.61 us -> 0.02 us
    ppermute x9, starting transfers between devices: 8.7 us -> 13.1 us  [shift(): lax.ppermute(block, 'dp', [(i, (i + distance) % size) for i in range(size)])]
    all_to_all x1, blocking collectives: 14.5 us -> 16.8 us  [body(): norms = lax.all_to_all(partial, ('dp', 'ctx'), 0, 0, tiled=True)]
  transfers between devices with their start and end apart: 12 -> 12, of which waited for: 6 -> 5; matrix products, arithmetic and copies ran while one was open for 2% -> 2% of each run, Pallas kernels for 12% -> 16%
where the time goes in v6:
time: 180 us; the launch traced here: 179 us
  blocking collectives  49.7 us (28%)
  Pallas kernels  49.5 us (28%)
  waiting for transfers between devices  38.3 us (21%)
  starting transfers between devices  24 us (13%)
  between operations  13.6 us (8%)
  other arithmetic  3.63 us (2%)
    all_to_all x1, blocking collectives, body(): own = lax.all_to_all(chunk, 'ctx', 0, 0, tiled=True)  32.9 us
    all_to_all x1, waiting for transfers between devices, body(): own = lax.all_to_all(chunk, 'ctx', 0, 0, tiled=True)  20.6 us
    all_to_all x1, blocking collectives, body(): norms = lax.all_to_all(partial, ('dp', 'ctx'), 0, 0, tiled=True)  16.8 us
    pallas_call x1, Pallas kernels, gram_early(): pl.pallas_call(functools.partial(early_kernel, kinds), out_shape=[jax.Sha...  16.2 us
    ppermute x9, starting transfers between devices, shift(): lax.ppermute(block, 'dp', [(i, (i + distance) % size) for i in range(size)])  13.1 us
    pallas_call x1, Pallas kernels, product(): pl.pallas_call(functools.partial(product_kernel, nrows, bound), out_shape...  10.5 us
    pallas_call x1, Pallas kernels, hidden_gram(): pl.pallas_call(functools.partial(hidden_kernel, kinds), out_shape=pltpu.H...  9.23 us
    ppermute x9, waiting for transfers between devices, shift(): lax.ppermute(block, 'dp', [(i, (i + distance) % size) for i in range(size)])  9.04 us
  transfers between devices with their start and end apart: 12, of which 5 were waited for; matrix products, arithmetic and copies ran while one was open for 2% of the time, Pallas kernels for 16%

profile of v6, /device:TPU:1, one launch (start us, length us, event | category | flops | bytes accessed | tf_op | source)
XLA Modules:
  0.0 179.4 jit_solution(9308262704886817724)
XLA Ops:
  6.5 0.0 all-gather.3.cloned.1.call-start
  6.5 2.0 %quarters.1 = (bf16[144,640]{1,0:T(8,128)(2,1)}, bf16[144,640]{1,0:T(8,128)(2,1)}, bf16[144,640]{1,0:T(8,128)(2,1)}, bf16[144,640]{1,0:T(8,128)(2,1)}) custom-call(s32[1]{0:T(128)} %bitcast.1.me_ref, s32[1,128]{1,0:T(1,128)} %ids_ref.1, bf16[128,2560]{1,0:T(8,128)(2,1)} %bitcast.12, bf16[128,2560]{1,0:T(8,128)(2,1)} %bitcast.13, bf16[128,2560]{1,0:T(8,128)(2,1)} %bitcast.14, ...), custom_call_target="tpu_custom_call" | custom-call | tf_op jit(solution)/shard_map/quarters/pallas_call | solution.py:349
  8.6 0.0 copy-start.3
  8.6 2.1 %collective-permute-start = (bf16[144,640]{1,0:T(8,128)(2,1)}, bf16[144,640]{1,0:T(8,128)(2,1)S(1)}, u32[]{:S(2)}, u32[]{:S(2)}) collective-permute-start(bf16[144,640]{1,0:T(8,128)(2,1)} %get-tuple-element.28), channel_id=1, source_target_pairs={{0,32},{32,64},{64,96},{96,0},{1,33},{33,65},{65,97},{97,1},{2,34}... | collective-permute-start | bytes 552968 | tf_op jit(solution)/shard_map/ppermute | solution.py:388
  10.7 1.5 collective-permute-start.1
  12.2 1.6 collective-permute-start.2
  13.8 3.9 %columns.1 = (bf16[32,128,128]{2,1,0:T(8,128)(2,1)}, bf16[32,128,128]{2,1,0:T(8,128)(2,1)}) custom-call(bf16[128,8192]{1,0:T(8,128)(2,1)} %bitcast.16), custom_call_target="tpu_custom_call" | custom-call | tf_op jit(solution)/shard_map/columns/pallas_call | solution.py:376
  17.7 0.0 copy-start.2
  17.7 0.0 collective-permute-done
  17.7 0.0 collective-permute-done.1
  17.7 3.8 %collective-permute-done.2 = bf16[144,640]{1,0:T(8,128)(2,1)S(1)} collective-permute-done((bf16[144,640]{1,0:T(8,128)(2,1)}, bf16[144,640]{1,0:T(8,128)(2,1)S(1)}, u32[]{:S(2)}, u32[]{:S(2)}) %collective-permute-start.2) | collective-permute-done | bytes 184352 | tf_op jit(solution)/shard_map/ppermute | solution.py:388
  21.6 0.0 copy-done.3
  21.6 0.9 pad_maximum_fusion
  22.6 0.0 all-gather.3.cloned.1.call-update
  22.6 0.0 copy-done.2
  22.6 0.0 copy-start.4
  22.6 32.9 %all_to_all.20.refs_0_.refs_2_ = bf16[32,128,128]{2,1,0:T(8,128)(2,1)S(1)} all-to-all(bf16[32,128,128]{2,1,0:T(8,128)(2,1)S(1)} %copy-done.2), channel_id=1, replica_groups=mesh['dp'=4,'ctx'=32] {'ctx'}, dimensions={0} | all-to-all | bytes 2097152 | tf_op jit(solution)/shard_map/all_to_all | solution.py:420
  55.6 5.3 %all-to-all-start.1 = ((bf16[32,128,128]{2,1,0:T(8,128)(2,1)}), bf16[32,128,128]{2,1,0:T(8,128)(2,1)S(1)}, u32[]{:S(2)}, u32[]{:S(2)}) async-start(bf16[32,128,128]{2,1,0:T(8,128)(2,1)} %get-tuple-element.37), calls=%async_computation.1 | async-start | bytes 2097152 | tf_op jit(solution)/shard_map/all_to_all | solution.py:420
  60.9 0.8 collective-permute-start.3
  61.6 2.0 %collective-permute-start.4 = (bf16[32,128,128]{2,1,0:T(8,128)(2,1)S(1)}, bf16[32,128,128]{2,1,0:T(8,128)(2,1)}, u32[]{:S(2)}, u32[]{:S(2)}) collective-permute-start(bf16[32,128,128]{2,1,0:T(8,128)(2,1)S(1)} %all_to_all.20.refs_0_.refs_2_), channel_id=1, source_target_pairs={{0,96},{32,0},{64,32},{96,64},{1,97},{33,1},{65,33},{97,65},{2,98}... | collective-permute-start | bytes 3145736 | tf_op jit(solution)/shard_map/ppermute | solution.py:388
  63.6 20.6 %all-to-all-done.1.refs_1_.refs_3_ = bf16[32,128,128]{2,1,0:T(8,128)(2,1)S(1)} async-done(((bf16[32,128,128]{2,1,0:T(8,128)(2,1)}), bf16[32,128,128]{2,1,0:T(8,128)(2,1)S(1)}, u32[]{:S(2)}, u32[]{:S(2)}) %all-to-all-start.1) | async-done | bytes 1048608 | tf_op jit(solution)/shard_map/all_to_all | solution.py:420
  84.2 0.0 copy-start
  84.2 0.2 collective-permute-start.6
  84.4 2.5 %collective-permute-start.7 = (bf16[32,128,128]{2,1,0:T(8,128)(2,1)S(1)}, bf16[32,128,128]{2,1,0:T(8,128)(2,1)}, u32[]{:S(2)}, u32[]{:S(2)}) collective-permute-start(bf16[32,128,128]{2,1,0:T(8,128)(2,1)S(1)} %all-to-all-done.1.refs_1_.refs_3_), channel_id=1, source_target_pairs={{0,96},{32,0},{64,32},{96,64},{1,97},{33,1},{65,33},{97,65},{2,98}... | collective-permute-start | bytes 3145736 | tf_op jit(solution)/shard_map/ppermute | solution.py:388
  86.9 0.6 broadcast_in_dim.13
  87.6 5.6 %all-to-all-start.2 = ((s32[32,4,128]{2,1,0:T(4,128)}), s32[32,4,128]{2,1,0:T(4,128)S(1)}, u32[]{:S(2)}, u32[]{:S(2)}) async-start(s32[32,4,128]{2,1,0:T(4,128)} %broadcast_in_dim.13), calls=%async_computation.2 | async-start | bytes 131072 | tf_op jit(solution)/shard_map/all_to_all | solution.py:430
  93.2 0.0 copy-done.4
  93.2 0.0 collective-permute-done.3.refs_4_.refs_6_.refs_2_
  93.2 0.0 collective-permute-done.4.refs_8_.refs_10_.refs_4_
  93.2 0.1 collective-permute-start.5
  93.3 7.7 %all-to-all-done.2.ids_ref = s32[32,4,128]{2,1,0:T(4,128)S(1)} async-done(((s32[32,4,128]{2,1,0:T(4,128)}), s32[32,4,128]{2,1,0:T(4,128)S(1)}, u32[]{:S(2)}, u32[]{:S(2)}) %all-to-all-start.2) | async-done | bytes 65568 | tf_op jit(solution)/shard_map/all_to_all | solution.py:430
  101.0 2.4 %convert_reduce_fusion = s32[32,4]{1,0:T(8,128)S(1)} fusion(s32[32,4,128]{2,0,1:T(8,128)S(1)} %copy.5), kind=kLoop, calls=%fused_computation.1 | loop fusion | flops 1572736 | bytes 66048 | tf_op jit(solution)/shard_map/reduce_sum | solution.py:393
  103.4 0.3 select_reduce_fusion
  103.8 5.2 %collective-permute-done.6.refs_5_.refs_7_.refs_3_ = bf16[32,128,128]{2,1,0:T(8,128)(2,1)} collective-permute-done((bf16[32,128,128]{2,1,0:T(8,128)(2,1)S(1)}, bf16[32,128,128]{2,1,0:T(8,128)(2,1)}, u32[]{:S(2)}, u32[]{:S(2)}) %collective-permute-start.6) | collective-permute-done | bytes 1048608 | tf_op jit(solution)/shard_map/ppermute | solution.py:388
  109.0 0.0 collective-permute-done.7.refs_9_.refs_11_.refs_5_
  109.0 2.4 %collective-permute-start.8 = (bf16[32,128,128]{2,1,0:T(8,128)(2,1)}, bf16[32,128,128]{2,1,0:T(8,128)(2,1)}, u32[]{:S(2)}, u32[]{:S(2)}) collective-permute-start(bf16[32,128,128]{2,1,0:T(8,128)(2,1)} %collective-permute-done.7.refs_9_.refs_11_.refs_5_), channel_id=1, source_target_pairs={{0,96},{32,0},{64,32},{96,64},{1,97},{33,1},{65,33},{97,65},{2,98}... | collective-permute-start | bytes 3145736 | tf_op jit(solution)/shard_map/ppermute | solution.py:388
  111.4 9.2 %hidden_gram.1.pairs_hbm = f32[3,16,256,256]{3,2,1,0:T(8,128)} custom-call(s32[32,4,128]{2,1,0:T(4,128)S(1)} %copy.7.first_ref, bf16[32,128,128]{2,1,0:T(8,128)(2,1)S(1)} %all_to_all.20.refs_0_.refs_2_, bf16[32,128,128]{2,1,0:T(8,128)(2,1)S(1)} %all-to-all-done.1.refs_1_.refs_3_, bf16[32,128,128]{2,1,0:T(8,128)(2,1)S(1)} %all_to_all.20.refs_0_.refs_2_, ...), custom_call_target="tpu_custom_call" | custom-call | flops 3221225472 | bytes 18874368 | tf_op jit(solution)/shard_map/hidden_gram/pallas_call | solution.py:90
  120.6 0.0 copy-done
  120.6 0.9 all-gather.3.cloned.1.call-done
  121.5 16.2 %gram.1 = (f32[128,128]{1,0:T(8,128)S(1)}, bf16[32,4,128,640]{3,2,1,0:T(8,128)(2,1)S(1)}) custom-call(s32[4]{0:T(128)S(1)} %compare_select_fusion.rows_ref, s32[32,4,128]{2,1,0:T(4,128)S(1)} %all-to-all-done.2.ids_ref, f32[3,16,256,256]{3,2,1,0:T(8,128)} %hidden_gram.1.pairs_hbm, bf16[32,4,128,640]{3,2,1,0:T(8,128)(2,1)} %bitcast.17), custom_call_target="tpu_custom_call" | custom-call | flops 11274289152 | bytes 20971520 | tf_op jit(solution)/shard_map/gram/pallas_call | solution.py:214
  137.7 0.0 collective-permute-done.5.refs_0_.refs_6_
  137.7 0.0 collective-permute-done.8.refs_1_.refs_7_
  137.7 0.0 copy-start.1
  137.8 7.5 %gram_late.1 = f32[128,1,128]{2,1,0:T(1,128)S(1)} custom-call(s32[4]{0:T(128)S(1)} %compare_select_fusion.rows_ref, s32[32,4,128]{2,1,0:T(4,128)S(1)} %all-to-all-done.2.ids_ref, s32[32,4,128]{2,1,0:T(4,128)S(1)} %copy.7.first_ref, bf16[32,128,128]{2,1,0:T(8,128)(2,1)} %collective-permute-done.5.refs_0_.refs_6_, ...), custom_call_target="tpu_custom_call" | custom-call | flops 3758096384 | bytes 20971520 | tf_op jit(solution)/shard_map/gram_late/pallas_call | solution.py:238
  145.3 16.8 %all_to_all.21.norms_ref = f32[128,1,128]{2,1,0:T(1,128)S(1)} all-to-all(f32[128,1,128]{2,1,0:T(1,128)S(1)} %gram_late.1), channel_id=1, replica_groups=mesh['dp'=4,'ctx'=32] {'dp','ctx'}, dimensions={0} | all-to-all | bytes 131072 | tf_op jit(solution)/shard_map/all_to_all | solution.py:439
  162.1 0.0 copy-done.1
  162.1 10.5 %product.1 = f32[256,640]{1,0:T(8,128)} custom-call(s32[4]{0:T(128)S(1)} %compare_select_fusion.rows_ref, s32[32,4,128]{2,1,0:T(4,128)S(1)} %all-to-all-done.2.ids_ref, f32[128,1,128]{2,1,0:T(1,128)S(1)} %all_to_all.21.norms_ref, bf16[32,128,128]{2,1,0:T(8,128)(2,1)S(1)} %all_to_all.20.refs_0_.refs_2_, bf16[32,128,128]{2,1,0:T(8,128)(2,1)S(1)} %copy-done.1, ...), custom_call_target="tpu_custom_call" | custom-call | flops 5368709120 | bytes 29360128 | tf_op jit(solution)/shard_map/product/pallas_call | solution.py:310
  (10 shorter events, 0.2 us)
Async XLA Ops:
  6.5 115.0 %all-gather.3.cloned.1.call-start = ((), (), s32[]{:S(2)}) async-start(), calls=%async_computation.4 | async-start | bytes 21626880 | tf_op jit(solution)/shard_map/all_gather | solution.py:413
  8.6 13.0 %copy-start.3 = (bf16[144,640]{1,0:T(8,128)(2,1)S(1)}, bf16[144,640]{1,0:T(8,128)(2,1)}, u32[]{:S(2)}) copy-start(bf16[144,640]{1,0:T(8,128)(2,1)} %get-tuple-element.31) | copy-start | bytes 552964
  8.6 9.1 %collective-permute-start = (bf16[144,640]{1,0:T(8,128)(2,1)}, bf16[144,640]{1,0:T(8,128)(2,1)S(1)}, u32[]{:S(2)}, u32[]{:S(2)}) collective-permute-start(bf16[144,640]{1,0:T(8,128)(2,1)} %get-tuple-element.28), channel_id=1, source_target_pairs={{0,32},{32,64},{64,96},{96,0},{1,33},{33,65},{65,97},{97,1},{2,34}... | collective-permute-start | bytes 552968 | tf_op jit(solution)/shard_map/ppermute | solution.py:388
  10.7 7.0 %collective-permute-start.1 = (bf16[144,640]{1,0:T(8,128)(2,1)}, bf16[144,640]{1,0:T(8,128)(2,1)S(1)}, u32[]{:S(2)}, u32[]{:S(2)}) collective-permute-start(bf16[144,640]{1,0:T(8,128)(2,1)} %get-tuple-element.29), channel_id=1, source_target_pairs={{0,96},{32,0},{64,32},{96,64},{1,97},{33,1},{65,33},{97,65},{2,98}... | collective-permute-start | bytes 552968 | tf_op jit(solution)/shard_map/ppermute | solution.py:388
  12.2 9.3 %collective-permute-start.2 = (bf16[144,640]{1,0:T(8,128)(2,1)}, bf16[144,640]{1,0:T(8,128)(2,1)S(1)}, u32[]{:S(2)}, u32[]{:S(2)}) collective-permute-start(bf16[144,640]{1,0:T(8,128)(2,1)} %get-tuple-element.30), channel_id=1, source_target_pairs={{0,64},{32,96},{64,0},{96,32},{1,65},{33,97},{65,1},{97,33},{2,66}... | collective-permute-start | bytes 552968 | tf_op jit(solution)/shard_map/ppermute | solution.py:388
  17.7 4.9 %copy-start.2 = (bf16[32,128,128]{2,1,0:T(8,128)(2,1)S(1)}, bf16[32,128,128]{2,1,0:T(8,128)(2,1)}, u32[]{:S(2)}) copy-start(bf16[32,128,128]{2,1,0:T(8,128)(2,1)} %get-tuple-element.36) | copy-start | bytes 3145732
  22.6 70.5 %copy-start.4 = (s32[4]{0:T(128)S(1)}, s32[4]{0:T(128)}, u32[]{:S(2)}) copy-start(s32[4]{0:T(128)} %constant.14.clone) | copy-start | bytes 52
  55.6 28.7 %all-to-all-start.1 = ((bf16[32,128,128]{2,1,0:T(8,128)(2,1)}), bf16[32,128,128]{2,1,0:T(8,128)(2,1)S(1)}, u32[]{:S(2)}, u32[]{:S(2)}) async-start(bf16[32,128,128]{2,1,0:T(8,128)(2,1)} %get-tuple-element.37), calls=%async_computation.1 | async-start | bytes 2097152 | tf_op jit(solution)/shard_map/all_to_all | solution.py:420
  60.9 32.3 %collective-permute-start.3 = (bf16[32,128,128]{2,1,0:T(8,128)(2,1)S(1)}, bf16[32,128,128]{2,1,0:T(8,128)(2,1)}, u32[]{:S(2)}, u32[]{:S(2)}) collective-permute-start(bf16[32,128,128]{2,1,0:T(8,128)(2,1)S(1)} %all_to_all.20.refs_0_.refs_2_), channel_id=1, source_target_pairs={{0,32},{32,64},{64,96},{96,0},{1,33},{33,65},{65,97},{97,1},{2,34}... | collective-permute-start | bytes 3145736 | tf_op jit(solution)/shard_map/ppermute | solution.py:388
  61.6 31.6 %collective-permute-start.4 = (bf16[32,128,128]{2,1,0:T(8,128)(2,1)S(1)}, bf16[32,128,128]{2,1,0:T(8,128)(2,1)}, u32[]{:S(2)}, u32[]{:S(2)}) collective-permute-start(bf16[32,128,128]{2,1,0:T(8,128)(2,1)S(1)} %all_to_all.20.refs_0_.refs_2_), channel_id=1, source_target_pairs={{0,96},{32,0},{64,32},{96,64},{1,97},{33,1},{65,33},{97,65},{2,98}... | collective-permute-start | bytes 3145736 | tf_op jit(solution)/shard_map/ppermute | solution.py:388
  84.2 36.4 %copy-start = (bf16[32,128,128]{2,1,0:T(8,128)(2,1)}, bf16[32,128,128]{2,1,0:T(8,128)(2,1)S(1)}, u32[]{:S(2)}) copy-start(bf16[32,128,128]{2,1,0:T(8,128)(2,1)S(1)} %all-to-all-done.1.refs_1_.refs_3_) | copy-start | bytes 3145732
  84.2 24.8 %collective-permute-start.6 = (bf16[32,128,128]{2,1,0:T(8,128)(2,1)S(1)}, bf16[32,128,128]{2,1,0:T(8,128)(2,1)}, u32[]{:S(2)}, u32[]{:S(2)}) collective-permute-start(bf16[32,128,128]{2,1,0:T(8,128)(2,1)S(1)} %all-to-all-done.1.refs_1_.refs_3_), channel_id=1, source_target_pairs={{0,32},{32,64},{64,96},{96,0},{1,33},{33,65},{65,97},{97,1},{2,34}... | collective-permute-start | bytes 3145736 | tf_op jit(solution)/shard_map/ppermute | solution.py:388
  84.4 24.6 %collective-permute-start.7 = (bf16[32,128,128]{2,1,0:T(8,128)(2,1)S(1)}, bf16[32,128,128]{2,1,0:T(8,128)(2,1)}, u32[]{:S(2)}, u32[]{:S(2)}) collective-permute-start(bf16[32,128,128]{2,1,0:T(8,128)(2,1)S(1)} %all-to-all-done.1.refs_1_.refs_3_), channel_id=1, source_target_pairs={{0,96},{32,0},{64,32},{96,64},{1,97},{33,1},{65,33},{97,65},{2,98}... | collective-permute-start | bytes 3145736 | tf_op jit(solution)/shard_map/ppermute | solution.py:388
  87.6 13.5 %all-to-all-start.2 = ((s32[32,4,128]{2,1,0:T(4,128)}), s32[32,4,128]{2,1,0:T(4,128)S(1)}, u32[]{:S(2)}, u32[]{:S(2)}) async-start(s32[32,4,128]{2,1,0:T(4,128)} %broadcast_in_dim.13), calls=%async_computation.2 | async-start | bytes 131072 | tf_op jit(solution)/shard_map/all_to_all | solution.py:430
  93.2 44.5 %collective-permute-start.5 = (bf16[32,128,128]{2,1,0:T(8,128)(2,1)}, bf16[32,128,128]{2,1,0:T(8,128)(2,1)}, u32[]{:S(2)}, u32[]{:S(2)}) collective-permute-start(bf16[32,128,128]{2,1,0:T(8,128)(2,1)} %collective-permute-done.3.refs_4_.refs_6_.refs_2_), channel_id=1, source_target_pairs={{0,32},{32,64},{64,96},{96,0},{1,33},{33,65},{65,97},{97,1},{2,34}... | collective-permute-start | bytes 3145736 | tf_op jit(solution)/shard_map/ppermute | solution.py:388
  109.0 28.7 %collective-permute-start.8 = (bf16[32,128,128]{2,1,0:T(8,128)(2,1)}, bf16[32,128,128]{2,1,0:T(8,128)(2,1)}, u32[]{:S(2)}, u32[]{:S(2)}) collective-permute-start(bf16[32,128,128]{2,1,0:T(8,128)(2,1)} %collective-permute-done.7.refs_9_.refs_11_.refs_5_), channel_id=1, source_target_pairs={{0,96},{32,0},{64,32},{96,64},{1,97},{33,1},{65,33},{97,65},{2,98}... | collective-permute-start | bytes 3145736 | tf_op jit(solution)/shard_map/ppermute | solution.py:388
  137.7 24.3 %copy-start.1 = (bf16[32,128,128]{2,1,0:T(8,128)(2,1)S(1)}, bf16[32,128,128]{2,1,0:T(8,128)(2,1)}, u32[]{:S(2)}) copy-start(bf16[32,128,128]{2,1,0:T(8,128)(2,1)} %copy-done) | copy-start | bytes 3145732
Sparse Core Ops, SparseCore 0:
  22.7 98.7 all-gather.2

commit v7 on v6

--- a/solution.py
+++ b/solution.py
@@ -14,7 +14,7 @@
 DEPTH = 8
 HALVES = 2
 PARTS = 4
-AHEAD = 3
+AHEAD = 6
 
 NT = (((1,), (1,)), ((), ()))
 TN = (((0,), (0,)), ((), ()))
@@ -63,9 +63,8 @@
 
 
 def hidden_kernel(kinds, first_ref, *refs):
-    nrows = len(kinds)
     per_row = 2 * HALVES
-    out_ref = refs[per_row * nrows]
+    out_ref = refs[-1]
     tiles = out_ref.shape[1]
     step = pl.program_id(0)
     for k, row in enumerate(kinds):
@@ -79,7 +78,7 @@
             old = own
 
 
-def hidden_gram(first, kinds, hidden):
+def hidden_gram(first, kinds, hidden, total, into=None):
     pieces = [piece for row in hidden for piece in row]
     blocks = pieces[0].shape[0]
     count = blocks // PARTS
@@ -87,15 +86,24 @@
     nrows = len(kinds)
     own = pl.BlockSpec((count, BLK, BLK), lambda i: (i, 0, 0))
     old = pl.BlockSpec((2, BLK, BLK), lambda i: (jnp.maximum(i * tiles - 1, 0), 0, 0))
+    place = kinds[0] // nrows
+    operands = [first, *[piece for row in hidden for piece in [*row, *row]]]
+    specs = [
+        pl.BlockSpec(first.shape, lambda i: (0, 0, 0)),
+        *[spec for _ in kinds for spec in [own] * HALVES + [old] * HALVES],
+    ]
+    aliases = {}
+    if into is not None:
+        aliases = {len(operands): 0}
+        operands.append(keep_in(pltpu.HBM, into))
+        specs.append(pl.BlockSpec(memory_space=pltpu.HBM))
     return pl.pallas_call(
         functools.partial(hidden_kernel, kinds),
-        out_shape=pltpu.HBM((nrows, blocks // 2, TILE, TILE), jnp.float32),
+        out_shape=pltpu.HBM((total, blocks // 2, TILE, TILE), jnp.float32),
         grid=(PARTS,),
-        in_specs=[
-            pl.BlockSpec(first.shape, lambda i: (0, 0, 0)),
-            *[spec for _ in kinds for spec in [own] * HALVES + [old] * HALVES],
-        ],
-        out_specs=pl.BlockSpec((nrows, tiles, TILE, TILE), lambda i: (0, i, 0, 0)),
+        in_specs=specs,
+        out_specs=pl.BlockSpec((nrows, tiles, TILE, TILE), lambda i: (place, i, 0, 0)),
+        input_output_aliases=aliases,
         compiler_params=pltpu.CompilerParams(vmem_limit_bytes=24 * 2**20),
         cost_estimate=pl.CostEstimate(
             flops=nrows * blocks * BLK * 4 * TILE * TILE,
@@ -103,10 +111,10 @@
             transcendentals=0,
         ),
         name="hidden_gram",
-    )(first, *[piece for row in hidden for piece in [*row, *row]])
-
-
-def early_kernel(kinds, rows_ref, ids_ref, pairs_hbm, g_hbm, out_ref, g_ref, pairs_ref, pair_sems, sems):
+    )(*operands)
+
+
+def early_kernel(kinds, rows_ref, ids_ref, pairs_hbm, g_hbm, out_ref, g_ref, last_ref, pairs_ref, pair_sems, sems):
     nrows = len(kinds)
     blocks, every = g_ref.shape[:2]
     count = blocks // PARTS
@@ -119,7 +127,7 @@
 
     def pair_copy(n):
         here = pl.ds(lax.rem(n, PARTS) * tiles, tiles)
-        slot = lax.rem(n, AHEAD + 1)
+        slot = lax.rem(n, AHEAD + 2)
         return pltpu.make_async_copy(pairs_hbm.at[n // PARTS, here], pairs_ref.at[slot], pair_sems.at[n])
 
     for n in range(AHEAD):
@@ -128,58 +136,62 @@
     out_ref[...] = jnp.zeros_like(out_ref)
     for k, row in enumerate(kinds):
 
-        @pl.loop(0, PARTS)
-        def _(c, k=k, row=row):
-            n = k * PARTS + c
-            copy(n).wait()
-            pair_copy(n).wait()
-
-            @pl.when(n + AHEAD < every * PARTS)
-            def _():
-                copy(n + AHEAD).start()
-
-            @pl.when(n + AHEAD < nrows * PARTS)
-            def _():
-                pair_copy(n + AHEAD).start()
-
-            slot = lax.rem(n, AHEAD + 1)
+        @pl.loop(0, PARTS // 2)
+        def _(i, k=k, row=row):
+            for n in (k * PARTS + 2 * i, k * PARTS + 2 * i + 1):
+                copy(n).wait()
+                pair_copy(n).wait()
+
+                @pl.when(n + AHEAD < every * PARTS)
+                def _():
+                    copy(n + AHEAD).start()
+
+                @pl.when(n + AHEAD < nrows * PARTS)
+                def _():
+                    pair_copy(n + AHEAD).start()
+
             share = jnp.zeros((DOCS, BLK), jnp.float32)
-            old = flat(g_ref[pl.ds(jnp.maximum(c * count - 2, 0), 2), row])
-            for t in range(tiles):
-                at = c * count + 2 * t
+            begin = 2 * i * count
+            old = flat(g_ref[pl.ds(jnp.maximum(begin - 2, 0), 2), row])
+            for t in range(2 * tiles):
+                at = begin + 2 * t
+                slot = lax.rem(k * PARTS + 2 * i + t // tiles, AHEAD + 2)
                 own = flat(g_ref[pl.ds(at, 2), row])
-                terms = pairs_ref[slot, t] * pair_products(old, own)
+                terms = pairs_ref[slot, t % tiles] * pair_products(old, own)
                 share += doc_sums(terms, line_of(ids_ref, at, row))
                 old = own
             here = pl.ds(pl.multiple_of(rows_ref[row] * DOCS, DOCS), DOCS)
             out_ref[here, :] += share
 
-    for n in range(nrows * PARTS, every * PARTS):
-        copy(n).wait()
-        if n + AHEAD < every * PARTS:
-            copy(n + AHEAD).start()
+    @pl.loop(0, PARTS // 2)
+    def _(i):
+        for n in (nrows * PARTS + 2 * i, nrows * PARTS + 2 * i + 1):
+            copy(n).wait()
+        begin = 2 * i * count
+        old = flat(g_ref[pl.ds(jnp.maximum(begin - 2, 0), 2), nrows])
+        for t in range(2 * tiles):
+            own = flat(g_ref[pl.ds(begin + 2 * t, 2), nrows])
+            last_ref[2 * i * tiles + t] = pair_products(old, own)
+            old = own
 
 
 def late_kernel(row, rows_ref, ids_ref, first_ref, *refs):
     h_refs = refs[:HALVES]
-    g_ref, init_ref, out_ref, acc = refs[HALVES:]
-    count = g_ref.shape[0] // PARTS
+    last_ref, init_ref, out_ref, acc = refs[HALVES:]
+    tiles = last_ref.shape[0] // 2
     acc[...] = init_ref[...]
 
-    @pl.loop(0, PARTS)
-    def _(c):
+    @pl.loop(0, 2)
+    def _(i):
         share = jnp.zeros((DOCS, BLK), jnp.float32)
-        before = jnp.maximum(c * count - 2, 0)
-        old_h = columns_of(h_refs, before, 2)
-        old_g = flat(g_ref[pl.ds(before, 2), row])
-        for t in range(count // 2):
-            at = c * count + 2 * t
-            first = line_of(first_ref, at, row) - at * BLK
-            own_h = columns_of(h_refs, at, 2)
-            own_g = flat(g_ref[pl.ds(at, 2), row])
-            terms = counted(pair_products(old_h, own_h) * pair_products(old_g, own_g), first)
-            share += doc_sums(terms, line_of(ids_ref, at, row))
-            old_h, old_g = own_h, own_g
+        old = columns_of(h_refs, jnp.maximum(2 * i * tiles - 2, 0), 2)
+        for t in range(tiles):
+            number = i * tiles + t
+            first = line_of(first_ref, 2 * number, row) - number * TILE
+            own = columns_of(h_refs, 2 * number, 2)
+            terms = counted(pair_products(old, own), first) * last_ref[number]
+            share += doc_sums(terms, line_of(ids_ref, 2 * number, row))
+            old = own
         here = pl.ds(pl.multiple_of(rows_ref[row] * DOCS, DOCS), DOCS)
         acc[here, :] += share
 
@@ -216,25 +228,26 @@
         out_shape=[
             jax.ShapeDtypeStruct((every * DOCS, BLK), jnp.float32),
             pltpu.VMEM(grad.shape, grad.dtype),
+            pltpu.VMEM((pairs.shape[1], TILE, TILE), jnp.float32),
         ],
         grid_spec=pltpu.PrefetchScalarGridSpec(
             num_scalar_prefetch=1,
             grid=(),
             in_specs=[*in_vmem(1), *in_hbm(2)],
-            out_specs=in_vmem(2),
+            out_specs=in_vmem(3),
             scratch_shapes=[
-                pltpu.VMEM((AHEAD + 1, tiles, TILE, TILE), jnp.float32),
+                pltpu.VMEM((AHEAD + 2, tiles, TILE, TILE), jnp.float32),
                 pltpu.SemaphoreType.DMA((len(kinds) * PARTS,)),
                 pltpu.SemaphoreType.DMA((every * PARTS,)),
             ],
         ),
-        compiler_params=pltpu.CompilerParams(vmem_limit_bytes=8 * 2**20),
+        compiler_params=pltpu.CompilerParams(vmem_limit_bytes=12 * 2**20),
         cost_estimate=gram_cost(len(kinds), grad),
         name="gram",
     )(rows, ids, keep_in(pltpu.HBM, pairs), keep_in(pltpu.HBM, grad))
 
 
-def gram_late(rows, ids, first, row, hidden, grad, init, devices):
+def gram_late(rows, ids, first, row, hidden, last, init, devices):
     return pl.pallas_call(
         functools.partial(late_kernel, row),
         out_shape=jax.ShapeDtypeStruct((devices, 1, BLK), jnp.float32),
@@ -245,10 +258,12 @@
             out_specs=pl.BlockSpec(memory_space=pltpu.VMEM),
             scratch_shapes=[pltpu.VMEM(init.shape, jnp.float32)],
         ),
-        compiler_params=pltpu.CompilerParams(vmem_limit_bytes=4 * 2**20),
-        cost_estimate=gram_cost(1, grad),
+        compiler_params=pltpu.CompilerParams(vmem_limit_bytes=8 * 2**20),
+        cost_estimate=pl.CostEstimate(
+            flops=2 * 2 * last.size * TILE, bytes_accessed=last.size * 4, transcendentals=0
+        ),
         name="gram_late",
-    )(rows, ids, first, *hidden, keep_in(pltpu.VMEM, grad), init)
+    )(rows, ids, first, *hidden, keep_in(pltpu.VMEM, last), init)
 
 
 def product_kernel(nrows, bound, rows_ref, ids_ref, norms_ref, *refs):
@@ -257,13 +272,15 @@
     blocks = g_ref.shape[0]
     steps = blocks // DEPTH
 
+    order = [nrows - 2, *range(nrows - 2), nrows - 1]
+
     def hidden_copies(k):
         return [
             pltpu.make_async_copy(pieces[n], h_ref.at[n], h_sems.at[n])
             for n in range(HALVES * k, HALVES * (k + 1))
         ]
 
-    for piece in hidden_copies(0):
+    for piece in hidden_copies(order[0]):
         piece.start()
     norms = jnp.sum(norms_ref[...], axis=0)
     clip = bound / jnp.maximum(jnp.sqrt(norms), bound) / nrows
@@ -273,7 +290,7 @@
         factor[k] = jnp.take_along_axis(table, ids, axis=1)
 
     def scale(n, slot):
-        k, begin = n // steps, n % steps * DEPTH
+        k, begin = order[n // steps], n % steps * DEPTH
         lines = jnp.concatenate([factor[k, begin : begin + DEPTH, :]] * (BLK // DEPTH), axis=0).T
         for j in range(DEPTH):
             factors = jnp.broadcast_to(lines[:, j : j + 1], (BLK, BLK))
@@ -283,12 +300,12 @@
 
     scale(0, 0)
     for n in range(nrows * steps):
-        k, begin = n // steps, n % steps * DEPTH
+        k, begin = order[n // steps], n % steps * DEPTH
         if begin == 0:
             for piece in hidden_copies(k):
                 piece.wait()
-            if k + 1 < nrows:
-                for piece in hidden_copies(k + 1):
+            if n // steps + 1 < nrows:
+                for piece in hidden_copies(order[n // steps + 1]):
                     piece.start()
         if n + 1 < nrows * steps:
             scale(n + 1, (n + 1) % 2)
@@ -404,10 +421,10 @@
 
     keep, up, down, across = quarters(me[None], (0, 1, 3, 2), grad_out[0], segment)
     across = shift(across, 2)
-    received = [keep, shift(up, 1), shift(down, -1), across]
+    received = [shift(up, 1), shift(down, -1), keep, across]
 
     chunks = columns(hidden[0], blocks)
-    chunks, received = lax.optimization_barrier((chunks, received))
+    received, _ = lax.optimization_barrier((received, chunks))
 
     every_grad = jnp.stack([part[:tokens] for part in received])
     every_grad = lax.all_gather(every_grad, "ctx", axis=0, tiled=False)
@@ -421,7 +438,7 @@
         ready = own
         below, above = lax.optimization_barrier((shift(own, 1), shift(own, -1)))
         far = shift(below, 1) if q < HALVES // 2 else shift(above, -1)
-        for row, piece in zip(hidden_rows, (own, below, above, far)):
+        for row, piece in zip(hidden_rows, (below, above, own, far)):
             row.append(piece)
 
     ids = jnp.stack([part[tokens, :BLK] for part in received]).astype(jnp.int32)
@@ -430,12 +447,13 @@
     ids = lax.all_to_all(ids, "ctx", 0, 0, tiled=True)
     first = starts(ids)
 
-    rows = lax.rem(me + jnp.array([0, 3, 1, 2], jnp.int32), row_count)
+    rows = lax.rem(me + jnp.array([3, 1, 0, 2], jnp.int32), row_count)
     kinds = (0, 1, 2)
-    pairs = hidden_gram(first, kinds, hidden_rows[:3])
-    early, grads = gram_early(rows, ids, kinds, pairs, every_grad)
+    pairs = hidden_gram(first, kinds[2:], hidden_rows[2:3], len(kinds))
+    pairs = hidden_gram(first, kinds[:2], hidden_rows[:2], len(kinds), pairs)
+    early, grads, last = gram_early(rows, ids, kinds, pairs, every_grad)
     devices = row_count * blocks
-    partial = gram_late(rows, ids, first, 3, hidden_rows[3], grads, early, devices)
+    partial = gram_late(rows, ids, first, 3, hidden_rows[3], last, early, devices)
     norms = lax.all_to_all(partial, ("dp", "ctx"), 0, 0, tiled=True)
 
     bound = math.sqrt(tokens * width_hidden * width_grad)

time: 180 us -> 176 us (0.978)
  waiting for transfers between devices: 38.3 us -> 36.2 us
    pallas_call x1, Pallas kernels: 7.53 us -> 3.83 us  [gram_late(): pl.pallas_call(functools.partial(late_kernel, row), out_shape=jax.ShapeDt...]
    ppermute x9, waiting for transfers between devices: 9.04 us -> 5.55 us  [shift(): lax.ppermute(block, 'dp', [(i, (i + distance) % size) for i in range(size)])]
    pallas_call x1 -> x2, Pallas kernels: 9.23 us -> 11.3 us  [hidden_gram(): pl.pallas_call(functools.partial(hidden_kernel, kinds), out_shape=pltpu.H...]
  transfers between devices with their start and end apart: 12 -> 12, of which waited for: 5 -> 5; matrix products, arithmetic and copies ran while one was open for 2% -> 2% of each run, Pallas kernels for 16% -> 19%
where the time goes in v7:
time: 176 us
  Pallas kernels  49.5 us (28%)
  blocking collectives  48.1 us (27%)
  waiting for transfers between devices  36.2 us (21%)
  starting transfers between devices  24 us (14%)
  between operations  13.6 us (8%)
  other arithmetic  3.63 us (2%)
    all_to_all x1, blocking collectives, body(): own = lax.all_to_all(chunk, 'ctx', 0, 0, tiled=True)  32.9 us
    all_to_all x1, waiting for transfers between devices, body(): own = lax.all_to_all(chunk, 'ctx', 0, 0, tiled=True)  20.6 us
    pallas_call x1, Pallas kernels, gram_early(): pl.pallas_call(functools.partial(early_kernel, kinds), out_shape=[jax.Sha...  17.9 us
    all_to_all x1, blocking collectives, body(): norms = lax.all_to_all(partial, ('dp', 'ctx'), 0, 0, tiled=True)  15.2 us
    ppermute x9, starting transfers between devices, shift(): lax.ppermute(block, 'dp', [(i, (i + distance) % size) for i in range(size)])  13.1 us
    pallas_call x2, Pallas kernels, hidden_gram(): pl.pallas_call(functools.partial(hidden_kernel, kinds), out_shape=pltpu.H...  11.3 us
    pallas_call x1, Pallas kernels, product(): pl.pallas_call(functools.partial(product_kernel, nrows, bound), out_shape...  10.5 us
    all_to_all x1, waiting for transfers between devices, body(): ids = lax.all_to_all(ids, 'ctx', 0, 0, tiled=True)  7.75 us
  transfers between devices with their start and end apart: 12, of which 5 were waited for; matrix products, arithmetic and copies ran while one was open for 2% of the time, Pallas kernels for 19%

profile of v7, /device:TPU:1, one launch (start us, length us, event | category | flops | bytes accessed | tf_op | source)
XLA Modules:
  0.0 175.8 jit_solution(7402753950871923219)
XLA Ops:
  6.5 0.0 all-gather.3.cloned.1.call-start
  6.5 2.0 %quarters.1 = (bf16[144,640]{1,0:T(8,128)(2,1)}, bf16[144,640]{1,0:T(8,128)(2,1)}, bf16[144,640]{1,0:T(8,128)(2,1)}, bf16[144,640]{1,0:T(8,128)(2,1)}) custom-call(s32[1]{0:T(128)} %bitcast.me_ref, s32[1,128]{1,0:T(1,128)} %ids_ref.1, bf16[128,2560]{1,0:T(8,128)(2,1)} %bitcast.12, bf16[128,2560]{1,0:T(8,128)(2,1)} %bitcast.13, bf16[128,2560]{1,0:T(8,128)(2,1)} %bitcast.14, ...), custom_call_target="tpu_custom_call" | custom-call | tf_op jit(solution)/shard_map/quarters/pallas_call | solution.py:366
  8.6 0.0 copy-start.3
  8.6 2.1 %collective-permute-start = (bf16[144,640]{1,0:T(8,128)(2,1)}, bf16[144,640]{1,0:T(8,128)(2,1)S(1)}, u32[]{:S(2)}, u32[]{:S(2)}) collective-permute-start(bf16[144,640]{1,0:T(8,128)(2,1)} %get-tuple-element.24), channel_id=1, source_target_pairs={{0,32},{32,64},{64,96},{96,0},{1,33},{33,65},{65,97},{97,1},{2,34}... | collective-permute-start | bytes 552968 | tf_op jit(solution)/shard_map/ppermute | solution.py:405
  10.7 1.5 collective-permute-start.1
  12.2 1.6 collective-permute-start.2
  13.8 3.9 %columns.1 = (bf16[32,128,128]{2,1,0:T(8,128)(2,1)}, bf16[32,128,128]{2,1,0:T(8,128)(2,1)}) custom-call(bf16[128,8192]{1,0:T(8,128)(2,1)} %bitcast.16), custom_call_target="tpu_custom_call" | custom-call | tf_op jit(solution)/shard_map/columns/pallas_call | solution.py:393
  17.7 0.0 copy-start.2
  17.7 0.0 collective-permute-done
  17.7 0.0 collective-permute-done.1
  17.7 3.8 %collective-permute-done.2 = bf16[144,640]{1,0:T(8,128)(2,1)S(1)} collective-permute-done((bf16[144,640]{1,0:T(8,128)(2,1)}, bf16[144,640]{1,0:T(8,128)(2,1)S(1)}, u32[]{:S(2)}, u32[]{:S(2)}) %collective-permute-start.2) | collective-permute-done | bytes 184352 | tf_op jit(solution)/shard_map/ppermute | solution.py:405
  21.5 0.0 copy-done.3
  21.6 0.9 pad_maximum_fusion
  22.6 0.0 all-gather.3.cloned.1.call-update
  22.6 0.0 copy-done.2
  22.6 0.0 copy-start.4
  22.6 32.9 %all_to_all.20.refs_0_.refs_2_.refs_4_ = bf16[32,128,128]{2,1,0:T(8,128)(2,1)S(1)} all-to-all(bf16[32,128,128]{2,1,0:T(8,128)(2,1)S(1)} %copy-done.2), channel_id=1, replica_groups=mesh['dp'=4,'ctx'=32] {'ctx'}, dimensions={0} | all-to-all | bytes 2097152 | tf_op jit(solution)/shard_map/all_to_all | solution.py:437
  55.5 5.3 %all-to-all-start.1 = ((bf16[32,128,128]{2,1,0:T(8,128)(2,1)}), bf16[32,128,128]{2,1,0:T(8,128)(2,1)S(1)}, u32[]{:S(2)}, u32[]{:S(2)}) async-start(bf16[32,128,128]{2,1,0:T(8,128)(2,1)} %get-tuple-element.34), calls=%async_computation.1 | async-start | bytes 2097152 | tf_op jit(solution)/shard_map/all_to_all | solution.py:437
  60.8 0.8 collective-permute-start.3
  61.6 2.0 %collective-permute-start.4 = (bf16[32,128,128]{2,1,0:T(8,128)(2,1)S(1)}, bf16[32,128,128]{2,1,0:T(8,128)(2,1)}, u32[]{:S(2)}, u32[]{:S(2)}) collective-permute-start(bf16[32,128,128]{2,1,0:T(8,128)(2,1)S(1)} %all_to_all.20.refs_0_.refs_2_.refs_4_), channel_id=1, source_target_pairs={{0,96},{32,0},{64,32},{96,64},{1,97},{33,1},{65,33},{97,65},{2,98}... | collective-permute-start | bytes 3145736 | tf_op jit(solution)/shard_map/ppermute | solution.py:405
  63.6 20.6 %all-to-all-done.1.refs_1_.refs_3_.refs_5_ = bf16[32,128,128]{2,1,0:T(8,128)(2,1)S(1)} async-done(((bf16[32,128,128]{2,1,0:T(8,128)(2,1)}), bf16[32,128,128]{2,1,0:T(8,128)(2,1)S(1)}, u32[]{:S(2)}, u32[]{:S(2)}) %all-to-all-start.1) | async-done | bytes 1048608 | tf_op jit(solution)/shard_map/all_to_all | solution.py:437
  84.2 0.0 copy-start
  84.2 0.2 collective-permute-start.6
  84.4 2.5 %collective-permute-start.7 = (bf16[32,128,128]{2,1,0:T(8,128)(2,1)S(1)}, bf16[32,128,128]{2,1,0:T(8,128)(2,1)}, u32[]{:S(2)}, u32[]{:S(2)}) collective-permute-start(bf16[32,128,128]{2,1,0:T(8,128)(2,1)S(1)} %all-to-all-done.1.refs_1_.refs_3_.refs_5_), channel_id=1, source_target_pairs={{0,96},{32,0},{64,32},{96,64},{1,97},{33,1},{65,33},{97,65},{2,98}... | collective-permute-start | bytes 3145736 | tf_op jit(solution)/shard_map/ppermute | solution.py:405
  86.9 0.6 broadcast_in_dim.13
  87.6 5.6 %all-to-all-start.2 = ((s32[32,4,128]{2,1,0:T(4,128)}), s32[32,4,128]{2,1,0:T(4,128)S(1)}, u32[]{:S(2)}, u32[]{:S(2)}) async-start(s32[32,4,128]{2,1,0:T(4,128)} %broadcast_in_dim.13), calls=%async_computation.2 | async-start | bytes 131072 | tf_op jit(solution)/shard_map/all_to_all | solution.py:447
  93.1 0.0 copy-done.4
  93.2 0.0 collective-permute-done.3.refs_0_.refs_2_
  93.2 0.0 collective-permute-done.4.refs_4_.refs_6_.refs_2_
  93.2 0.1 collective-permute-start.5
  93.3 7.7 %all-to-all-done.2.ids_ref = s32[32,4,128]{2,1,0:T(4,128)S(1)} async-done(((s32[32,4,128]{2,1,0:T(4,128)}), s32[32,4,128]{2,1,0:T(4,128)S(1)}, u32[]{:S(2)}, u32[]{:S(2)}) %all-to-all-start.2) | async-done | bytes 65568 | tf_op jit(solution)/shard_map/all_to_all | solution.py:447
  101.0 2.4 %convert_reduce_fusion = s32[32,4]{1,0:T(8,128)S(1)} fusion(s32[32,4,128]{2,0,1:T(8,128)S(1)} %copy.6), kind=kLoop, calls=%fused_computation.1 | loop fusion | flops 1572736 | bytes 66048 | tf_op jit(solution)/shard_map/reduce_sum | solution.py:410
  103.4 0.3 select_reduce_fusion
  103.8 3.5 %hidden_gram.2.refs_8_ = f32[3,16,256,256]{3,2,1,0:T(8,128)} custom-call(s32[32,4,128]{2,1,0:T(4,128)S(1)} %copy.9.first_ref, bf16[32,128,128]{2,1,0:T(8,128)(2,1)S(1)} %all_to_all.20.refs_0_.refs_2_.refs_4_, bf16[32,128,128]{2,1,0:T(8,128)(2,1)S(1)} %all-to-all-done.1.refs_1_.refs_3_.refs_5_, bf16[32,128,128]{2,1,0:T(8,128)(2,1)S(1)} %all_to_all.20.refs_0_.refs_2_.refs_4_, ...), custom_call_target="tpu_custom_call" | custom-call | flops 1073741824 | bytes 6291456 | tf_op jit(solution)/shard_map/hidden_gram/pallas_call | solution.py:100
  107.2 0.0 copy-done
  107.2 1.7 collective-permute-done.6.refs_1_.refs_3_
  109.0 0.0 collective-permute-done.7.refs_5_.refs_7_.refs_3_
  109.0 2.4 %collective-permute-start.8 = (bf16[32,128,128]{2,1,0:T(8,128)(2,1)}, bf16[32,128,128]{2,1,0:T(8,128)(2,1)}, u32[]{:S(2)}, u32[]{:S(2)}) collective-permute-start(bf16[32,128,128]{2,1,0:T(8,128)(2,1)} %collective-permute-done.7.refs_5_.refs_7_.refs_3_), channel_id=1, source_target_pairs={{0,96},{32,0},{64,32},{96,64},{1,97},{33,1},{65,33},{97,65},{2,98}... | collective-permute-start | bytes 3145736 | tf_op jit(solution)/shard_map/ppermute | solution.py:405
  111.4 7.8 %hidden_gram.3.pairs_hbm = f32[3,16,256,256]{3,2,1,0:T(8,128)} custom-call(s32[32,4,128]{2,1,0:T(4,128)S(1)} %copy.9.first_ref, bf16[32,128,128]{2,1,0:T(8,128)(2,1)} %collective-permute-done.3.refs_0_.refs_2_, bf16[32,128,128]{2,1,0:T(8,128)(2,1)} %collective-permute-done.6.refs_1_.refs_3_, ...), custom_call_target="tpu_custom_call", output_to_operand_aliasing={{}: (9, {})} | custom-call | flops 2147483648 | bytes 12582912 | tf_op jit(solution)/shard_map/hidden_gram/pallas_call | solution.py:100
  119.2 2.3 %all-gather.3.cloned.1.call-done = bf16[128,128,640]{2,1,0:T(8,128)(2,1)} async-done(((bf16[4,128,640]{2,1,0:T(8,128)(2,1)}), bf16[128,128,640]{2,1,0:T(8,128)(2,1)}) %all-gather.3.cloned.1.call-update) | async-done | bytes 20971536 | tf_op jit(solution)/shard_map/all_gather | solution.py:430
  121.5 17.9 %gram.1 = (f32[128,128]{1,0:T(8,128)S(1)}, bf16[32,4,128,640]{3,2,1,0:T(8,128)(2,1)S(1)}, f32[16,256,256]{2,1,0:T(8,128)S(1)}) custom-call(s32[4]{0:T(128)S(1)} %compare_select_fusion.rows_ref, s32[32,4,128]{2,1,0:T(4,128)S(1)} %all-to-all-done.2.ids_ref, f32[3,16,256,256]{3,2,1,0:T(8,128)} %hidden_gram.3.pairs_hbm, bf16[32,4,128,640]{3,2,1,0:T(8,128)(2,1)} %bitcast.17), custom_call_target="tpu_custom_call" | custom-call | flops 11274289152 | bytes 20971520 | tf_op jit(solution)/shard_map/gram/pallas_call | solution.py:226
  139.4 0.0 collective-permute-done.5.refs_0_.refs_6_
  139.4 0.0 collective-permute-done.8.refs_1_.refs_7_
  139.4 0.0 copy-start.1
  139.4 3.8 %gram_late.1 = f32[128,1,128]{2,1,0:T(1,128)S(1)} custom-call(s32[4]{0:T(128)S(1)} %compare_select_fusion.rows_ref, s32[32,4,128]{2,1,0:T(4,128)S(1)} %all-to-all-done.2.ids_ref, s32[32,4,128]{2,1,0:T(4,128)S(1)} %copy.9.first_ref, bf16[32,128,128]{2,1,0:T(8,128)(2,1)} %collective-permute-done.5.refs_0_.refs_6_, ...), custom_call_target="tpu_custom_call" | custom-call | flops 1073741824 | bytes 4194304 | tf_op jit(solution)/shard_map/gram_late/pallas_call | solution.py:251
  143.3 15.2 %all_to_all.21.norms_ref = f32[128,1,128]{2,1,0:T(1,128)S(1)} all-to-all(f32[128,1,128]{2,1,0:T(1,128)S(1)} %gram_late.1), channel_id=1, replica_groups=mesh['dp'=4,'ctx'=32] {'dp','ctx'}, dimensions={0} | all-to-all | bytes 131072 | tf_op jit(solution)/shard_map/all_to_all | solution.py:457
  158.4 0.0 copy-done.1
  158.4 10.5 %product.1 = f32[256,640]{1,0:T(8,128)} custom-call(s32[4]{0:T(128)S(1)} %compare_select_fusion.rows_ref, s32[32,4,128]{2,1,0:T(4,128)S(1)} %all-to-all-done.2.ids_ref, f32[128,1,128]{2,1,0:T(1,128)S(1)} %all_to_all.21.norms_ref, bf16[32,128,128]{2,1,0:T(8,128)(2,1)} %collective-permute-done.3.refs_0_.refs_2_, ...), custom_call_target="tpu_custom_call" | custom-call | flops 5368709120 | bytes 29360128 | tf_op jit(solution)/shard_map/product/pallas_call | solution.py:327
  (10 shorter events, 0.2 us)
Async XLA Ops:
  6.5 114.9 %all-gather.3.cloned.1.call-start = ((), (), s32[]{:S(2)}) async-start(), calls=%async_computation.4 | async-start | bytes 21626880 | tf_op jit(solution)/shard_map/all_gather | solution.py:430
  8.6 13.0 %copy-start.3 = (bf16[144,640]{1,0:T(8,128)(2,1)S(1)}, bf16[144,640]{1,0:T(8,128)(2,1)}, u32[]{:S(2)}) copy-start(bf16[144,640]{1,0:T(8,128)(2,1)} %get-tuple-element.32) | copy-start | bytes 552964
  8.6 9.1 %collective-permute-start = (bf16[144,640]{1,0:T(8,128)(2,1)}, bf16[144,640]{1,0:T(8,128)(2,1)S(1)}, u32[]{:S(2)}, u32[]{:S(2)}) collective-permute-start(bf16[144,640]{1,0:T(8,128)(2,1)} %get-tuple-element.24), channel_id=1, source_target_pairs={{0,32},{32,64},{64,96},{96,0},{1,33},{33,65},{65,97},{97,1},{2,34}... | collective-permute-start | bytes 552968 | tf_op jit(solution)/shard_map/ppermute | solution.py:405
  10.7 7.0 %collective-permute-start.1 = (bf16[144,640]{1,0:T(8,128)(2,1)}, bf16[144,640]{1,0:T(8,128)(2,1)S(1)}, u32[]{:S(2)}, u32[]{:S(2)}) collective-permute-start(bf16[144,640]{1,0:T(8,128)(2,1)} %get-tuple-element.25), channel_id=1, source_target_pairs={{0,96},{32,0},{64,32},{96,64},{1,97},{33,1},{65,33},{97,65},{2,98}... | collective-permute-start | bytes 552968 | tf_op jit(solution)/shard_map/ppermute | solution.py:405
  12.2 9.3 %collective-permute-start.2 = (bf16[144,640]{1,0:T(8,128)(2,1)}, bf16[144,640]{1,0:T(8,128)(2,1)S(1)}, u32[]{:S(2)}, u32[]{:S(2)}) collective-permute-start(bf16[144,640]{1,0:T(8,128)(2,1)} %get-tuple-element.27), channel_id=1, source_target_pairs={{0,64},{32,96},{64,0},{96,32},{1,65},{33,97},{65,1},{97,33},{2,66}... | collective-permute-start | bytes 552968 | tf_op jit(solution)/shard_map/ppermute | solution.py:405
  17.7 4.9 %copy-start.2 = (bf16[32,128,128]{2,1,0:T(8,128)(2,1)S(1)}, bf16[32,128,128]{2,1,0:T(8,128)(2,1)}, u32[]{:S(2)}) copy-start(bf16[32,128,128]{2,1,0:T(8,128)(2,1)} %get-tuple-element.28) | copy-start | bytes 3145732
  22.6 70.5 %copy-start.4 = (s32[4]{0:T(128)S(1)}, s32[4]{0:T(128)}, u32[]{:S(2)}) copy-start(s32[4]{0:T(128)} %constant.14.clone) | copy-start | bytes 52
  55.5 28.7 %all-to-all-start.1 = ((bf16[32,128,128]{2,1,0:T(8,128)(2,1)}), bf16[32,128,128]{2,1,0:T(8,128)(2,1)S(1)}, u32[]{:S(2)}, u32[]{:S(2)}) async-start(bf16[32,128,128]{2,1,0:T(8,128)(2,1)} %get-tuple-element.34), calls=%async_computation.1 | async-start | bytes 2097152 | tf_op jit(solution)/shard_map/all_to_all | solution.py:437
  60.8 32.3 %collective-permute-start.3 = (bf16[32,128,128]{2,1,0:T(8,128)(2,1)S(1)}, bf16[32,128,128]{2,1,0:T(8,128)(2,1)}, u32[]{:S(2)}, u32[]{:S(2)}) collective-permute-start(bf16[32,128,128]{2,1,0:T(8,128)(2,1)S(1)} %all_to_all.20.refs_0_.refs_2_.refs_4_), channel_id=1, source_target_pairs={{0,32},{32,64},{64,96},{96,0},{1,33},{33,65},{65,97},{97,1},{2,34}... | collective-permute-start | bytes 3145736 | tf_op jit(solution)/shard_map/ppermute | solution.py:405
  61.6 31.6 %collective-permute-start.4 = (bf16[32,128,128]{2,1,0:T(8,128)(2,1)S(1)}, bf16[32,128,128]{2,1,0:T(8,128)(2,1)}, u32[]{:S(2)}, u32[]{:S(2)}) collective-permute-start(bf16[32,128,128]{2,1,0:T(8,128)(2,1)S(1)} %all_to_all.20.refs_0_.refs_2_.refs_4_), channel_id=1, source_target_pairs={{0,96},{32,0},{64,32},{96,64},{1,97},{33,1},{65,33},{97,65},{2,98}... | collective-permute-start | bytes 3145736 | tf_op jit(solution)/shard_map/ppermute | solution.py:405
  84.2 23.0 %copy-start = (bf16[32,128,128]{2,1,0:T(8,128)(2,1)}, bf16[32,128,128]{2,1,0:T(8,128)(2,1)S(1)}, u32[]{:S(2)}) copy-start(bf16[32,128,128]{2,1,0:T(8,128)(2,1)S(1)} %all-to-all-done.1.refs_1_.refs_3_.refs_5_) | copy-start | bytes 3145732
  84.2 24.8 %collective-permute-start.6 = (bf16[32,128,128]{2,1,0:T(8,128)(2,1)S(1)}, bf16[32,128,128]{2,1,0:T(8,128)(2,1)}, u32[]{:S(2)}, u32[]{:S(2)}) collective-permute-start(bf16[32,128,128]{2,1,0:T(8,128)(2,1)S(1)} %all-to-all-done.1.refs_1_.refs_3_.refs_5_), channel_id=1, source_target_pairs={{0,32},{32,64},{64,96},{96,0},{1,33},{33,65},{65,97},{97,1},{2,34}... | collective-permute-start | bytes 3145736 | tf_op jit(solution)/shard_map/ppermute | solution.py:405
  84.4 24.6 %collective-permute-start.7 = (bf16[32,128,128]{2,1,0:T(8,128)(2,1)S(1)}, bf16[32,128,128]{2,1,0:T(8,128)(2,1)}, u32[]{:S(2)}, u32[]{:S(2)}) collective-permute-start(bf16[32,128,128]{2,1,0:T(8,128)(2,1)S(1)} %all-to-all-done.1.refs_1_.refs_3_.refs_5_), channel_id=1, source_target_pairs={{0,96},{32,0},{64,32},{96,64},{1,97},{33,1},{65,33},{97,65},{2,98}... | collective-permute-start | bytes 3145736 | tf_op jit(solution)/shard_map/ppermute | solution.py:405
  87.6 13.5 %all-to-all-start.2 = ((s32[32,4,128]{2,1,0:T(4,128)}), s32[32,4,128]{2,1,0:T(4,128)S(1)}, u32[]{:S(2)}, u32[]{:S(2)}) async-start(s32[32,4,128]{2,1,0:T(4,128)} %broadcast_in_dim.13), calls=%async_computation.2 | async-start | bytes 131072 | tf_op jit(solution)/shard_map/all_to_all | solution.py:447
  93.2 46.2 %collective-permute-start.5 = (bf16[32,128,128]{2,1,0:T(8,128)(2,1)}, bf16[32,128,128]{2,1,0:T(8,128)(2,1)}, u32[]{:S(2)}, u32[]{:S(2)}) collective-permute-start(bf16[32,128,128]{2,1,0:T(8,128)(2,1)} %collective-permute-done.3.refs_0_.refs_2_), channel_id=1, source_target_pairs={{0,32},{32,64},{64,96},{96,0},{1,33},{33,65},{65,97},{97,1},{2,34}... | collective-permute-start | bytes 3145736 | tf_op jit(solution)/shard_map/ppermute | solution.py:405
  109.0 30.4 %collective-permute-start.8 = (bf16[32,128,128]{2,1,0:T(8,128)(2,1)}, bf16[32,128,128]{2,1,0:T(8,128)(2,1)}, u32[]{:S(2)}, u32[]{:S(2)}) collective-permute-start(bf16[32,128,128]{2,1,0:T(8,128)(2,1)} %collective-permute-done.7.refs_5_.refs_7_.refs_3_), channel_id=1, source_target_pairs={{0,96},{32,0},{64,32},{96,64},{1,97},{33,1},{65,33},{97,65},{2,98}... | collective-permute-start | bytes 3145736 | tf_op jit(solution)/shard_map/ppermute | solution.py:405
  139.4 19.0 %copy-start.1 = (bf16[32,128,128]{2,1,0:T(8,128)(2,1)S(1)}, bf16[32,128,128]{2,1,0:T(8,128)(2,1)}, u32[]{:S(2)}) copy-start(bf16[32,128,128]{2,1,0:T(8,128)(2,1)} %copy-done) | copy-start | bytes 3145732
Sparse Core Ops, SparseCore 0:
  22.7 98.7 all-gather.2

commit v8 on v7

--- a/solution.py
+++ b/solution.py
@@ -134,34 +134,39 @@
         copy(n).start()
         pair_copy(n).start()
     out_ref[...] = jnp.zeros_like(out_ref)
+
+    def add(k, row, c, parts):
+        for n in (k * PARTS + c + p for p in range(parts)):
+            copy(n).wait()
+            pair_copy(n).wait()
+
+            @pl.when(n + AHEAD < every * PARTS)
+            def _():
+                copy(n + AHEAD).start()
+
+            @pl.when(n + AHEAD < nrows * PARTS)
+            def _():
+                pair_copy(n + AHEAD).start()
+
+        share = jnp.zeros((DOCS, BLK), jnp.float32)
+        begin = c * count
+        old = flat(g_ref[pl.ds(jnp.maximum(begin - 2, 0), 2), row])
+        for t in range(parts * tiles):
+            at = begin + 2 * t
+            slot = lax.rem(k * PARTS + c + t // tiles, AHEAD + 2)
+            own = flat(g_ref[pl.ds(at, 2), row])
+            terms = pairs_ref[slot, t % tiles] * pair_products(old, own)
+            share += doc_sums(terms, line_of(ids_ref, at, row))
+            old = own
+        here = pl.ds(pl.multiple_of(rows_ref[row] * DOCS, DOCS), DOCS)
+        out_ref[here, :] += share
+
     for k, row in enumerate(kinds):
-
-        @pl.loop(0, PARTS // 2)
-        def _(i, k=k, row=row):
-            for n in (k * PARTS + 2 * i, k * PARTS + 2 * i + 1):
-                copy(n).wait()
-                pair_copy(n).wait()
-
-                @pl.when(n + AHEAD < every * PARTS)
-                def _():
-                    copy(n + AHEAD).start()
-
-                @pl.when(n + AHEAD < nrows * PARTS)
-                def _():
-                    pair_copy(n + AHEAD).start()
-
-            share = jnp.zeros((DOCS, BLK), jnp.float32)
-            begin = 2 * i * count
-            old = flat(g_ref[pl.ds(jnp.maximum(begin - 2, 0), 2), row])
-            for t in range(2 * tiles):
-                at = begin + 2 * t
-                slot = lax.rem(k * PARTS + 2 * i + t // tiles, AHEAD + 2)
-                own = flat(g_ref[pl.ds(at, 2), row])
-                terms = pairs_ref[slot, t % tiles] * pair_products(old, own)
-                share += doc_sums(terms, line_of(ids_ref, at, row))
-                old = own
-            here = pl.ds(pl.multiple_of(rows_ref[row] * DOCS, DOCS), DOCS)
-            out_ref[here, :] += share
+        if k == 0:
+            pl.loop(0, 2)(lambda c, k=k, row=row: add(k, row, c, 1))
+            add(k, row, 2, PARTS - 2)
+        else:
+            pl.loop(0, PARTS // 2)(lambda i, k=k, row=row: add(k, row, 2 * i, 2))
 
     @pl.loop(0, PARTS // 2)
     def _(i):
@@ -176,24 +181,37 @@
 
 
 def late_kernel(row, rows_ref, ids_ref, first_ref, *refs):
-    h_refs = refs[:HALVES]
-    last_ref, init_ref, out_ref, acc = refs[HALVES:]
-    tiles = last_ref.shape[0] // 2
+    pieces = refs[:HALVES]
+    last_ref, init_ref, out_ref, acc, h_ref, sems = refs[HALVES:]
+    count = h_ref.shape[1] // PARTS
+    tiles = count // 2
+
+    def copies(c):
+        here = pl.ds(c * count, count)
+        return [
+            pltpu.make_async_copy(piece.at[here], h_ref.at[q, here], sems.at[c, q])
+            for q, piece in enumerate(pieces)
+        ]
+
+    for c in range(PARTS):
+        for copy in copies(c):
+            copy.start()
     acc[...] = init_ref[...]
-
-    @pl.loop(0, 2)
-    def _(i):
-        share = jnp.zeros((DOCS, BLK), jnp.float32)
-        old = columns_of(h_refs, jnp.maximum(2 * i * tiles - 2, 0), 2)
+    h_refs = [h_ref.at[q] for q in range(HALVES)]
+    share = jnp.zeros((DOCS, BLK), jnp.float32)
+    for c in range(PARTS):
+        for copy in copies(c):
+            copy.wait()
+        old = columns_of(h_refs, max(c * count - 2, 0), 2)
         for t in range(tiles):
-            number = i * tiles + t
+            number = c * tiles + t
             first = line_of(first_ref, 2 * number, row) - number * TILE
             own = columns_of(h_refs, 2 * number, 2)
             terms = counted(pair_products(old, own), first) * last_ref[number]
             share += doc_sums(terms, line_of(ids_ref, 2 * number, row))
             old = own
-        here = pl.ds(pl.multiple_of(rows_ref[row] * DOCS, DOCS), DOCS)
-        acc[here, :] += share
+    here = pl.ds(pl.multiple_of(rows_ref[row] * DOCS, DOCS), DOCS)
+    acc[here, :] += share
 
     sums = jnp.sum(acc[...].T, axis=0, keepdims=True)
     out_ref[...] = jnp.broadcast_to(sums[None], out_ref.shape)
@@ -254,9 +272,13 @@
         grid_spec=pltpu.PrefetchScalarGridSpec(
             num_scalar_prefetch=1,
             grid=(),
-            in_specs=in_vmem(2 + len(hidden) + 2),
+            in_specs=[*in_vmem(2), *in_hbm(len(hidden)), *in_vmem(2)],
             out_specs=pl.BlockSpec(memory_space=pltpu.VMEM),
-            scratch_shapes=[pltpu.VMEM(init.shape, jnp.float32)],
+            scratch_shapes=[
+                pltpu.VMEM(init.shape, jnp.float32),
+                pltpu.VMEM((len(hidden), *hidden[0].shape), hidden[0].dtype),
+                pltpu.SemaphoreType.DMA((PARTS, len(hidden))),
+            ],
         ),
         compiler_params=pltpu.CompilerParams(vmem_limit_bytes=8 * 2**20),
         cost_estimate=pl.CostEstimate(
@@ -282,7 +304,7 @@
 
     for piece in hidden_copies(order[0]):
         piece.start()
-    norms = jnp.sum(norms_ref[...], axis=0)
+    norms = jnp.maximum(jnp.sum(norms_ref[...], axis=0), 0.0)
     clip = bound / jnp.maximum(jnp.sqrt(norms), bound) / nrows
     for k in range(nrows):
         ids = ids_ref[:, k, :] + rows_ref[k] * DOCS
@@ -349,35 +371,41 @@
     )(rows, ids, norms, *pieces, keep_in(pltpu.VMEM, grad))
 
 
-def quarters_kernel(me_ref, ids_ref, *refs):
-    ins, outs = refs[: len(refs) // 2], refs[len(refs) // 2 :]
-    tokens = ins[0].shape[0]
-    for in_ref, out_ref in zip(ins, outs):
-        out_ref[:tokens, :] = in_ref[...]
-        ids = ids_ref[...].astype(jnp.float32).astype(jnp.bfloat16)
-        out_ref[tokens:, :BLK] = jnp.broadcast_to(ids, (16, BLK))
-        out_ref[tokens:, BLK:] = jnp.zeros((16, out_ref.shape[1] - BLK), jnp.bfloat16)
+def quarters_kernel(offsets, me_ref, ids_ref, grad_ref, *refs):
+    out_refs, sems = refs[:-1], refs[-1]
+    tokens = grad_ref.shape[0]
+    part = out_refs[0].shape[1]
+    count = len(offsets)
+    copies = []
+    for n, (offset, out_ref) in enumerate(zip(offsets, out_refs)):
+        begin = pl.multiple_of(lax.rem(me_ref[0] + offset, count) * part, BLK)
+        source = grad_ref.at[:, pl.ds(begin, part)]
+        copies.append(pltpu.make_async_copy(source, out_ref.at[pl.ds(0, tokens)], sems.at[n]))
+    for copy in copies:
+        copy.start()
+    ids = jnp.broadcast_to(ids_ref[...].astype(jnp.float32).astype(jnp.bfloat16), (16, BLK))
+    for out_ref in out_refs:
+        out_ref[tokens:, :BLK] = ids
+        out_ref[tokens:, BLK:] = jnp.zeros((16, part - BLK), jnp.bfloat16)
+    for copy in copies:
+        copy.wait()
 
 
 def quarters(me, offsets, grad, ids):
     tokens, width = grad.shape
     count = len(offsets)
-    part = width // count
-    return pl.pallas_call(
-        quarters_kernel,
-        out_shape=[jax.ShapeDtypeStruct((tokens + 16, part), grad.dtype)] * count,
+    return pl.pallas_call(
+        functools.partial(quarters_kernel, offsets),
+        out_shape=[pltpu.VMEM((tokens + 16, width // count), grad.dtype)] * count,
         grid_spec=pltpu.PrefetchScalarGridSpec(
             num_scalar_prefetch=1,
-            grid=(1,),
-            in_specs=[pl.BlockSpec(ids.shape, lambda i, m: (0, 0))]
-            + [
-                pl.BlockSpec((tokens, part), lambda i, m, o=o: (0, lax.rem(m[0] + o, count)))
-                for o in offsets
-            ],
-            out_specs=[pl.BlockSpec((tokens + 16, part), lambda i, m: (0, 0))] * count,
+            grid=(),
+            in_specs=[*in_vmem(1), *in_hbm(1)],
+            out_specs=in_vmem(count),
+            scratch_shapes=[pltpu.SemaphoreType.DMA((count,))],
         ),
         name="quarters",
-    )(me, ids, *[grad] * count)
+    )(me, ids, keep_in(pltpu.HBM, grad))
 
 
 def columns_kernel(in_ref, *out_refs):
@@ -420,8 +448,7 @@
     me = lax.axis_index("dp")
 
     keep, up, down, across = quarters(me[None], (0, 1, 3, 2), grad_out[0], segment)
-    across = shift(across, 2)
-    received = [shift(up, 1), shift(down, -1), keep, across]
+    received = [shift(up, 1), shift(down, -1), keep, shift(across, 2)]
 
     chunks = columns(hidden[0], blocks)
     received, _ = lax.optimization_barrier((received, chunks))

time: 176 us -> 176 us (level)
  no operation moved by 1% of the time
where the time goes in v8:
time: 176 us; the launch traced here: 175 us
  Pallas kernels  48.9 us (28%)
  blocking collectives  48.4 us (28%)
  waiting for transfers between devices  36 us (20%)
  starting transfers between devices  24 us (14%)
  between operations  13.6 us (8%)
  other arithmetic  3.63 us (2%)
    all_to_all x1, blocking collectives, body(): own = lax.all_to_all(chunk, 'ctx', 0, 0, tiled=True)  32.9 us
    all_to_all x1, waiting for transfers between devices, body(): own = lax.all_to_all(chunk, 'ctx', 0, 0, tiled=True)  20.6 us
    pallas_call x1, Pallas kernels, gram_early(): pl.pallas_call(functools.partial(early_kernel, kinds), out_shape=[jax.Sha...  17.4 us
    all_to_all x1, blocking collectives, body(): norms = lax.all_to_all(partial, ('dp', 'ctx'), 0, 0, tiled=True)  15.5 us
    ppermute x9, starting transfers between devices, shift(): lax.ppermute(block, 'dp', [(i, (i + distance) % size) for i in range(size)])  13.2 us
    pallas_call x2, Pallas kernels, hidden_gram(): pl.pallas_call(functools.partial(hidden_kernel, kinds), out_shape=pltpu.H...  11.4 us
    pallas_call x1, Pallas kernels, product(): pl.pallas_call(functools.partial(product_kernel, nrows, bound), out_shape...  10.5 us
    all_to_all x1, waiting for transfers between devices, body(): ids = lax.all_to_all(ids, 'ctx', 0, 0, tiled=True)  7.75 us
  transfers between devices with their start and end apart: 12, of which 5 were waited for; matrix products, arithmetic and copies ran while one was open for 2% of the time, Pallas kernels for 19%

profile of v8, /device:TPU:1, one launch (start us, length us, event | category | flops | bytes accessed | tf_op | source)
XLA Modules:
  0.0 175.3 jit_solution(13812818124659909847)
XLA Ops:
  6.5 0.0 all-gather.3.cloned.1.call-start
  6.5 1.8 %quarters.1 = (bf16[144,640]{1,0:T(8,128)(2,1)S(1)}, bf16[144,640]{1,0:T(8,128)(2,1)S(1)}, bf16[144,640]{1,0:T(8,128)(2,1)S(1)}, bf16[144,640]{1,0:T(8,128)(2,1)S(1)}) custom-call(s32[1]{0:T(128)} %bitcast.me_ref, s32[1,128]{1,0:T(1,128)} %ids_ref.1, bf16[128,2560]{1,0:T(8,128)(2,1)} %bitcast.13), custom_call_target="tpu_custom_call" | custom-call | tf_op jit(solution)/shard_map/quarters/pallas_call | solution.py:397
  8.4 2.2 %collective-permute-start = (bf16[144,640]{1,0:T(8,128)(2,1)S(1)}, bf16[144,640]{1,0:T(8,128)(2,1)S(1)}, u32[]{:S(2)}, u32[]{:S(2)}) collective-permute-start(bf16[144,640]{1,0:T(8,128)(2,1)S(1)} %get-tuple-element.24), channel_id=1, source_target_pairs={{0,32},{32,64},{64,96},{96,0},{1,33},{33,65},{65,97},{97,1},{2,34}... | collective-permute-start | bytes 552968 | tf_op jit(solution)/shard_map/ppermute | solution.py:433
  10.6 1.5 collective-permute-start.1
  12.1 1.6 collective-permute-start.2
  13.7 3.9 %columns.1 = (bf16[32,128,128]{2,1,0:T(8,128)(2,1)}, bf16[32,128,128]{2,1,0:T(8,128)(2,1)}) custom-call(bf16[128,8192]{1,0:T(8,128)(2,1)} %bitcast.12), custom_call_target="tpu_custom_call" | custom-call | tf_op jit(solution)/shard_map/columns/pallas_call | solution.py:421
  17.6 0.0 copy-start.2
  17.6 0.0 collective-permute-done
  17.6 0.0 collective-permute-done.1
  17.6 3.6 %collective-permute-done.2 = bf16[144,640]{1,0:T(8,128)(2,1)S(1)} collective-permute-done((bf16[144,640]{1,0:T(8,128)(2,1)S(1)}, bf16[144,640]{1,0:T(8,128)(2,1)S(1)}, u32[]{:S(2)}, u32[]{:S(2)}) %collective-permute-start.2) | collective-permute-done | bytes 184352 | tf_op jit(solution)/shard_map/ppermute | solution.py:433
  21.3 0.9 pad_maximum_fusion
  22.2 0.0 all-gather.3.cloned.1.call-update
  22.2 0.0 copy-done.2
  22.3 0.0 copy-start.3
  22.3 32.9 %all_to_all.20.refs_0_.refs_2_.refs_4_ = bf16[32,128,128]{2,1,0:T(8,128)(2,1)S(1)} all-to-all(bf16[32,128,128]{2,1,0:T(8,128)(2,1)S(1)} %copy-done.2), channel_id=1, replica_groups=mesh['dp'=4,'ctx'=32] {'ctx'}, dimensions={0} | all-to-all | bytes 2097152 | tf_op jit(solution)/shard_map/all_to_all | solution.py:464
  55.2 5.3 %all-to-all-start.1 = ((bf16[32,128,128]{2,1,0:T(8,128)(2,1)}), bf16[32,128,128]{2,1,0:T(8,128)(2,1)S(1)}, u32[]{:S(2)}, u32[]{:S(2)}) async-start(bf16[32,128,128]{2,1,0:T(8,128)(2,1)} %get-tuple-element.34), calls=%async_computation.1 | async-start | bytes 2097152 | tf_op jit(solution)/shard_map/all_to_all | solution.py:464
  60.5 0.8 collective-permute-start.3
  61.2 2.0 %collective-permute-start.4 = (bf16[32,128,128]{2,1,0:T(8,128)(2,1)S(1)}, bf16[32,128,128]{2,1,0:T(8,128)(2,1)}, u32[]{:S(2)}, u32[]{:S(2)}) collective-permute-start(bf16[32,128,128]{2,1,0:T(8,128)(2,1)S(1)} %all_to_all.20.refs_0_.refs_2_.refs_4_), channel_id=1, source_target_pairs={{0,96},{32,0},{64,32},{96,64},{1,97},{33,1},{65,33},{97,65},{2,98}... | collective-permute-start | bytes 3145736 | tf_op jit(solution)/shard_map/ppermute | solution.py:433
  63.2 20.6 %all-to-all-done.1.refs_1_.refs_3_.refs_5_ = bf16[32,128,128]{2,1,0:T(8,128)(2,1)S(1)} async-done(((bf16[32,128,128]{2,1,0:T(8,128)(2,1)}), bf16[32,128,128]{2,1,0:T(8,128)(2,1)S(1)}, u32[]{:S(2)}, u32[]{:S(2)}) %all-to-all-start.1) | async-done | bytes 1048608 | tf_op jit(solution)/shard_map/all_to_all | solution.py:464
  83.8 0.0 copy-start
  83.8 0.2 collective-permute-start.6
  84.0 2.5 %collective-permute-start.7 = (bf16[32,128,128]{2,1,0:T(8,128)(2,1)S(1)}, bf16[32,128,128]{2,1,0:T(8,128)(2,1)}, u32[]{:S(2)}, u32[]{:S(2)}) collective-permute-start(bf16[32,128,128]{2,1,0:T(8,128)(2,1)S(1)} %all-to-all-done.1.refs_1_.refs_3_.refs_5_), channel_id=1, source_target_pairs={{0,96},{32,0},{64,32},{96,64},{1,97},{33,1},{65,33},{97,65},{2,98}... | collective-permute-start | bytes 3145736 | tf_op jit(solution)/shard_map/ppermute | solution.py:433
  86.6 0.6 broadcast_in_dim.13
  87.2 5.6 %all-to-all-start.2 = ((s32[32,4,128]{2,1,0:T(4,128)}), s32[32,4,128]{2,1,0:T(4,128)S(1)}, u32[]{:S(2)}, u32[]{:S(2)}) async-start(s32[32,4,128]{2,1,0:T(4,128)} %broadcast_in_dim.13), calls=%async_computation.2 | async-start | bytes 131072 | tf_op jit(solution)/shard_map/all_to_all | solution.py:474
  92.8 0.0 copy-done.3
  92.8 0.0 collective-permute-done.3.refs_0_.refs_2_
  92.8 0.0 collective-permute-done.4.refs_4_.refs_6_.refs_2_
  92.8 0.1 collective-permute-start.5
  92.9 7.7 %all-to-all-done.2.ids_ref = s32[32,4,128]{2,1,0:T(4,128)S(1)} async-done(((s32[32,4,128]{2,1,0:T(4,128)}), s32[32,4,128]{2,1,0:T(4,128)S(1)}, u32[]{:S(2)}, u32[]{:S(2)}) %all-to-all-start.2) | async-done | bytes 65568 | tf_op jit(solution)/shard_map/all_to_all | solution.py:474
  100.6 2.4 %convert_reduce_fusion = s32[32,4]{1,0:T(8,128)S(1)} fusion(s32[32,4,128]{2,0,1:T(8,128)S(1)} %copy.6), kind=kLoop, calls=%fused_computation.1 | loop fusion | flops 1572736 | bytes 66048 | tf_op jit(solution)/shard_map/reduce_sum | solution.py:438
  103.0 0.3 select_reduce_fusion
  103.4 3.5 %hidden_gram.2.refs_8_ = f32[3,16,256,256]{3,2,1,0:T(8,128)} custom-call(s32[32,4,128]{2,1,0:T(4,128)S(1)} %copy.9.first_ref, bf16[32,128,128]{2,1,0:T(8,128)(2,1)S(1)} %all_to_all.20.refs_0_.refs_2_.refs_4_, bf16[32,128,128]{2,1,0:T(8,128)(2,1)S(1)} %all-to-all-done.1.refs_1_.refs_3_.refs_5_, bf16[32,128,128]{2,1,0:T(8,128)(2,1)S(1)} %all_to_all.20.refs_0_.refs_2_.refs_4_, ...), custom_call_target="tpu_custom_call" | custom-call | flops 1073741824 | bytes 6291456 | tf_op jit(solution)/shard_map/hidden_gram/pallas_call | solution.py:100
  106.9 0.0 copy-done
  106.9 1.7 collective-permute-done.6.refs_1_.refs_3_
  108.6 0.0 collective-permute-done.7.refs_5_.refs_7_.refs_3_
  108.6 2.4 %collective-permute-start.8 = (bf16[32,128,128]{2,1,0:T(8,128)(2,1)}, bf16[32,128,128]{2,1,0:T(8,128)(2,1)}, u32[]{:S(2)}, u32[]{:S(2)}) collective-permute-start(bf16[32,128,128]{2,1,0:T(8,128)(2,1)} %collective-permute-done.7.refs_5_.refs_7_.refs_3_), channel_id=1, source_target_pairs={{0,96},{32,0},{64,32},{96,64},{1,97},{33,1},{65,33},{97,65},{2,98}... | collective-permute-start | bytes 3145736 | tf_op jit(solution)/shard_map/ppermute | solution.py:433
  111.0 7.9 %hidden_gram.3.pairs_hbm = f32[3,16,256,256]{3,2,1,0:T(8,128)} custom-call(s32[32,4,128]{2,1,0:T(4,128)S(1)} %copy.9.first_ref, bf16[32,128,128]{2,1,0:T(8,128)(2,1)} %collective-permute-done.3.refs_0_.refs_2_, bf16[32,128,128]{2,1,0:T(8,128)(2,1)} %collective-permute-done.6.refs_1_.refs_3_, ...), custom_call_target="tpu_custom_call", output_to_operand_aliasing={{}: (9, {})} | custom-call | flops 2147483648 | bytes 12582912 | tf_op jit(solution)/shard_map/hidden_gram/pallas_call | solution.py:100
  118.9 2.2 %all-gather.3.cloned.1.call-done = bf16[128,128,640]{2,1,0:T(8,128)(2,1)} async-done(((bf16[4,128,640]{2,1,0:T(8,128)(2,1)}), bf16[128,128,640]{2,1,0:T(8,128)(2,1)}) %all-gather.3.cloned.1.call-update) | async-done | bytes 20971536 | tf_op jit(solution)/shard_map/all_gather | solution.py:457
  121.1 17.4 %gram.1 = (f32[128,128]{1,0:T(8,128)S(1)}, bf16[32,4,128,640]{3,2,1,0:T(8,128)(2,1)S(1)}, f32[16,256,256]{2,1,0:T(8,128)S(1)}) custom-call(s32[4]{0:T(128)S(1)} %compare_select_fusion.rows_ref, s32[32,4,128]{2,1,0:T(4,128)S(1)} %all-to-all-done.2.ids_ref, f32[3,16,256,256]{3,2,1,0:T(8,128)} %hidden_gram.3.pairs_hbm, bf16[32,4,128,640]{3,2,1,0:T(8,128)(2,1)} %bitcast.14), custom_call_target="tpu_custom_call" | custom-call | flops 11274289152 | bytes 20971520 | tf_op jit(solution)/shard_map/gram/pallas_call | solution.py:244
  138.6 0.0 collective-permute-done.5.refs_0_.refs_6_
  138.6 0.0 collective-permute-done.8.refs_1_.refs_7_
  138.6 0.0 copy-start.1
  138.6 3.8 %gram_late.1 = f32[128,1,128]{2,1,0:T(1,128)S(1)} custom-call(s32[4]{0:T(128)S(1)} %compare_select_fusion.rows_ref, s32[32,4,128]{2,1,0:T(4,128)S(1)} %all-to-all-done.2.ids_ref, s32[32,4,128]{2,1,0:T(4,128)S(1)} %copy.9.first_ref, bf16[32,128,128]{2,1,0:T(8,128)(2,1)} %collective-permute-done.5.refs_0_.refs_6_, ...), custom_call_target="tpu_custom_call" | custom-call | flops 1073741824 | bytes 4194304 | tf_op jit(solution)/shard_map/gram_late/pallas_call | solution.py:269
  142.4 15.5 %all_to_all.21.norms_ref = f32[128,1,128]{2,1,0:T(1,128)S(1)} all-to-all(f32[128,1,128]{2,1,0:T(1,128)S(1)} %gram_late.1), channel_id=1, replica_groups=mesh['dp'=4,'ctx'=32] {'dp','ctx'}, dimensions={0} | all-to-all | bytes 131072 | tf_op jit(solution)/shard_map/all_to_all | solution.py:484
  157.9 0.0 copy-done.1
  158.0 10.5 %product.1 = f32[256,640]{1,0:T(8,128)} custom-call(s32[4]{0:T(128)S(1)} %compare_select_fusion.rows_ref, s32[32,4,128]{2,1,0:T(4,128)S(1)} %all-to-all-done.2.ids_ref, f32[128,1,128]{2,1,0:T(1,128)S(1)} %all_to_all.21.norms_ref, bf16[32,128,128]{2,1,0:T(8,128)(2,1)} %collective-permute-done.3.refs_0_.refs_2_, ...), custom_call_target="tpu_custom_call" | custom-call | flops 5368709120 | bytes 29360128 | tf_op jit(solution)/shard_map/product/pallas_call | solution.py:349
  (10 shorter events, 0.2 us)
Async XLA Ops:
  6.5 114.6 %all-gather.3.cloned.1.call-start = ((), (), s32[]{:S(2)}) async-start(), calls=%async_computation.4 | async-start | bytes 21626880 | tf_op jit(solution)/shard_map/all_gather | solution.py:457
  8.4 9.2 %collective-permute-start = (bf16[144,640]{1,0:T(8,128)(2,1)S(1)}, bf16[144,640]{1,0:T(8,128)(2,1)S(1)}, u32[]{:S(2)}, u32[]{:S(2)}) collective-permute-start(bf16[144,640]{1,0:T(8,128)(2,1)S(1)} %get-tuple-element.24), channel_id=1, source_target_pairs={{0,32},{32,64},{64,96},{96,0},{1,33},{33,65},{65,97},{97,1},{2,34}... | collective-permute-start | bytes 552968 | tf_op jit(solution)/shard_map/ppermute | solution.py:433
  10.6 7.0 %collective-permute-start.1 = (bf16[144,640]{1,0:T(8,128)(2,1)S(1)}, bf16[144,640]{1,0:T(8,128)(2,1)S(1)}, u32[]{:S(2)}, u32[]{:S(2)}) collective-permute-start(bf16[144,640]{1,0:T(8,128)(2,1)S(1)} %get-tuple-element.25), channel_id=1, source_target_pairs={{0,96},{32,0},{64,32},{96,64},{1,97},{33,1},{65,33},{97,65},{2,98}... | collective-permute-start | bytes 552968 | tf_op jit(solution)/shard_map/ppermute | solution.py:433
  12.1 9.1 %collective-permute-start.2 = (bf16[144,640]{1,0:T(8,128)(2,1)S(1)}, bf16[144,640]{1,0:T(8,128)(2,1)S(1)}, u32[]{:S(2)}, u32[]{:S(2)}) collective-permute-start(bf16[144,640]{1,0:T(8,128)(2,1)S(1)} %get-tuple-element.27), channel_id=1, source_target_pairs={{0,64},{32,96},{64,0},{96,32},{1,65},{33,97},{65,1},{97,33},{2,66}... | collective-permute-start | bytes 552968 | tf_op jit(solution)/shard_map/ppermute | solution.py:433
  17.6 4.7 %copy-start.2 = (bf16[32,128,128]{2,1,0:T(8,128)(2,1)S(1)}, bf16[32,128,128]{2,1,0:T(8,128)(2,1)}, u32[]{:S(2)}) copy-start(bf16[32,128,128]{2,1,0:T(8,128)(2,1)} %get-tuple-element.28) | copy-start | bytes 3145732
  22.3 70.5 %copy-start.3 = (s32[4]{0:T(128)S(1)}, s32[4]{0:T(128)}, u32[]{:S(2)}) copy-start(s32[4]{0:T(128)} %constant.14.clone) | copy-start | bytes 52
  55.2 28.7 %all-to-all-start.1 = ((bf16[32,128,128]{2,1,0:T(8,128)(2,1)}), bf16[32,128,128]{2,1,0:T(8,128)(2,1)S(1)}, u32[]{:S(2)}, u32[]{:S(2)}) async-start(bf16[32,128,128]{2,1,0:T(8,128)(2,1)} %get-tuple-element.34), calls=%async_computation.1 | async-start | bytes 2097152 | tf_op jit(solution)/shard_map/all_to_all | solution.py:464
  60.5 32.3 %collective-permute-start.3 = (bf16[32,128,128]{2,1,0:T(8,128)(2,1)S(1)}, bf16[32,128,128]{2,1,0:T(8,128)(2,1)}, u32[]{:S(2)}, u32[]{:S(2)}) collective-permute-start(bf16[32,128,128]{2,1,0:T(8,128)(2,1)S(1)} %all_to_all.20.refs_0_.refs_2_.refs_4_), channel_id=1, source_target_pairs={{0,32},{32,64},{64,96},{96,0},{1,33},{33,65},{65,97},{97,1},{2,34}... | collective-permute-start | bytes 3145736 | tf_op jit(solution)/shard_map/ppermute | solution.py:433
  61.2 31.6 %collective-permute-start.4 = (bf16[32,128,128]{2,1,0:T(8,128)(2,1)S(1)}, bf16[32,128,128]{2,1,0:T(8,128)(2,1)}, u32[]{:S(2)}, u32[]{:S(2)}) collective-permute-start(bf16[32,128,128]{2,1,0:T(8,128)(2,1)S(1)} %all_to_all.20.refs_0_.refs_2_.refs_4_), channel_id=1, source_target_pairs={{0,96},{32,0},{64,32},{96,64},{1,97},{33,1},{65,33},{97,65},{2,98}... | collective-permute-start | bytes 3145736 | tf_op jit(solution)/shard_map/ppermute | solution.py:433
  83.8 23.0 %copy-start = (bf16[32,128,128]{2,1,0:T(8,128)(2,1)}, bf16[32,128,128]{2,1,0:T(8,128)(2,1)S(1)}, u32[]{:S(2)}) copy-start(bf16[32,128,128]{2,1,0:T(8,128)(2,1)S(1)} %all-to-all-done.1.refs_1_.refs_3_.refs_5_) | copy-start | bytes 3145732
  83.8 24.8 %collective-permute-start.6 = (bf16[32,128,128]{2,1,0:T(8,128)(2,1)S(1)}, bf16[32,128,128]{2,1,0:T(8,128)(2,1)}, u32[]{:S(2)}, u32[]{:S(2)}) collective-permute-start(bf16[32,128,128]{2,1,0:T(8,128)(2,1)S(1)} %all-to-all-done.1.refs_1_.refs_3_.refs_5_), channel_id=1, source_target_pairs={{0,32},{32,64},{64,96},{96,0},{1,33},{33,65},{65,97},{97,1},{2,34}... | collective-permute-start | bytes 3145736 | tf_op jit(solution)/shard_map/ppermute | solution.py:433
  84.0 24.6 %collective-permute-start.7 = (bf16[32,128,128]{2,1,0:T(8,128)(2,1)S(1)}, bf16[32,128,128]{2,1,0:T(8,128)(2,1)}, u32[]{:S(2)}, u32[]{:S(2)}) collective-permute-start(bf16[32,128,128]{2,1,0:T(8,128)(2,1)S(1)} %all-to-all-done.1.refs_1_.refs_3_.refs_5_), channel_id=1, source_target_pairs={{0,96},{32,0},{64,32},{96,64},{1,97},{33,1},{65,33},{97,65},{2,98}... | collective-permute-start | bytes 3145736 | tf_op jit(solution)/shard_map/ppermute | solution.py:433
  87.2 13.5 %all-to-all-start.2 = ((s32[32,4,128]{2,1,0:T(4,128)}), s32[32,4,128]{2,1,0:T(4,128)S(1)}, u32[]{:S(2)}, u32[]{:S(2)}) async-start(s32[32,4,128]{2,1,0:T(4,128)} %broadcast_in_dim.13), calls=%async_computation.2 | async-start | bytes 131072 | tf_op jit(solution)/shard_map/all_to_all | solution.py:474
  92.8 45.8 %collective-permute-start.5 = (bf16[32,128,128]{2,1,0:T(8,128)(2,1)}, bf16[32,128,128]{2,1,0:T(8,128)(2,1)}, u32[]{:S(2)}, u32[]{:S(2)}) collective-permute-start(bf16[32,128,128]{2,1,0:T(8,128)(2,1)} %collective-permute-done.3.refs_0_.refs_2_), channel_id=1, source_target_pairs={{0,32},{32,64},{64,96},{96,0},{1,33},{33,65},{65,97},{97,1},{2,34}... | collective-permute-start | bytes 3145736 | tf_op jit(solution)/shard_map/ppermute | solution.py:433
  108.6 30.0 %collective-permute-start.8 = (bf16[32,128,128]{2,1,0:T(8,128)(2,1)}, bf16[32,128,128]{2,1,0:T(8,128)(2,1)}, u32[]{:S(2)}, u32[]{:S(2)}) collective-permute-start(bf16[32,128,128]{2,1,0:T(8,128)(2,1)} %collective-permute-done.7.refs_5_.refs_7_.refs_3_), channel_id=1, source_target_pairs={{0,96},{32,0},{64,32},{96,64},{1,97},{33,1},{65,33},{97,65},{2,98}... | collective-permute-start | bytes 3145736 | tf_op jit(solution)/shard_map/ppermute | solution.py:433
  138.6 19.4 %copy-start.1 = (bf16[32,128,128]{2,1,0:T(8,128)(2,1)S(1)}, bf16[32,128,128]{2,1,0:T(8,128)(2,1)}, u32[]{:S(2)}) copy-start(bf16[32,128,128]{2,1,0:T(8,128)(2,1)} %copy-done) | copy-start | bytes 3145732
Sparse Core Ops, SparseCore 0:
  22.4 98.7 all-gather.2

commit v9 on v8

--- a/solution.py
+++ b/solution.py
@@ -348,7 +348,7 @@
     pieces = [piece for row in hidden for piece in row]
     return pl.pallas_call(
         functools.partial(product_kernel, nrows, bound),
-        out_shape=jax.ShapeDtypeStruct((TILE, width), jnp.float32),
+        out_shape=pltpu.HBM((TILE, width), jnp.float32),
         grid_spec=pltpu.PrefetchScalarGridSpec(
             num_scalar_prefetch=1,
             grid=(),
@@ -451,40 +451,44 @@
     received = [shift(up, 1), shift(down, -1), keep, shift(across, 2)]
 
     chunks = columns(hidden[0], blocks)
-    received, _ = lax.optimization_barrier((received, chunks))
-
-    every_grad = jnp.stack([part[:tokens] for part in received])
-    every_grad = lax.all_gather(every_grad, "ctx", axis=0, tiled=False)
-
-    hidden_rows = [[], [], [], []]
-    ready = None
-    for q, chunk in enumerate(chunks):
-        if ready is not None:
-            chunk, ready = lax.optimization_barrier((chunk, ready))
-        own = lax.all_to_all(chunk, "ctx", 0, 0, tiled=True)
-        ready = own
-        below, above = lax.optimization_barrier((shift(own, 1), shift(own, -1)))
-        far = shift(below, 1) if q < HALVES // 2 else shift(above, -1)
-        for row, piece in zip(hidden_rows, (below, above, own, far)):
-            row.append(piece)
-
-    ids = jnp.stack([part[tokens, :BLK] for part in received]).astype(jnp.int32)
-    ids, ready = lax.optimization_barrier((ids, ready))
-    ids = jnp.broadcast_to(ids[None], (blocks, row_count, tokens))
-    ids = lax.all_to_all(ids, "ctx", 0, 0, tiled=True)
-    first = starts(ids)
-
-    rows = lax.rem(me + jnp.array([3, 1, 0, 2], jnp.int32), row_count)
-    kinds = (0, 1, 2)
-    pairs = hidden_gram(first, kinds[2:], hidden_rows[2:3], len(kinds))
-    pairs = hidden_gram(first, kinds[:2], hidden_rows[:2], len(kinds), pairs)
-    early, grads, last = gram_early(rows, ids, kinds, pairs, every_grad)
-    devices = row_count * blocks
-    partial = gram_late(rows, ids, first, 3, hidden_rows[3], last, early, devices)
-    norms = lax.all_to_all(partial, ("dp", "ctx"), 0, 0, tiled=True)
-
-    bound = math.sqrt(tokens * width_hidden * width_grad)
-    return product(rows, ids, norms, hidden_rows, grads, bound)
+    def rest(received, chunks):
+        received, _ = lax.optimization_barrier((received, chunks))
+
+        every_grad = jnp.stack([part[:tokens] for part in received])
+        every_grad = lax.all_gather(every_grad, "ctx", axis=0, tiled=False)
+
+        hidden_rows = [[], [], [], []]
+        ready = None
+        for q, chunk in enumerate(chunks):
+            if ready is not None:
+                chunk, ready = lax.optimization_barrier((chunk, ready))
+            own = lax.all_to_all(chunk, "ctx", 0, 0, tiled=True)
+            ready = own
+            below, above = lax.optimization_barrier((shift(own, 1), shift(own, -1)))
+            far = shift(below, 1) if q < HALVES // 2 else shift(above, -1)
+            for row, piece in zip(hidden_rows, (below, above, own, far)):
+                row.append(piece)
+
+        ids = jnp.stack([part[tokens, :BLK] for part in received]).astype(jnp.int32)
+        ids, ready = lax.optimization_barrier((ids, ready))
+        ids = jnp.broadcast_to(ids[None], (blocks, row_count, tokens))
+        ids = lax.all_to_all(ids, "ctx", 0, 0, tiled=True)
+        first = starts(ids)
+
+        rows = lax.rem(me + jnp.array([3, 1, 0, 2], jnp.int32), row_count)
+        kinds = (0, 1, 2)
+        pairs = hidden_gram(first, kinds[2:], hidden_rows[2:3], len(kinds))
+        pairs = hidden_gram(first, kinds[:2], hidden_rows[:2], len(kinds), pairs)
+        early, grads, last = gram_early(rows, ids, kinds, pairs, every_grad)
+        devices = row_count * blocks
+        partial = gram_late(rows, ids, first, 3, hidden_rows[3], last, early, devices)
+        norms = lax.all_to_all(partial, ("dp", "ctx"), 0, 0, tiled=True)
+
+        bound = math.sqrt(tokens * width_hidden * width_grad)
+        return product(rows, ids, norms, hidden_rows, grads, bound)
+
+    nothing = lambda *_: jnp.zeros((TILE, width_grad // row_count), jnp.float32)
+    return lax.cond(me < row_count, rest, nothing, received, chunks)
 
 
 def solution(mesh):

time: 176 us -> 175 us (level)
  blocking collectives: 48.4 us -> 46.2 us
    all_to_all x2, blocking collectives: 48.4 us -> 46.2 us  [the longest x1 31.1 us: rest(): own = lax.all_to_all(chunk, 'ctx', 0, 0, tiled=True)]
    ppermute x9, waiting for transfers between devices: 5.36 us -> 7.41 us  [shift(): lax.ppermute(block, 'dp', [(i, (i + distance) % size) for i in range(size)])]
where the time goes in v9:
time: 175 us; the launch traced here: 174 us
  Pallas kernels  49.4 us (28%)
  blocking collectives  46.2 us (26%)
  waiting for transfers between devices  36.3 us (21%)
  starting transfers between devices  24.1 us (14%)
  between operations  13.4 us (8%)
  other arithmetic  3.63 us (2%)
    all_to_all x1, blocking collectives, rest(): own = lax.all_to_all(chunk, 'ctx', 0, 0, tiled=True)  31.1 us
    all_to_all x1, waiting for transfers between devices, rest(): own = lax.all_to_all(chunk, 'ctx', 0, 0, tiled=True)  18.9 us
    pallas_call x1, Pallas kernels, gram_early(): pl.pallas_call(functools.partial(early_kernel, kinds), out_shape=[jax.Sha...  17.6 us
    all_to_all x1, blocking collectives, rest(): norms = lax.all_to_all(partial, ('dp', 'ctx'), 0, 0, tiled=True)  15.1 us
    ppermute x9, starting transfers between devices, shift(): lax.ppermute(block, 'dp', [(i, (i + distance) % size) for i in range(size)])  13.2 us
    pallas_call x2, Pallas kernels, hidden_gram(): pl.pallas_call(functools.partial(hidden_kernel, kinds), out_shape=pltpu.H...  11.4 us
    pallas_call x1, Pallas kernels, product(): pl.pallas_call(functools.partial(product_kernel, nrows, bound), out_shape...  11 us
    all_to_all x1, waiting for transfers between devices, rest(): ids = lax.all_to_all(ids, 'ctx', 0, 0, tiled=True)  7.75 us
  transfers between devices with their start and end apart: 12, of which 5 were waited for; matrix products, arithmetic and copies ran while one was open for 2% of the time, Pallas kernels for 19%

profile of v9, /device:TPU:1, one launch (start us, length us, event | category | flops | bytes accessed | tf_op | source)
XLA Modules:
  0.0 174.0 jit_solution(9999038800820798077)
XLA Ops:
  6.5 1.8 %quarters.1 = (bf16[144,640]{1,0:T(8,128)(2,1)S(1)}, bf16[144,640]{1,0:T(8,128)(2,1)S(1)}, bf16[144,640]{1,0:T(8,128)(2,1)S(1)}, bf16[144,640]{1,0:T(8,128)(2,1)S(1)}) custom-call(s32[1]{0:T(128)} %bitcast.5.me_ref, s32[1,128]{1,0:T(1,128)} %ids_ref.1, bf16[128,2560]{1,0:T(8,128)(2,1)} %bitcast.13), custom_call_target="tpu_custom_call" | custom-call | tf_op jit(solution)/shard_map/quarters/pallas_call | solution.py:397
  8.4 2.2 %collective-permute-start.6 = (bf16[144,640]{1,0:T(8,128)(2,1)S(1)}, bf16[144,640]{1,0:T(8,128)(2,1)S(1)}, u32[]{:S(2)}, u32[]{:S(2)}) collective-permute-start(bf16[144,640]{1,0:T(8,128)(2,1)S(1)} %get-tuple-element.51), channel_id=1, source_target_pairs={{0,32},{32,64},{64,96},{96,0},{1,33},{33,65},{65,97},{97,1},{2,34}... | collective-permute-start | bytes 552968 | tf_op jit(solution)/shard_map/ppermute | solution.py:433
  10.6 1.5 collective-permute-start.7
  12.1 1.6 collective-permute-start.8
  13.7 3.7 %columns.1 = (bf16[32,128,128]{2,1,0:T(8,128)(2,1)S(1)}, bf16[32,128,128]{2,1,0:T(8,128)(2,1)}) custom-call(bf16[128,8192]{1,0:T(8,128)(2,1)} %bitcast.12), custom_call_target="tpu_custom_call" | custom-call | tf_op jit(solution)/shard_map/columns/pallas_call | solution.py:421
  17.4 0.0 collective-permute-done.6
  17.4 0.0 collective-permute-done.7
  17.4 3.8 %collective-permute-done.8 = bf16[144,640]{1,0:T(8,128)(2,1)S(1)} collective-permute-done((bf16[144,640]{1,0:T(8,128)(2,1)S(1)}, bf16[144,640]{1,0:T(8,128)(2,1)S(1)}, u32[]{:S(2)}, u32[]{:S(2)}) %collective-permute-start.8) | collective-permute-done | bytes 184352 | tf_op jit(solution)/shard_map/ppermute | solution.py:433
  21.2 145.9 %conditional.1 = (f32[256,640]{1,0:T(8,128)}) conditional(s32[]{:T(128)} %convert_element_type.9, () %tuple.16, (s32[]{:T(128)}, (), bf16[144,640]{1,0:T(8,128)(2,1)S(1)}, bf16[144,640]{1,0:T(8,128)(2,1)S(1)}, bf16[144,640]{1,0:T(8,128)(2,1)S(1)}, /*index=5*/bf16[144,640]{1,0:T(8,128)(2,1)S(1)}, bf16[32,128,128]{2,1,0:T(8,128)(2,1)S(1)}, ...), branch_computations={%region_0.0_spmd, %region_1.4_spmd} | conditional | flops 20942082048 | bytes 180560416 | solution.py:491
  21.2 0.0 all-gather.3.cloned.1.call-start
  21.3 0.9 pad_maximum_fusion
  22.2 0.0 all-gather.3.cloned.1.call-update
  22.2 0.0 copy-start.2
  22.3 31.1 %all_to_all.16.refs_0_.refs_2_.refs_4_ = bf16[32,128,128]{2,1,0:T(8,128)(2,1)S(1)} all-to-all(bf16[32,128,128]{2,1,0:T(8,128)(2,1)S(1)} %get-tuple-element.30), channel_id=1, replica_groups=mesh['dp'=4,'ctx'=32] {'ctx'}, dimensions={0} | all-to-all | bytes 2097152 | tf_op jit(solution)/shard_map/cond/branch_1_fun/all_to_all | solution.py:465
  53.3 5.4 %all-to-all-start.1 = ((bf16[32,128,128]{2,1,0:T(8,128)(2,1)}), bf16[32,128,128]{2,1,0:T(8,128)(2,1)S(1)}, u32[]{:S(2)}, u32[]{:S(2)}) async-start(bf16[32,128,128]{2,1,0:T(8,128)(2,1)} %get-tuple-element.36), calls=%async_computation.1 | async-start | bytes 2097152 | tf_op jit(solution)/shard_map/cond/branch_1_fun/all_to_all | solution.py:465
  58.7 0.6 collective-permute-start
  59.3 2.1 %collective-permute-start.1 = (bf16[32,128,128]{2,1,0:T(8,128)(2,1)S(1)}, bf16[32,128,128]{2,1,0:T(8,128)(2,1)}, u32[]{:S(2)}, u32[]{:S(2)}) collective-permute-start(bf16[32,128,128]{2,1,0:T(8,128)(2,1)S(1)} %all_to_all.16.refs_0_.refs_2_.refs_4_), channel_id=1, source_target_pairs={{0,96},{32,0},{64,32},{96,64},{1,97},{33,1},{65,33},{97,65},{2,98}... | collective-permute-start | bytes 3145736 | tf_op jit(solution)/shard_map/cond/branch_1_fun/ppermute | solution.py:433
  61.5 18.9 %all-to-all-done.1.refs_1_.refs_3_.refs_5_ = bf16[32,128,128]{2,1,0:T(8,128)(2,1)S(1)} async-done(((bf16[32,128,128]{2,1,0:T(8,128)(2,1)}), bf16[32,128,128]{2,1,0:T(8,128)(2,1)S(1)}, u32[]{:S(2)}, u32[]{:S(2)}) %all-to-all-start.1) | async-done | bytes 1048608 | tf_op jit(solution)/shard_map/cond/branch_1_fun/all_to_all | solution.py:465
  80.3 0.0 copy-start
  80.3 0.0 collective-permute-start.3
  80.3 2.7 %collective-permute-start.4 = (bf16[32,128,128]{2,1,0:T(8,128)(2,1)S(1)}, bf16[32,128,128]{2,1,0:T(8,128)(2,1)}, u32[]{:S(2)}, u32[]{:S(2)}) collective-permute-start(bf16[32,128,128]{2,1,0:T(8,128)(2,1)S(1)} %all-to-all-done.1.refs_1_.refs_3_.refs_5_), channel_id=1, source_target_pairs={{0,96},{32,0},{64,32},{96,64},{1,97},{33,1},{65,33},{97,65},{2,98}... | collective-permute-start | bytes 3145736 | tf_op jit(solution)/shard_map/cond/branch_1_fun/ppermute | solution.py:433
  83.0 0.6 broadcast_in_dim.8
  83.7 5.6 %all-to-all-start.2 = ((s32[32,4,128]{2,1,0:T(4,128)}), s32[32,4,128]{2,1,0:T(4,128)S(1)}, u32[]{:S(2)}, u32[]{:S(2)}) async-start(s32[32,4,128]{2,1,0:T(4,128)} %broadcast_in_dim.8), calls=%async_computation.2 | async-start | bytes 131072 | tf_op jit(solution)/shard_map/cond/branch_1_fun/all_to_all | solution.py:475
  89.2 0.0 copy-done.2
  89.3 0.0 collective-permute-done.refs_0_.refs_2_
  89.3 0.0 collective-permute-done.1.refs_4_.refs_6_.refs_2_
  89.3 0.1 collective-permute-start.2
  89.4 7.8 %all-to-all-done.2.ids_ref = s32[32,4,128]{2,1,0:T(4,128)S(1)} async-done(((s32[32,4,128]{2,1,0:T(4,128)}), s32[32,4,128]{2,1,0:T(4,128)S(1)}, u32[]{:S(2)}, u32[]{:S(2)}) %all-to-all-start.2) | async-done | bytes 65568 | tf_op jit(solution)/shard_map/cond/branch_1_fun/all_to_all | solution.py:475
  97.1 2.4 %convert_reduce_fusion = s32[32,4]{1,0:T(8,128)S(1)} fusion(s32[32,4,128]{2,0,1:T(8,128)S(1)} %copy.9), kind=kLoop, calls=%fused_computation.1 | loop fusion | flops 1572736 | bytes 66048 | tf_op jit(solution)/shard_map/cond/branch_1_fun/reduce_sum | solution.py:438
  99.5 0.3 select_reduce_fusion
  99.9 3.5 %hidden_gram.2.refs_8_ = f32[3,16,256,256]{3,2,1,0:T(8,128)} custom-call(s32[32,4,128]{2,1,0:T(4,128)S(1)} %copy.12.first_ref, bf16[32,128,128]{2,1,0:T(8,128)(2,1)S(1)} %all_to_all.16.refs_0_.refs_2_.refs_4_, bf16[32,128,128]{2,1,0:T(8,128)(2,1)S(1)} %all-to-all-done.1.refs_1_.refs_3_.refs_5_, bf16[32,128,128]{2,1,0:T(8,128)(2,1)S(1)} %all_to_all.16.refs_0_.refs_2_.refs_4_, ...), custom_call_target="tpu_custom_call" | custom-call | flops 1073741824 | bytes 6291456 | tf_op jit(solution)/shard_map/cond/branch_1_fun/hidden_gram/pallas_call | solution.py:100
  103.3 0.0 copy-done
  103.3 3.6 %collective-permute-done.3.refs_1_.refs_3_ = bf16[32,128,128]{2,1,0:T(8,128)(2,1)} collective-permute-done((bf16[32,128,128]{2,1,0:T(8,128)(2,1)S(1)}, bf16[32,128,128]{2,1,0:T(8,128)(2,1)}, u32[]{:S(2)}, u32[]{:S(2)}) %collective-permute-start.3) | collective-permute-done | bytes 1048608 | tf_op jit(solution)/shard_map/cond/branch_1_fun/ppermute | solution.py:433
  107.0 0.0 collective-permute-done.4.refs_5_.refs_7_.refs_3_
  107.0 2.4 %collective-permute-start.5 = (bf16[32,128,128]{2,1,0:T(8,128)(2,1)}, bf16[32,128,128]{2,1,0:T(8,128)(2,1)}, u32[]{:S(2)}, u32[]{:S(2)}) collective-permute-start(bf16[32,128,128]{2,1,0:T(8,128)(2,1)} %collective-permute-done.4.refs_5_.refs_7_.refs_3_), channel_id=1, source_target_pairs={{0,96},{32,0},{64,32},{96,64},{1,97},{33,1},{65,33},{97,65},{2,98}... | collective-permute-start | bytes 3145736 | tf_op jit(solution)/shard_map/cond/branch_1_fun/ppermute | solution.py:433
  109.3 7.9 %hidden_gram.3.pairs_hbm = f32[3,16,256,256]{3,2,1,0:T(8,128)} custom-call(s32[32,4,128]{2,1,0:T(4,128)S(1)} %copy.12.first_ref, bf16[32,128,128]{2,1,0:T(8,128)(2,1)} %collective-permute-done.refs_0_.refs_2_, bf16[32,128,128]{2,1,0:T(8,128)(2,1)} %collective-permute-done.3.refs_1_.refs_3_, ...), custom_call_target="tpu_custom_call", output_to_operand_aliasing={{}: (9, {})} | custom-call | flops 2147483648 | bytes 12582912 | tf_op jit(solution)/shard_map/cond/branch_1_fun/hidden_gram/pallas_call | solution.py:100
  117.2 2.3 %all-gather.3.cloned.1.call-done = bf16[128,128,640]{2,1,0:T(8,128)(2,1)} async-done(((bf16[4,128,640]{2,1,0:T(8,128)(2,1)}), bf16[128,128,640]{2,1,0:T(8,128)(2,1)}) %all-gather.3.cloned.1.call-update) | async-done | bytes 20971536 | tf_op jit(solution)/shard_map/cond/branch_1_fun/all_gather | solution.py:458
  119.5 17.6 %gram.1 = (f32[128,128]{1,0:T(8,128)S(1)}, bf16[32,4,128,640]{3,2,1,0:T(8,128)(2,1)S(1)}, f32[16,256,256]{2,1,0:T(8,128)S(1)}) custom-call(s32[4]{0:T(128)S(1)} %compare_select_fusion.rows_ref, s32[32,4,128]{2,1,0:T(4,128)S(1)} %all-to-all-done.2.ids_ref, f32[3,16,256,256]{3,2,1,0:T(8,128)} %hidden_gram.3.pairs_hbm, bf16[32,4,128,640]{3,2,1,0:T(8,128)(2,1)} %bitcast.14), custom_call_target="tpu_custom_call" | custom-call | flops 11274289152 | bytes 20971520 | tf_op jit(solution)/shard_map/cond/branch_1_fun/gram/pallas_call | solution.py:244
  137.1 0.0 collective-permute-done.2.refs_0_.refs_6_
  137.1 0.0 collective-permute-done.5.refs_1_.refs_7_
  137.1 0.0 copy-start.1
  137.1 3.9 %gram_late.1 = f32[128,1,128]{2,1,0:T(1,128)S(1)} custom-call(s32[4]{0:T(128)S(1)} %compare_select_fusion.rows_ref, s32[32,4,128]{2,1,0:T(4,128)S(1)} %all-to-all-done.2.ids_ref, s32[32,4,128]{2,1,0:T(4,128)S(1)} %copy.12.first_ref, bf16[32,128,128]{2,1,0:T(8,128)(2,1)} %collective-permute-done.2.refs_0_.refs_6_, ...), custom_call_target="tpu_custom_call" | custom-call | flops 1073741824 | bytes 4194304 | tf_op jit(solution)/shard_map/cond/branch_1_fun/gram_late/pallas_call | solution.py:269
  141.0 15.1 %all_to_all.17.norms_ref = f32[128,1,128]{2,1,0:T(1,128)S(1)} all-to-all(f32[128,1,128]{2,1,0:T(1,128)S(1)} %gram_late.1), channel_id=1, replica_groups=mesh['dp'=4,'ctx'=32] {'dp','ctx'}, dimensions={0} | all-to-all | bytes 131072 | tf_op jit(solution)/shard_map/cond/branch_1_fun/all_to_all | solution.py:485
  156.1 0.0 copy-done.1
  156.1 11.0 %product.1 = f32[256,640]{1,0:T(8,128)} custom-call(s32[4]{0:T(128)S(1)} %compare_select_fusion.rows_ref, s32[32,4,128]{2,1,0:T(4,128)S(1)} %all-to-all-done.2.ids_ref, f32[128,1,128]{2,1,0:T(1,128)S(1)} %all_to_all.17.norms_ref, bf16[32,128,128]{2,1,0:T(8,128)(2,1)} %collective-permute-done.refs_0_.refs_2_, ...), custom_call_target="tpu_custom_call" | custom-call | flops 5368709120 | bytes 29360128 | tf_op jit(solution)/shard_map/cond/branch_1_fun/product/pallas_call | solution.py:349
  (10 shorter events, 0.2 us)
Async XLA Ops:
  8.4 9.0 %collective-permute-start.6 = (bf16[144,640]{1,0:T(8,128)(2,1)S(1)}, bf16[144,640]{1,0:T(8,128)(2,1)S(1)}, u32[]{:S(2)}, u32[]{:S(2)}) collective-permute-start(bf16[144,640]{1,0:T(8,128)(2,1)S(1)} %get-tuple-element.51), channel_id=1, source_target_pairs={{0,32},{32,64},{64,96},{96,0},{1,33},{33,65},{65,97},{97,1},{2,34}... | collective-permute-start | bytes 552968 | tf_op jit(solution)/shard_map/ppermute | solution.py:433
  10.6 6.8 %collective-permute-start.7 = (bf16[144,640]{1,0:T(8,128)(2,1)S(1)}, bf16[144,640]{1,0:T(8,128)(2,1)S(1)}, u32[]{:S(2)}, u32[]{:S(2)}) collective-permute-start(bf16[144,640]{1,0:T(8,128)(2,1)S(1)} %get-tuple-element.52), channel_id=1, source_target_pairs={{0,96},{32,0},{64,32},{96,64},{1,97},{33,1},{65,33},{97,65},{2,98}... | collective-permute-start | bytes 552968 | tf_op jit(solution)/shard_map/ppermute | solution.py:433
  12.1 9.1 %collective-permute-start.8 = (bf16[144,640]{1,0:T(8,128)(2,1)S(1)}, bf16[144,640]{1,0:T(8,128)(2,1)S(1)}, u32[]{:S(2)}, u32[]{:S(2)}) collective-permute-start(bf16[144,640]{1,0:T(8,128)(2,1)S(1)} %get-tuple-element.54), channel_id=1, source_target_pairs={{0,64},{32,96},{64,0},{96,32},{1,65},{33,97},{65,1},{97,33},{2,66}... | collective-permute-start | bytes 552968 | tf_op jit(solution)/shard_map/ppermute | solution.py:433
  21.2 98.3 %all-gather.3.cloned.1.call-start = ((), (), s32[]{:S(2)}) async-start(), calls=%async_computation.4 | async-start | bytes 21626880 | tf_op jit(solution)/shard_map/cond/branch_1_fun/all_gather | solution.py:458
  22.2 67.0 %copy-start.2 = (s32[4]{0:T(128)S(1)}, s32[4]{0:T(128)}, u32[]{:S(2)}) copy-start(s32[4]{0:T(128)} %constant.18.clone.1) | copy-start | bytes 52 | tf_op jit(solution)/shard_map/cond
  53.3 27.0 %all-to-all-start.1 = ((bf16[32,128,128]{2,1,0:T(8,128)(2,1)}), bf16[32,128,128]{2,1,0:T(8,128)(2,1)S(1)}, u32[]{:S(2)}, u32[]{:S(2)}) async-start(bf16[32,128,128]{2,1,0:T(8,128)(2,1)} %get-tuple-element.36), calls=%async_computation.1 | async-start | bytes 2097152 | tf_op jit(solution)/shard_map/cond/branch_1_fun/all_to_all | solution.py:465
  58.7 30.6 %collective-permute-start = (bf16[32,128,128]{2,1,0:T(8,128)(2,1)S(1)}, bf16[32,128,128]{2,1,0:T(8,128)(2,1)}, u32[]{:S(2)}, u32[]{:S(2)}) collective-permute-start(bf16[32,128,128]{2,1,0:T(8,128)(2,1)S(1)} %all_to_all.16.refs_0_.refs_2_.refs_4_), channel_id=1, source_target_pairs={{0,32},{32,64},{64,96},{96,0},{1,33},{33,65},{65,97},{97,1},{2,34}... | collective-permute-start | bytes 3145736 | tf_op jit(solution)/shard_map/cond/branch_1_fun/ppermute | solution.py:433
  59.3 30.0 %collective-permute-start.1 = (bf16[32,128,128]{2,1,0:T(8,128)(2,1)S(1)}, bf16[32,128,128]{2,1,0:T(8,128)(2,1)}, u32[]{:S(2)}, u32[]{:S(2)}) collective-permute-start(bf16[32,128,128]{2,1,0:T(8,128)(2,1)S(1)} %all_to_all.16.refs_0_.refs_2_.refs_4_), channel_id=1, source_target_pairs={{0,96},{32,0},{64,32},{96,64},{1,97},{33,1},{65,33},{97,65},{2,98}... | collective-permute-start | bytes 3145736 | tf_op jit(solution)/shard_map/cond/branch_1_fun/ppermute | solution.py:433
  80.3 23.0 %copy-start = (bf16[32,128,128]{2,1,0:T(8,128)(2,1)}, bf16[32,128,128]{2,1,0:T(8,128)(2,1)S(1)}, u32[]{:S(2)}) copy-start(bf16[32,128,128]{2,1,0:T(8,128)(2,1)S(1)} %all-to-all-done.1.refs_1_.refs_3_.refs_5_) | copy-start | bytes 3145732 | tf_op jit(solution)/shard_map/cond
  80.3 26.6 %collective-permute-start.3 = (bf16[32,128,128]{2,1,0:T(8,128)(2,1)S(1)}, bf16[32,128,128]{2,1,0:T(8,128)(2,1)}, u32[]{:S(2)}, u32[]{:S(2)}) collective-permute-start(bf16[32,128,128]{2,1,0:T(8,128)(2,1)S(1)} %all-to-all-done.1.refs_1_.refs_3_.refs_5_), channel_id=1, source_target_pairs={{0,32},{32,64},{64,96},{96,0},{1,33},{33,65},{65,97},{97,1},{2,34}... | collective-permute-start | bytes 3145736 | tf_op jit(solution)/shard_map/cond/branch_1_fun/ppermute | solution.py:433
  80.3 26.6 %collective-permute-start.4 = (bf16[32,128,128]{2,1,0:T(8,128)(2,1)S(1)}, bf16[32,128,128]{2,1,0:T(8,128)(2,1)}, u32[]{:S(2)}, u32[]{:S(2)}) collective-permute-start(bf16[32,128,128]{2,1,0:T(8,128)(2,1)S(1)} %all-to-all-done.1.refs_1_.refs_3_.refs_5_), channel_id=1, source_target_pairs={{0,96},{32,0},{64,32},{96,64},{1,97},{33,1},{65,33},{97,65},{2,98}... | collective-permute-start | bytes 3145736 | tf_op jit(solution)/shard_map/cond/branch_1_fun/ppermute | solution.py:433
  83.7 13.5 %all-to-all-start.2 = ((s32[32,4,128]{2,1,0:T(4,128)}), s32[32,4,128]{2,1,0:T(4,128)S(1)}, u32[]{:S(2)}, u32[]{:S(2)}) async-start(s32[32,4,128]{2,1,0:T(4,128)} %broadcast_in_dim.8), calls=%async_computation.2 | async-start | bytes 131072 | tf_op jit(solution)/shard_map/cond/branch_1_fun/all_to_all | solution.py:475
  89.3 47.8 %collective-permute-start.2 = (bf16[32,128,128]{2,1,0:T(8,128)(2,1)}, bf16[32,128,128]{2,1,0:T(8,128)(2,1)}, u32[]{:S(2)}, u32[]{:S(2)}) collective-permute-start(bf16[32,128,128]{2,1,0:T(8,128)(2,1)} %collective-permute-done.refs_0_.refs_2_), channel_id=1, source_target_pairs={{0,32},{32,64},{64,96},{96,0},{1,33},{33,65},{65,97},{97,1},{2,34}... | collective-permute-start | bytes 3145736 | tf_op jit(solution)/shard_map/cond/branch_1_fun/ppermute | solution.py:433
  107.0 30.1 %collective-permute-start.5 = (bf16[32,128,128]{2,1,0:T(8,128)(2,1)}, bf16[32,128,128]{2,1,0:T(8,128)(2,1)}, u32[]{:S(2)}, u32[]{:S(2)}) collective-permute-start(bf16[32,128,128]{2,1,0:T(8,128)(2,1)} %collective-permute-done.4.refs_5_.refs_7_.refs_3_), channel_id=1, source_target_pairs={{0,96},{32,0},{64,32},{96,64},{1,97},{33,1},{65,33},{97,65},{2,98}... | collective-permute-start | bytes 3145736 | tf_op jit(solution)/shard_map/cond/branch_1_fun/ppermute | solution.py:433
  137.1 19.0 %copy-start.1 = (bf16[32,128,128]{2,1,0:T(8,128)(2,1)S(1)}, bf16[32,128,128]{2,1,0:T(8,128)(2,1)}, u32[]{:S(2)}) copy-start(bf16[32,128,128]{2,1,0:T(8,128)(2,1)} %copy-done) | copy-start | bytes 3145732 | tf_op jit(solution)/shard_map/cond
Sparse Core Ops, SparseCore 0:
  24.3 95.1 all-gather.2

commit v10 on v9

--- a/solution.py
+++ b/solution.py
@@ -114,7 +114,7 @@
     )(*operands)
 
 
-def early_kernel(kinds, rows_ref, ids_ref, pairs_hbm, g_hbm, out_ref, g_ref, last_ref, pairs_ref, pair_sems, sems):
+def early_kernel(kinds, rows_ref, ids_ref, first_ref, pairs_hbm, g_hbm, out_ref, g_ref, last_ref, pairs_ref, pair_sems, sems):
     nrows = len(kinds)
     blocks, every = g_ref.shape[:2]
     count = blocks // PARTS
@@ -176,11 +176,13 @@
         old = flat(g_ref[pl.ds(jnp.maximum(begin - 2, 0), 2), nrows])
         for t in range(2 * tiles):
             own = flat(g_ref[pl.ds(begin + 2 * t, 2), nrows])
-            last_ref[2 * i * tiles + t] = pair_products(old, own)
+            number = 2 * i * tiles + t
+            first = line_of(first_ref, 2 * number, nrows) - number * TILE
+            last_ref[number] = counted(pair_products(old, own), first)
             old = own
 
 
-def late_kernel(row, rows_ref, ids_ref, first_ref, *refs):
+def late_kernel(row, rows_ref, ids_ref, *refs):
     pieces = refs[:HALVES]
     last_ref, init_ref, out_ref, acc, h_ref, sems = refs[HALVES:]
     count = h_ref.shape[1] // PARTS
@@ -205,9 +207,8 @@
         old = columns_of(h_refs, max(c * count - 2, 0), 2)
         for t in range(tiles):
             number = c * tiles + t
-            first = line_of(first_ref, 2 * number, row) - number * TILE
             own = columns_of(h_refs, 2 * number, 2)
-            terms = counted(pair_products(old, own), first) * last_ref[number]
+            terms = pair_products(old, own) * last_ref[number]
             share += doc_sums(terms, line_of(ids_ref, 2 * number, row))
             old = own
     here = pl.ds(pl.multiple_of(rows_ref[row] * DOCS, DOCS), DOCS)
@@ -238,7 +239,7 @@
     )
 
 
-def gram_early(rows, ids, kinds, pairs, grad):
+def gram_early(rows, ids, first, kinds, pairs, grad):
     every = grad.shape[1]
     tiles = pairs.shape[1] // PARTS
     return pl.pallas_call(
@@ -251,7 +252,7 @@
         grid_spec=pltpu.PrefetchScalarGridSpec(
             num_scalar_prefetch=1,
             grid=(),
-            in_specs=[*in_vmem(1), *in_hbm(2)],
+            in_specs=[*in_vmem(2), *in_hbm(2)],
             out_specs=in_vmem(3),
             scratch_shapes=[
                 pltpu.VMEM((AHEAD + 2, tiles, TILE, TILE), jnp.float32),
@@ -262,17 +263,17 @@
         compiler_params=pltpu.CompilerParams(vmem_limit_bytes=12 * 2**20),
         cost_estimate=gram_cost(len(kinds), grad),
         name="gram",
-    )(rows, ids, keep_in(pltpu.HBM, pairs), keep_in(pltpu.HBM, grad))
-
-
-def gram_late(rows, ids, first, row, hidden, last, init, devices):
+    )(rows, ids, first, keep_in(pltpu.HBM, pairs), keep_in(pltpu.HBM, grad))
+
+
+def gram_late(rows, ids, row, hidden, last, init, devices):
     return pl.pallas_call(
         functools.partial(late_kernel, row),
         out_shape=jax.ShapeDtypeStruct((devices, 1, BLK), jnp.float32),
         grid_spec=pltpu.PrefetchScalarGridSpec(
             num_scalar_prefetch=1,
             grid=(),
-            in_specs=[*in_vmem(2), *in_hbm(len(hidden)), *in_vmem(2)],
+            in_specs=[*in_vmem(1), *in_hbm(len(hidden)), *in_vmem(2)],
             out_specs=pl.BlockSpec(memory_space=pltpu.VMEM),
             scratch_shapes=[
                 pltpu.VMEM(init.shape, jnp.float32),
@@ -285,7 +286,7 @@
             flops=2 * 2 * last.size * TILE, bytes_accessed=last.size * 4, transcendentals=0
         ),
         name="gram_late",
-    )(rows, ids, first, *hidden, keep_in(pltpu.VMEM, last), init)
+    )(rows, ids, *hidden, keep_in(pltpu.VMEM, last), init)
 
 
 def product_kernel(nrows, bound, rows_ref, ids_ref, norms_ref, *refs):
@@ -479,9 +480,9 @@
         kinds = (0, 1, 2)
         pairs = hidden_gram(first, kinds[2:], hidden_rows[2:3], len(kinds))
         pairs = hidden_gram(first, kinds[:2], hidden_rows[:2], len(kinds), pairs)
-        early, grads, last = gram_early(rows, ids, kinds, pairs, every_grad)
+        early, grads, last = gram_early(rows, ids, first, kinds, pairs, every_grad)
         devices = row_count * blocks
-        partial = gram_late(rows, ids, first, 3, hidden_rows[3], last, early, devices)
+        partial = gram_late(rows, ids, 3, hidden_rows[3], last, early, devices)
         norms = lax.all_to_all(partial, ("dp", "ctx"), 0, 0, tiled=True)
 
         bound = math.sqrt(tokens * width_hidden * width_grad)

time: 175 us -> 174 us (level)
  no operation moved by 1% of the time
where the time goes in v10:
time: 174 us
  Pallas kernels  49.4 us (28%)
  blocking collectives  46.1 us (26%)
  waiting for transfers between devices  36.3 us (21%)
  starting transfers between devices  24.1 us (14%)
  between operations  13.4 us (8%)
  other arithmetic  3.63 us (2%)
    all_to_all x1, blocking collectives, rest(): own = lax.all_to_all(chunk, 'ctx', 0, 0, tiled=True)  31.1 us
    all_to_all x1, waiting for transfers between devices, rest(): own = lax.all_to_all(chunk, 'ctx', 0, 0, tiled=True)  18.9 us
    pallas_call x1, Pallas kernels, gram_early(): pl.pallas_call(functools.partial(early_kernel, kinds), out_shape=[jax.Sha...  17.6 us
    all_to_all x1, blocking collectives, rest(): norms = lax.all_to_all(partial, ('dp', 'ctx'), 0, 0, tiled=True)  15.1 us
    ppermute x9, starting transfers between devices, shift(): lax.ppermute(block, 'dp', [(i, (i + distance) % size) for i in range(size)])  13.2 us
    pallas_call x2, Pallas kernels, hidden_gram(): pl.pallas_call(functools.partial(hidden_kernel, kinds), out_shape=pltpu.H...  11.4 us
    pallas_call x1, Pallas kernels, product(): pl.pallas_call(functools.partial(product_kernel, nrows, bound), out_shape...  11 us
    all_to_all x1, waiting for transfers between devices, rest(): ids = lax.all_to_all(ids, 'ctx', 0, 0, tiled=True)  7.75 us
  transfers between devices with their start and end apart: 12, of which 5 were waited for; matrix products, arithmetic and copies ran while one was open for 2% of the time, Pallas kernels for 19%

profile of v10, /device:TPU:1, one launch (start us, length us, event | category | flops | bytes accessed | tf_op | source)
XLA Modules:
  0.0 173.9 jit_solution(6831807506968607484)
XLA Ops:
  6.5 1.8 %quarters.1 = (bf16[144,640]{1,0:T(8,128)(2,1)S(1)}, bf16[144,640]{1,0:T(8,128)(2,1)S(1)}, bf16[144,640]{1,0:T(8,128)(2,1)S(1)}, bf16[144,640]{1,0:T(8,128)(2,1)S(1)}) custom-call(s32[1]{0:T(128)} %bitcast.5.me_ref, s32[1,128]{1,0:T(1,128)} %ids_ref.1, bf16[128,2560]{1,0:T(8,128)(2,1)} %bitcast.13), custom_call_target="tpu_custom_call" | custom-call | tf_op jit(solution)/shard_map/quarters/pallas_call | solution.py:398
  8.4 2.2 %collective-permute-start.6 = (bf16[144,640]{1,0:T(8,128)(2,1)S(1)}, bf16[144,640]{1,0:T(8,128)(2,1)S(1)}, u32[]{:S(2)}, u32[]{:S(2)}) collective-permute-start(bf16[144,640]{1,0:T(8,128)(2,1)S(1)} %get-tuple-element.51), channel_id=1, source_target_pairs={{0,32},{32,64},{64,96},{96,0},{1,33},{33,65},{65,97},{97,1},{2,34}... | collective-permute-start | bytes 552968 | tf_op jit(solution)/shard_map/ppermute | solution.py:434
  10.6 1.5 collective-permute-start.7
  12.1 1.6 collective-permute-start.8
  13.7 3.7 %columns.1 = (bf16[32,128,128]{2,1,0:T(8,128)(2,1)S(1)}, bf16[32,128,128]{2,1,0:T(8,128)(2,1)}) custom-call(bf16[128,8192]{1,0:T(8,128)(2,1)} %bitcast.12), custom_call_target="tpu_custom_call" | custom-call | tf_op jit(solution)/shard_map/columns/pallas_call | solution.py:422
  17.4 0.0 collective-permute-done.6
  17.4 0.0 collective-permute-done.7
  17.4 3.8 %collective-permute-done.8 = bf16[144,640]{1,0:T(8,128)(2,1)S(1)} collective-permute-done((bf16[144,640]{1,0:T(8,128)(2,1)S(1)}, bf16[144,640]{1,0:T(8,128)(2,1)S(1)}, u32[]{:S(2)}, u32[]{:S(2)}) %collective-permute-start.8) | collective-permute-done | bytes 184352 | tf_op jit(solution)/shard_map/ppermute | solution.py:434
  21.2 145.8 %conditional.1 = (f32[256,640]{1,0:T(8,128)}) conditional(s32[]{:T(128)} %convert_element_type.9, () %tuple.16, (s32[]{:T(128)}, (), bf16[144,640]{1,0:T(8,128)(2,1)S(1)}, bf16[144,640]{1,0:T(8,128)(2,1)S(1)}, bf16[144,640]{1,0:T(8,128)(2,1)S(1)}, /*index=5*/bf16[144,640]{1,0:T(8,128)(2,1)S(1)}, bf16[32,128,128]{2,1,0:T(8,128)(2,1)S(1)}, ...), branch_computations={%region_0.0_spmd, %region_1.4_spmd} | conditional | flops 20942082048 | bytes 180560416 | solution.py:492
  21.2 0.0 all-gather.3.cloned.1.call-start
  21.3 0.9 pad_maximum_fusion
  22.2 0.0 all-gather.3.cloned.1.call-update
  22.2 0.0 copy-start.2
  22.3 31.1 %all_to_all.16.refs_0_.refs_2_.refs_4_ = bf16[32,128,128]{2,1,0:T(8,128)(2,1)S(1)} all-to-all(bf16[32,128,128]{2,1,0:T(8,128)(2,1)S(1)} %get-tuple-element.30), channel_id=1, replica_groups=mesh['dp'=4,'ctx'=32] {'ctx'}, dimensions={0} | all-to-all | bytes 2097152 | tf_op jit(solution)/shard_map/cond/branch_1_fun/all_to_all | solution.py:466
  53.3 5.4 %all-to-all-start.1 = ((bf16[32,128,128]{2,1,0:T(8,128)(2,1)}), bf16[32,128,128]{2,1,0:T(8,128)(2,1)S(1)}, u32[]{:S(2)}, u32[]{:S(2)}) async-start(bf16[32,128,128]{2,1,0:T(8,128)(2,1)} %get-tuple-element.36), calls=%async_computation.1 | async-start | bytes 2097152 | tf_op jit(solution)/shard_map/cond/branch_1_fun/all_to_all | solution.py:466
  58.7 0.6 collective-permute-start
  59.3 2.1 %collective-permute-start.1 = (bf16[32,128,128]{2,1,0:T(8,128)(2,1)S(1)}, bf16[32,128,128]{2,1,0:T(8,128)(2,1)}, u32[]{:S(2)}, u32[]{:S(2)}) collective-permute-start(bf16[32,128,128]{2,1,0:T(8,128)(2,1)S(1)} %all_to_all.16.refs_0_.refs_2_.refs_4_), channel_id=1, source_target_pairs={{0,96},{32,0},{64,32},{96,64},{1,97},{33,1},{65,33},{97,65},{2,98}... | collective-permute-start | bytes 3145736 | tf_op jit(solution)/shard_map/cond/branch_1_fun/ppermute | solution.py:434
  61.5 18.9 %all-to-all-done.1.refs_1_.refs_3_.refs_5_ = bf16[32,128,128]{2,1,0:T(8,128)(2,1)S(1)} async-done(((bf16[32,128,128]{2,1,0:T(8,128)(2,1)}), bf16[32,128,128]{2,1,0:T(8,128)(2,1)S(1)}, u32[]{:S(2)}, u32[]{:S(2)}) %all-to-all-start.1) | async-done | bytes 1048608 | tf_op jit(solution)/shard_map/cond/branch_1_fun/all_to_all | solution.py:466
  80.3 0.0 copy-start
  80.3 0.0 collective-permute-start.3
  80.3 2.7 %collective-permute-start.4 = (bf16[32,128,128]{2,1,0:T(8,128)(2,1)S(1)}, bf16[32,128,128]{2,1,0:T(8,128)(2,1)}, u32[]{:S(2)}, u32[]{:S(2)}) collective-permute-start(bf16[32,128,128]{2,1,0:T(8,128)(2,1)S(1)} %all-to-all-done.1.refs_1_.refs_3_.refs_5_), channel_id=1, source_target_pairs={{0,96},{32,0},{64,32},{96,64},{1,97},{33,1},{65,33},{97,65},{2,98}... | collective-permute-start | bytes 3145736 | tf_op jit(solution)/shard_map/cond/branch_1_fun/ppermute | solution.py:434
  83.0 0.6 broadcast_in_dim.8
  83.7 5.6 %all-to-all-start.2 = ((s32[32,4,128]{2,1,0:T(4,128)}), s32[32,4,128]{2,1,0:T(4,128)S(1)}, u32[]{:S(2)}, u32[]{:S(2)}) async-start(s32[32,4,128]{2,1,0:T(4,128)} %broadcast_in_dim.8), calls=%async_computation.2 | async-start | bytes 131072 | tf_op jit(solution)/shard_map/cond/branch_1_fun/all_to_all | solution.py:476
  89.2 0.0 copy-done.2
  89.3 0.0 collective-permute-done.refs_0_.refs_2_
  89.3 0.0 collective-permute-done.1.refs_4_.refs_6_.refs_2_
  89.3 0.1 collective-permute-start.2
  89.4 7.8 %all-to-all-done.2.ids_ref = s32[32,4,128]{2,1,0:T(4,128)S(1)} async-done(((s32[32,4,128]{2,1,0:T(4,128)}), s32[32,4,128]{2,1,0:T(4,128)S(1)}, u32[]{:S(2)}, u32[]{:S(2)}) %all-to-all-start.2) | async-done | bytes 65568 | tf_op jit(solution)/shard_map/cond/branch_1_fun/all_to_all | solution.py:476
  97.1 2.4 %convert_reduce_fusion = s32[32,4]{1,0:T(8,128)S(1)} fusion(s32[32,4,128]{2,0,1:T(8,128)S(1)} %copy.9), kind=kLoop, calls=%fused_computation.1 | loop fusion | flops 1572736 | bytes 66048 | tf_op jit(solution)/shard_map/cond/branch_1_fun/reduce_sum | solution.py:439
  99.5 0.3 select_reduce_fusion
  99.9 3.5 %hidden_gram.2.refs_8_ = f32[3,16,256,256]{3,2,1,0:T(8,128)} custom-call(s32[32,4,128]{2,1,0:T(4,128)S(1)} %copy.12.first_ref, bf16[32,128,128]{2,1,0:T(8,128)(2,1)S(1)} %all_to_all.16.refs_0_.refs_2_.refs_4_, bf16[32,128,128]{2,1,0:T(8,128)(2,1)S(1)} %all-to-all-done.1.refs_1_.refs_3_.refs_5_, bf16[32,128,128]{2,1,0:T(8,128)(2,1)S(1)} %all_to_all.16.refs_0_.refs_2_.refs_4_, ...), custom_call_target="tpu_custom_call" | custom-call | flops 1073741824 | bytes 6291456 | tf_op jit(solution)/shard_map/cond/branch_1_fun/hidden_gram/pallas_call | solution.py:100
  103.3 0.0 copy-done
  103.3 3.6 %collective-permute-done.3.refs_1_.refs_3_ = bf16[32,128,128]{2,1,0:T(8,128)(2,1)} collective-permute-done((bf16[32,128,128]{2,1,0:T(8,128)(2,1)S(1)}, bf16[32,128,128]{2,1,0:T(8,128)(2,1)}, u32[]{:S(2)}, u32[]{:S(2)}) %collective-permute-start.3) | collective-permute-done | bytes 1048608 | tf_op jit(solution)/shard_map/cond/branch_1_fun/ppermute | solution.py:434
  107.0 0.0 collective-permute-done.4.refs_5_.refs_7_.refs_3_
  107.0 2.4 %collective-permute-start.5 = (bf16[32,128,128]{2,1,0:T(8,128)(2,1)}, bf16[32,128,128]{2,1,0:T(8,128)(2,1)}, u32[]{:S(2)}, u32[]{:S(2)}) collective-permute-start(bf16[32,128,128]{2,1,0:T(8,128)(2,1)} %collective-permute-done.4.refs_5_.refs_7_.refs_3_), channel_id=1, source_target_pairs={{0,96},{32,0},{64,32},{96,64},{1,97},{33,1},{65,33},{97,65},{2,98}... | collective-permute-start | bytes 3145736 | tf_op jit(solution)/shard_map/cond/branch_1_fun/ppermute | solution.py:434
  109.3 7.9 %hidden_gram.3.pairs_hbm = f32[3,16,256,256]{3,2,1,0:T(8,128)} custom-call(s32[32,4,128]{2,1,0:T(4,128)S(1)} %copy.12.first_ref, bf16[32,128,128]{2,1,0:T(8,128)(2,1)} %collective-permute-done.refs_0_.refs_2_, bf16[32,128,128]{2,1,0:T(8,128)(2,1)} %collective-permute-done.3.refs_1_.refs_3_, ...), custom_call_target="tpu_custom_call", output_to_operand_aliasing={{}: (9, {})} | custom-call | flops 2147483648 | bytes 12582912 | tf_op jit(solution)/shard_map/cond/branch_1_fun/hidden_gram/pallas_call | solution.py:100
  117.2 2.3 %all-gather.3.cloned.1.call-done = bf16[128,128,640]{2,1,0:T(8,128)(2,1)} async-done(((bf16[4,128,640]{2,1,0:T(8,128)(2,1)}), bf16[128,128,640]{2,1,0:T(8,128)(2,1)}) %all-gather.3.cloned.1.call-update) | async-done | bytes 20971536 | tf_op jit(solution)/shard_map/cond/branch_1_fun/all_gather | solution.py:459
  119.5 17.6 %gram.1 = (f32[128,128]{1,0:T(8,128)S(1)}, bf16[32,4,128,640]{3,2,1,0:T(8,128)(2,1)S(1)}, f32[16,256,256]{2,1,0:T(8,128)S(1)}) custom-call(s32[4]{0:T(128)S(1)} %compare_select_fusion.rows_ref, s32[32,4,128]{2,1,0:T(4,128)S(1)} %all-to-all-done.2.ids_ref, s32[32,4,128]{2,1,0:T(4,128)S(1)} %copy.12.first_ref, f32[3,16,256,256]{3,2,1,0:T(8,128)} %hidden_gram.3.pairs_hbm, ...), custom_call_target="tpu_custom_call" | custom-call | flops 11274289152 | bytes 20971520 | tf_op jit(solution)/shard_map/cond/branch_1_fun/gram/pallas_call | solution.py:245
  137.1 0.0 collective-permute-done.2.refs_0_.refs_6_
  137.1 0.0 collective-permute-done.5.refs_1_.refs_7_
  137.1 0.0 copy-start.1
  137.2 3.8 %gram_late.1 = f32[128,1,128]{2,1,0:T(1,128)S(1)} custom-call(s32[4]{0:T(128)S(1)} %compare_select_fusion.rows_ref, s32[32,4,128]{2,1,0:T(4,128)S(1)} %all-to-all-done.2.ids_ref, bf16[32,128,128]{2,1,0:T(8,128)(2,1)} %collective-permute-done.2.refs_0_.refs_6_, bf16[32,128,128]{2,1,0:T(8,128)(2,1)} %collective-permute-done.5.refs_1_.refs_7_, ...), custom_call_target="tpu_custom_call" | custom-call | flops 1073741824 | bytes 4194304 | tf_op jit(solution)/shard_map/cond/branch_1_fun/gram_late/pallas_call | solution.py:270
  140.9 15.1 %all_to_all.17.norms_ref = f32[128,1,128]{2,1,0:T(1,128)S(1)} all-to-all(f32[128,1,128]{2,1,0:T(1,128)S(1)} %gram_late.1), channel_id=1, replica_groups=mesh['dp'=4,'ctx'=32] {'dp','ctx'}, dimensions={0} | all-to-all | bytes 131072 | tf_op jit(solution)/shard_map/cond/branch_1_fun/all_to_all | solution.py:486
  156.0 0.0 copy-done.1
  156.0 11.0 %product.1 = f32[256,640]{1,0:T(8,128)} custom-call(s32[4]{0:T(128)S(1)} %compare_select_fusion.rows_ref, s32[32,4,128]{2,1,0:T(4,128)S(1)} %all-to-all-done.2.ids_ref, f32[128,1,128]{2,1,0:T(1,128)S(1)} %all_to_all.17.norms_ref, bf16[32,128,128]{2,1,0:T(8,128)(2,1)} %collective-permute-done.refs_0_.refs_2_, ...), custom_call_target="tpu_custom_call" | custom-call | flops 5368709120 | bytes 29360128 | tf_op jit(solution)/shard_map/cond/branch_1_fun/product/pallas_call | solution.py:350
  (10 shorter events, 0.2 us)
Async XLA Ops:
  8.4 9.0 %collective-permute-start.6 = (bf16[144,640]{1,0:T(8,128)(2,1)S(1)}, bf16[144,640]{1,0:T(8,128)(2,1)S(1)}, u32[]{:S(2)}, u32[]{:S(2)}) collective-permute-start(bf16[144,640]{1,0:T(8,128)(2,1)S(1)} %get-tuple-element.51), channel_id=1, source_target_pairs={{0,32},{32,64},{64,96},{96,0},{1,33},{33,65},{65,97},{97,1},{2,34}... | collective-permute-start | bytes 552968 | tf_op jit(solution)/shard_map/ppermute | solution.py:434
  10.6 6.8 %collective-permute-start.7 = (bf16[144,640]{1,0:T(8,128)(2,1)S(1)}, bf16[144,640]{1,0:T(8,128)(2,1)S(1)}, u32[]{:S(2)}, u32[]{:S(2)}) collective-permute-start(bf16[144,640]{1,0:T(8,128)(2,1)S(1)} %get-tuple-element.52), channel_id=1, source_target_pairs={{0,96},{32,0},{64,32},{96,64},{1,97},{33,1},{65,33},{97,65},{2,98}... | collective-permute-start | bytes 552968 | tf_op jit(solution)/shard_map/ppermute | solution.py:434
  12.1 9.1 %collective-permute-start.8 = (bf16[144,640]{1,0:T(8,128)(2,1)S(1)}, bf16[144,640]{1,0:T(8,128)(2,1)S(1)}, u32[]{:S(2)}, u32[]{:S(2)}) collective-permute-start(bf16[144,640]{1,0:T(8,128)(2,1)S(1)} %get-tuple-element.54), channel_id=1, source_target_pairs={{0,64},{32,96},{64,0},{96,32},{1,65},{33,97},{65,1},{97,33},{2,66}... | collective-permute-start | bytes 552968 | tf_op jit(solution)/shard_map/ppermute | solution.py:434
  21.2 98.3 %all-gather.3.cloned.1.call-start = ((), (), s32[]{:S(2)}) async-start(), calls=%async_computation.4 | async-start | bytes 21626880 | tf_op jit(solution)/shard_map/cond/branch_1_fun/all_gather | solution.py:459
  22.2 67.0 %copy-start.2 = (s32[4]{0:T(128)S(1)}, s32[4]{0:T(128)}, u32[]{:S(2)}) copy-start(s32[4]{0:T(128)} %constant.18.clone.1) | copy-start | bytes 52 | tf_op jit(solution)/shard_map/cond
  53.3 27.0 %all-to-all-start.1 = ((bf16[32,128,128]{2,1,0:T(8,128)(2,1)}), bf16[32,128,128]{2,1,0:T(8,128)(2,1)S(1)}, u32[]{:S(2)}, u32[]{:S(2)}) async-start(bf16[32,128,128]{2,1,0:T(8,128)(2,1)} %get-tuple-element.36), calls=%async_computation.1 | async-start | bytes 2097152 | tf_op jit(solution)/shard_map/cond/branch_1_fun/all_to_all | solution.py:466
  58.7 30.6 %collective-permute-start = (bf16[32,128,128]{2,1,0:T(8,128)(2,1)S(1)}, bf16[32,128,128]{2,1,0:T(8,128)(2,1)}, u32[]{:S(2)}, u32[]{:S(2)}) collective-permute-start(bf16[32,128,128]{2,1,0:T(8,128)(2,1)S(1)} %all_to_all.16.refs_0_.refs_2_.refs_4_), channel_id=1, source_target_pairs={{0,32},{32,64},{64,96},{96,0},{1,33},{33,65},{65,97},{97,1},{2,34}... | collective-permute-start | bytes 3145736 | tf_op jit(solution)/shard_map/cond/branch_1_fun/ppermute | solution.py:434
  59.3 30.0 %collective-permute-start.1 = (bf16[32,128,128]{2,1,0:T(8,128)(2,1)S(1)}, bf16[32,128,128]{2,1,0:T(8,128)(2,1)}, u32[]{:S(2)}, u32[]{:S(2)}) collective-permute-start(bf16[32,128,128]{2,1,0:T(8,128)(2,1)S(1)} %all_to_all.16.refs_0_.refs_2_.refs_4_), channel_id=1, source_target_pairs={{0,96},{32,0},{64,32},{96,64},{1,97},{33,1},{65,33},{97,65},{2,98}... | collective-permute-start | bytes 3145736 | tf_op jit(solution)/shard_map/cond/branch_1_fun/ppermute | solution.py:434
  80.3 23.0 %copy-start = (bf16[32,128,128]{2,1,0:T(8,128)(2,1)}, bf16[32,128,128]{2,1,0:T(8,128)(2,1)S(1)}, u32[]{:S(2)}) copy-start(bf16[32,128,128]{2,1,0:T(8,128)(2,1)S(1)} %all-to-all-done.1.refs_1_.refs_3_.refs_5_) | copy-start | bytes 3145732 | tf_op jit(solution)/shard_map/cond
  80.3 26.6 %collective-permute-start.3 = (bf16[32,128,128]{2,1,0:T(8,128)(2,1)S(1)}, bf16[32,128,128]{2,1,0:T(8,128)(2,1)}, u32[]{:S(2)}, u32[]{:S(2)}) collective-permute-start(bf16[32,128,128]{2,1,0:T(8,128)(2,1)S(1)} %all-to-all-done.1.refs_1_.refs_3_.refs_5_), channel_id=1, source_target_pairs={{0,32},{32,64},{64,96},{96,0},{1,33},{33,65},{65,97},{97,1},{2,34}... | collective-permute-start | bytes 3145736 | tf_op jit(solution)/shard_map/cond/branch_1_fun/ppermute | solution.py:434
  80.3 26.6 %collective-permute-start.4 = (bf16[32,128,128]{2,1,0:T(8,128)(2,1)S(1)}, bf16[32,128,128]{2,1,0:T(8,128)(2,1)}, u32[]{:S(2)}, u32[]{:S(2)}) collective-permute-start(bf16[32,128,128]{2,1,0:T(8,128)(2,1)S(1)} %all-to-all-done.1.refs_1_.refs_3_.refs_5_), channel_id=1, source_target_pairs={{0,96},{32,0},{64,32},{96,64},{1,97},{33,1},{65,33},{97,65},{2,98}... | collective-permute-start | bytes 3145736 | tf_op jit(solution)/shard_map/cond/branch_1_fun/ppermute | solution.py:434
  83.7 13.5 %all-to-all-start.2 = ((s32[32,4,128]{2,1,0:T(4,128)}), s32[32,4,128]{2,1,0:T(4,128)S(1)}, u32[]{:S(2)}, u32[]{:S(2)}) async-start(s32[32,4,128]{2,1,0:T(4,128)} %broadcast_in_dim.8), calls=%async_computation.2 | async-start | bytes 131072 | tf_op jit(solution)/shard_map/cond/branch_1_fun/all_to_all | solution.py:476
  89.3 47.8 %collective-permute-start.2 = (bf16[32,128,128]{2,1,0:T(8,128)(2,1)}, bf16[32,128,128]{2,1,0:T(8,128)(2,1)}, u32[]{:S(2)}, u32[]{:S(2)}) collective-permute-start(bf16[32,128,128]{2,1,0:T(8,128)(2,1)} %collective-permute-done.refs_0_.refs_2_), channel_id=1, source_target_pairs={{0,32},{32,64},{64,96},{96,0},{1,33},{33,65},{65,97},{97,1},{2,34}... | collective-permute-start | bytes 3145736 | tf_op jit(solution)/shard_map/cond/branch_1_fun/ppermute | solution.py:434
  107.0 30.2 %collective-permute-start.5 = (bf16[32,128,128]{2,1,0:T(8,128)(2,1)}, bf16[32,128,128]{2,1,0:T(8,128)(2,1)}, u32[]{:S(2)}, u32[]{:S(2)}) collective-permute-start(bf16[32,128,128]{2,1,0:T(8,128)(2,1)} %collective-permute-done.4.refs_5_.refs_7_.refs_3_), channel_id=1, source_target_pairs={{0,96},{32,0},{64,32},{96,64},{1,97},{33,1},{65,33},{97,65},{2,98}... | collective-permute-start | bytes 3145736 | tf_op jit(solution)/shard_map/cond/branch_1_fun/ppermute | solution.py:434
  137.1 18.9 %copy-start.1 = (bf16[32,128,128]{2,1,0:T(8,128)(2,1)S(1)}, bf16[32,128,128]{2,1,0:T(8,128)(2,1)}, u32[]{:S(2)}) copy-start(bf16[32,128,128]{2,1,0:T(8,128)(2,1)} %copy-done) | copy-start | bytes 3145732 | tf_op jit(solution)/shard_map/cond
Sparse Core Ops, SparseCore 0:
  24.3 95.1 all-gather.2

commit v11 on v9

--- a/solution.py
+++ b/solution.py
@@ -371,11 +371,13 @@
     )(rows, ids, norms, *pieces, keep_in(pltpu.VMEM, grad))
 
 
-def quarters_kernel(offsets, me_ref, ids_ref, grad_ref, *refs):
-    out_refs, sems = refs[:-1], refs[-1]
+def quarters_kernel(offsets, me_ref, ids_hbm, grad_ref, *refs):
+    *out_refs, ids_ref, sems = refs
     tokens = grad_ref.shape[0]
     part = out_refs[0].shape[1]
     count = len(offsets)
+    ids_copy = pltpu.make_async_copy(ids_hbm, ids_ref, sems.at[count])
+    ids_copy.start()
     copies = []
     for n, (offset, out_ref) in enumerate(zip(offsets, out_refs)):
         begin = pl.multiple_of(lax.rem(me_ref[0] + offset, count) * part, BLK)
@@ -383,6 +385,7 @@
         copies.append(pltpu.make_async_copy(source, out_ref.at[pl.ds(0, tokens)], sems.at[n]))
     for copy in copies:
         copy.start()
+    ids_copy.wait()
     ids = jnp.broadcast_to(ids_ref[...].astype(jnp.float32).astype(jnp.bfloat16), (16, BLK))
     for out_ref in out_refs:
         out_ref[tokens:, :BLK] = ids
@@ -400,12 +403,15 @@
         grid_spec=pltpu.PrefetchScalarGridSpec(
             num_scalar_prefetch=1,
             grid=(),
-            in_specs=[*in_vmem(1), *in_hbm(1)],
+            in_specs=in_hbm(2),
             out_specs=in_vmem(count),
-            scratch_shapes=[pltpu.SemaphoreType.DMA((count,))],
+            scratch_shapes=[
+                pltpu.VMEM(ids.shape, ids.dtype),
+                pltpu.SemaphoreType.DMA((count + 1,)),
+            ],
         ),
         name="quarters",
-    )(me, ids, keep_in(pltpu.HBM, grad))
+    )(me, keep_in(pltpu.HBM, ids), keep_in(pltpu.HBM, grad))
 
 
 def columns_kernel(in_ref, *out_refs):

time: 175 us -> 174 us (level)
  no operation moved by 1% of the time
where the time goes in v11:
time: 174 us; the launch traced here: 173 us
  Pallas kernels  48.8 us (28%)
  blocking collectives  46.2 us (27%)
  waiting for transfers between devices  36.3 us (21%)
  starting transfers between devices  24.1 us (14%)
  between operations  13.4 us (8%)
  other arithmetic  3.63 us (2%)
    all_to_all x1, blocking collectives, rest(): own = lax.all_to_all(chunk, 'ctx', 0, 0, tiled=True)  31.1 us
    all_to_all x1, waiting for transfers between devices, rest(): own = lax.all_to_all(chunk, 'ctx', 0, 0, tiled=True)  18.9 us
    pallas_call x1, Pallas kernels, gram_early(): pl.pallas_call(functools.partial(early_kernel, kinds), out_shape=[jax.Sha...  17.6 us
    all_to_all x1, blocking collectives, rest(): norms = lax.all_to_all(partial, ('dp', 'ctx'), 0, 0, tiled=True)  15.1 us
    ppermute x9, starting transfers between devices, shift(): lax.ppermute(block, 'dp', [(i, (i + distance) % size) for i in range(size)])  13.2 us
    pallas_call x2, Pallas kernels, hidden_gram(): pl.pallas_call(functools.partial(hidden_kernel, kinds), out_shape=pltpu.H...  11.4 us
    pallas_call x1, Pallas kernels, product(): pl.pallas_call(functools.partial(product_kernel, nrows, bound), out_shape...  11 us
    all_to_all x1, waiting for transfers between devices, rest(): ids = lax.all_to_all(ids, 'ctx', 0, 0, tiled=True)  7.75 us
  transfers between devices with their start and end apart: 12, of which 5 were waited for; matrix products, arithmetic and copies ran while one was open for 2% of the time, Pallas kernels for 19%

profile of v11, /device:TPU:1, one launch (start us, length us, event | category | flops | bytes accessed | tf_op | source)
XLA Modules:
  0.0 173.4 jit_solution(11464386000957224045)
XLA Ops:
  6.5 1.2 quarters.1
  7.8 2.2 %collective-permute-start.6 = (bf16[144,640]{1,0:T(8,128)(2,1)S(1)}, bf16[144,640]{1,0:T(8,128)(2,1)S(1)}, u32[]{:S(2)}, u32[]{:S(2)}) collective-permute-start(bf16[144,640]{1,0:T(8,128)(2,1)S(1)} %get-tuple-element.51), channel_id=1, source_target_pairs={{0,32},{32,64},{64,96},{96,0},{1,33},{33,65},{65,97},{97,1},{2,34}... | collective-permute-start | bytes 552968 | tf_op jit(solution)/shard_map/ppermute | solution.py:439
  9.9 1.5 collective-permute-start.7
  11.5 1.6 collective-permute-start.8
  13.0 3.7 %columns.1 = (bf16[32,128,128]{2,1,0:T(8,128)(2,1)S(1)}, bf16[32,128,128]{2,1,0:T(8,128)(2,1)}) custom-call(bf16[128,8192]{1,0:T(8,128)(2,1)} %bitcast.12), custom_call_target="tpu_custom_call" | custom-call | tf_op jit(solution)/shard_map/columns/pallas_call | solution.py:427
  16.8 0.0 collective-permute-done.6
  16.8 0.0 collective-permute-done.7
  16.8 3.8 %collective-permute-done.8 = bf16[144,640]{1,0:T(8,128)(2,1)S(1)} collective-permute-done((bf16[144,640]{1,0:T(8,128)(2,1)S(1)}, bf16[144,640]{1,0:T(8,128)(2,1)S(1)}, u32[]{:S(2)}, u32[]{:S(2)}) %collective-permute-start.8) | collective-permute-done | bytes 184352 | tf_op jit(solution)/shard_map/ppermute | solution.py:439
  20.6 145.9 %conditional.1 = (f32[256,640]{1,0:T(8,128)}) conditional(s32[]{:T(128)} %convert_element_type.9, () %tuple.16, (s32[]{:T(128)}, (), bf16[144,640]{1,0:T(8,128)(2,1)S(1)}, bf16[144,640]{1,0:T(8,128)(2,1)S(1)}, bf16[144,640]{1,0:T(8,128)(2,1)S(1)}, /*index=5*/bf16[144,640]{1,0:T(8,128)(2,1)S(1)}, bf16[32,128,128]{2,1,0:T(8,128)(2,1)S(1)}, ...), branch_computations={%region_0.0_spmd, %region_1.4_spmd} | conditional | flops 20942082048 | bytes 180560416 | solution.py:497
  20.6 0.0 all-gather.3.cloned.1.call-start
  20.6 0.9 pad_maximum_fusion
  21.6 0.0 all-gather.3.cloned.1.call-update
  21.6 0.0 copy-start.2
  21.6 31.1 %all_to_all.16.refs_0_.refs_2_.refs_4_ = bf16[32,128,128]{2,1,0:T(8,128)(2,1)S(1)} all-to-all(bf16[32,128,128]{2,1,0:T(8,128)(2,1)S(1)} %get-tuple-element.30), channel_id=1, replica_groups=mesh['dp'=4,'ctx'=32] {'ctx'}, dimensions={0} | all-to-all | bytes 2097152 | tf_op jit(solution)/shard_map/cond/branch_1_fun/all_to_all | solution.py:471
  52.7 5.4 %all-to-all-start.1 = ((bf16[32,128,128]{2,1,0:T(8,128)(2,1)}), bf16[32,128,128]{2,1,0:T(8,128)(2,1)S(1)}, u32[]{:S(2)}, u32[]{:S(2)}) async-start(bf16[32,128,128]{2,1,0:T(8,128)(2,1)} %get-tuple-element.36), calls=%async_computation.1 | async-start | bytes 2097152 | tf_op jit(solution)/shard_map/cond/branch_1_fun/all_to_all | solution.py:471
  58.1 0.6 collective-permute-start
  58.7 2.1 %collective-permute-start.1 = (bf16[32,128,128]{2,1,0:T(8,128)(2,1)S(1)}, bf16[32,128,128]{2,1,0:T(8,128)(2,1)}, u32[]{:S(2)}, u32[]{:S(2)}) collective-permute-start(bf16[32,128,128]{2,1,0:T(8,128)(2,1)S(1)} %all_to_all.16.refs_0_.refs_2_.refs_4_), channel_id=1, source_target_pairs={{0,96},{32,0},{64,32},{96,64},{1,97},{33,1},{65,33},{97,65},{2,98}... | collective-permute-start | bytes 3145736 | tf_op jit(solution)/shard_map/cond/branch_1_fun/ppermute | solution.py:439
  60.8 18.9 %all-to-all-done.1.refs_1_.refs_3_.refs_5_ = bf16[32,128,128]{2,1,0:T(8,128)(2,1)S(1)} async-done(((bf16[32,128,128]{2,1,0:T(8,128)(2,1)}), bf16[32,128,128]{2,1,0:T(8,128)(2,1)S(1)}, u32[]{:S(2)}, u32[]{:S(2)}) %all-to-all-start.1) | async-done | bytes 1048608 | tf_op jit(solution)/shard_map/cond/branch_1_fun/all_to_all | solution.py:471
  79.7 0.0 copy-start
  79.7 0.0 collective-permute-start.3
  79.7 2.7 %collective-permute-start.4 = (bf16[32,128,128]{2,1,0:T(8,128)(2,1)S(1)}, bf16[32,128,128]{2,1,0:T(8,128)(2,1)}, u32[]{:S(2)}, u32[]{:S(2)}) collective-permute-start(bf16[32,128,128]{2,1,0:T(8,128)(2,1)S(1)} %all-to-all-done.1.refs_1_.refs_3_.refs_5_), channel_id=1, source_target_pairs={{0,96},{32,0},{64,32},{96,64},{1,97},{33,1},{65,33},{97,65},{2,98}... | collective-permute-start | bytes 3145736 | tf_op jit(solution)/shard_map/cond/branch_1_fun/ppermute | solution.py:439
  82.4 0.6 broadcast_in_dim.8
  83.0 5.6 %all-to-all-start.2 = ((s32[32,4,128]{2,1,0:T(4,128)}), s32[32,4,128]{2,1,0:T(4,128)S(1)}, u32[]{:S(2)}, u32[]{:S(2)}) async-start(s32[32,4,128]{2,1,0:T(4,128)} %broadcast_in_dim.8), calls=%async_computation.2 | async-start | bytes 131072 | tf_op jit(solution)/shard_map/cond/branch_1_fun/all_to_all | solution.py:481
  88.6 0.0 copy-done.2
  88.6 0.0 collective-permute-done.refs_0_.refs_2_
  88.6 0.0 collective-permute-done.1.refs_4_.refs_6_.refs_2_
  88.7 0.1 collective-permute-start.2
  88.7 7.8 %all-to-all-done.2.ids_ref = s32[32,4,128]{2,1,0:T(4,128)S(1)} async-done(((s32[32,4,128]{2,1,0:T(4,128)}), s32[32,4,128]{2,1,0:T(4,128)S(1)}, u32[]{:S(2)}, u32[]{:S(2)}) %all-to-all-start.2) | async-done | bytes 65568 | tf_op jit(solution)/shard_map/cond/branch_1_fun/all_to_all | solution.py:481
  96.5 2.4 %convert_reduce_fusion = s32[32,4]{1,0:T(8,128)S(1)} fusion(s32[32,4,128]{2,0,1:T(8,128)S(1)} %copy.9), kind=kLoop, calls=%fused_computation.1 | loop fusion | flops 1572736 | bytes 66048 | tf_op jit(solution)/shard_map/cond/branch_1_fun/reduce_sum | solution.py:444
  98.9 0.3 select_reduce_fusion
  99.2 3.5 %hidden_gram.2.refs_8_ = f32[3,16,256,256]{3,2,1,0:T(8,128)} custom-call(s32[32,4,128]{2,1,0:T(4,128)S(1)} %copy.12.first_ref, bf16[32,128,128]{2,1,0:T(8,128)(2,1)S(1)} %all_to_all.16.refs_0_.refs_2_.refs_4_, bf16[32,128,128]{2,1,0:T(8,128)(2,1)S(1)} %all-to-all-done.1.refs_1_.refs_3_.refs_5_, bf16[32,128,128]{2,1,0:T(8,128)(2,1)S(1)} %all_to_all.16.refs_0_.refs_2_.refs_4_, ...), custom_call_target="tpu_custom_call" | custom-call | flops 1073741824 | bytes 6291456 | tf_op jit(solution)/shard_map/cond/branch_1_fun/hidden_gram/pallas_call | solution.py:100
  102.7 0.0 copy-done
  102.7 3.6 %collective-permute-done.3.refs_1_.refs_3_ = bf16[32,128,128]{2,1,0:T(8,128)(2,1)} collective-permute-done((bf16[32,128,128]{2,1,0:T(8,128)(2,1)S(1)}, bf16[32,128,128]{2,1,0:T(8,128)(2,1)}, u32[]{:S(2)}, u32[]{:S(2)}) %collective-permute-start.3) | collective-permute-done | bytes 1048608 | tf_op jit(solution)/shard_map/cond/branch_1_fun/ppermute | solution.py:439
  106.3 0.0 collective-permute-done.4.refs_5_.refs_7_.refs_3_
  106.3 2.4 %collective-permute-start.5 = (bf16[32,128,128]{2,1,0:T(8,128)(2,1)}, bf16[32,128,128]{2,1,0:T(8,128)(2,1)}, u32[]{:S(2)}, u32[]{:S(2)}) collective-permute-start(bf16[32,128,128]{2,1,0:T(8,128)(2,1)} %collective-permute-done.4.refs_5_.refs_7_.refs_3_), channel_id=1, source_target_pairs={{0,96},{32,0},{64,32},{96,64},{1,97},{33,1},{65,33},{97,65},{2,98}... | collective-permute-start | bytes 3145736 | tf_op jit(solution)/shard_map/cond/branch_1_fun/ppermute | solution.py:439
  108.7 7.9 %hidden_gram.3.pairs_hbm = f32[3,16,256,256]{3,2,1,0:T(8,128)} custom-call(s32[32,4,128]{2,1,0:T(4,128)S(1)} %copy.12.first_ref, bf16[32,128,128]{2,1,0:T(8,128)(2,1)} %collective-permute-done.refs_0_.refs_2_, bf16[32,128,128]{2,1,0:T(8,128)(2,1)} %collective-permute-done.3.refs_1_.refs_3_, ...), custom_call_target="tpu_custom_call", output_to_operand_aliasing={{}: (9, {})} | custom-call | flops 2147483648 | bytes 12582912 | tf_op jit(solution)/shard_map/cond/branch_1_fun/hidden_gram/pallas_call | solution.py:100
  116.6 2.3 %all-gather.3.cloned.1.call-done = bf16[128,128,640]{2,1,0:T(8,128)(2,1)} async-done(((bf16[4,128,640]{2,1,0:T(8,128)(2,1)}), bf16[128,128,640]{2,1,0:T(8,128)(2,1)}) %all-gather.3.cloned.1.call-update) | async-done | bytes 20971536 | tf_op jit(solution)/shard_map/cond/branch_1_fun/all_gather | solution.py:464
  118.9 17.6 %gram.1 = (f32[128,128]{1,0:T(8,128)S(1)}, bf16[32,4,128,640]{3,2,1,0:T(8,128)(2,1)S(1)}, f32[16,256,256]{2,1,0:T(8,128)S(1)}) custom-call(s32[4]{0:T(128)S(1)} %compare_select_fusion.rows_ref, s32[32,4,128]{2,1,0:T(4,128)S(1)} %all-to-all-done.2.ids_ref, f32[3,16,256,256]{3,2,1,0:T(8,128)} %hidden_gram.3.pairs_hbm, bf16[32,4,128,640]{3,2,1,0:T(8,128)(2,1)} %bitcast.14), custom_call_target="tpu_custom_call" | custom-call | flops 11274289152 | bytes 20971520 | tf_op jit(solution)/shard_map/cond/branch_1_fun/gram/pallas_call | solution.py:244
  136.4 0.0 collective-permute-done.2.refs_0_.refs_6_
  136.5 0.0 collective-permute-done.5.refs_1_.refs_7_
  136.5 0.0 copy-start.1
  136.5 3.9 %gram_late.1 = f32[128,1,128]{2,1,0:T(1,128)S(1)} custom-call(s32[4]{0:T(128)S(1)} %compare_select_fusion.rows_ref, s32[32,4,128]{2,1,0:T(4,128)S(1)} %all-to-all-done.2.ids_ref, s32[32,4,128]{2,1,0:T(4,128)S(1)} %copy.12.first_ref, bf16[32,128,128]{2,1,0:T(8,128)(2,1)} %collective-permute-done.2.refs_0_.refs_6_, ...), custom_call_target="tpu_custom_call" | custom-call | flops 1073741824 | bytes 4194304 | tf_op jit(solution)/shard_map/cond/branch_1_fun/gram_late/pallas_call | solution.py:269
  140.4 15.1 %all_to_all.17.norms_ref = f32[128,1,128]{2,1,0:T(1,128)S(1)} all-to-all(f32[128,1,128]{2,1,0:T(1,128)S(1)} %gram_late.1), channel_id=1, replica_groups=mesh['dp'=4,'ctx'=32] {'dp','ctx'}, dimensions={0} | all-to-all | bytes 131072 | tf_op jit(solution)/shard_map/cond/branch_1_fun/all_to_all | solution.py:491
  155.5 0.0 copy-done.1
  155.5 11.0 %product.1 = f32[256,640]{1,0:T(8,128)} custom-call(s32[4]{0:T(128)S(1)} %compare_select_fusion.rows_ref, s32[32,4,128]{2,1,0:T(4,128)S(1)} %all-to-all-done.2.ids_ref, f32[128,1,128]{2,1,0:T(1,128)S(1)} %all_to_all.17.norms_ref, bf16[32,128,128]{2,1,0:T(8,128)(2,1)} %collective-permute-done.refs_0_.refs_2_, ...), custom_call_target="tpu_custom_call" | custom-call | flops 5368709120 | bytes 29360128 | tf_op jit(solution)/shard_map/cond/branch_1_fun/product/pallas_call | solution.py:349
  (10 shorter events, 0.2 us)
Async XLA Ops:
  7.8 9.0 %collective-permute-start.6 = (bf16[144,640]{1,0:T(8,128)(2,1)S(1)}, bf16[144,640]{1,0:T(8,128)(2,1)S(1)}, u32[]{:S(2)}, u32[]{:S(2)}) collective-permute-start(bf16[144,640]{1,0:T(8,128)(2,1)S(1)} %get-tuple-element.51), channel_id=1, source_target_pairs={{0,32},{32,64},{64,96},{96,0},{1,33},{33,65},{65,97},{97,1},{2,34}... | collective-permute-start | bytes 552968 | tf_op jit(solution)/shard_map/ppermute | solution.py:439
  9.9 6.8 %collective-permute-start.7 = (bf16[144,640]{1,0:T(8,128)(2,1)S(1)}, bf16[144,640]{1,0:T(8,128)(2,1)S(1)}, u32[]{:S(2)}, u32[]{:S(2)}) collective-permute-start(bf16[144,640]{1,0:T(8,128)(2,1)S(1)} %get-tuple-element.52), channel_id=1, source_target_pairs={{0,96},{32,0},{64,32},{96,64},{1,97},{33,1},{65,33},{97,65},{2,98}... | collective-permute-start | bytes 552968 | tf_op jit(solution)/shard_map/ppermute | solution.py:439
  11.5 9.1 %collective-permute-start.8 = (bf16[144,640]{1,0:T(8,128)(2,1)S(1)}, bf16[144,640]{1,0:T(8,128)(2,1)S(1)}, u32[]{:S(2)}, u32[]{:S(2)}) collective-permute-start(bf16[144,640]{1,0:T(8,128)(2,1)S(1)} %get-tuple-element.54), channel_id=1, source_target_pairs={{0,64},{32,96},{64,0},{96,32},{1,65},{33,97},{65,1},{97,33},{2,66}... | collective-permute-start | bytes 552968 | tf_op jit(solution)/shard_map/ppermute | solution.py:439
  20.6 98.3 %all-gather.3.cloned.1.call-start = ((), (), s32[]{:S(2)}) async-start(), calls=%async_computation.4 | async-start | bytes 21626880 | tf_op jit(solution)/shard_map/cond/branch_1_fun/all_gather | solution.py:464
  21.6 67.0 %copy-start.2 = (s32[4]{0:T(128)S(1)}, s32[4]{0:T(128)}, u32[]{:S(2)}) copy-start(s32[4]{0:T(128)} %constant.18.clone.1) | copy-start | bytes 52 | tf_op jit(solution)/shard_map/cond
  52.7 27.0 %all-to-all-start.1 = ((bf16[32,128,128]{2,1,0:T(8,128)(2,1)}), bf16[32,128,128]{2,1,0:T(8,128)(2,1)S(1)}, u32[]{:S(2)}, u32[]{:S(2)}) async-start(bf16[32,128,128]{2,1,0:T(8,128)(2,1)} %get-tuple-element.36), calls=%async_computation.1 | async-start | bytes 2097152 | tf_op jit(solution)/shard_map/cond/branch_1_fun/all_to_all | solution.py:471
  58.1 30.6 %collective-permute-start = (bf16[32,128,128]{2,1,0:T(8,128)(2,1)S(1)}, bf16[32,128,128]{2,1,0:T(8,128)(2,1)}, u32[]{:S(2)}, u32[]{:S(2)}) collective-permute-start(bf16[32,128,128]{2,1,0:T(8,128)(2,1)S(1)} %all_to_all.16.refs_0_.refs_2_.refs_4_), channel_id=1, source_target_pairs={{0,32},{32,64},{64,96},{96,0},{1,33},{33,65},{65,97},{97,1},{2,34}... | collective-permute-start | bytes 3145736 | tf_op jit(solution)/shard_map/cond/branch_1_fun/ppermute | solution.py:439
  58.7 30.0 %collective-permute-start.1 = (bf16[32,128,128]{2,1,0:T(8,128)(2,1)S(1)}, bf16[32,128,128]{2,1,0:T(8,128)(2,1)}, u32[]{:S(2)}, u32[]{:S(2)}) collective-permute-start(bf16[32,128,128]{2,1,0:T(8,128)(2,1)S(1)} %all_to_all.16.refs_0_.refs_2_.refs_4_), channel_id=1, source_target_pairs={{0,96},{32,0},{64,32},{96,64},{1,97},{33,1},{65,33},{97,65},{2,98}... | collective-permute-start | bytes 3145736 | tf_op jit(solution)/shard_map/cond/branch_1_fun/ppermute | solution.py:439
  79.7 23.0 %copy-start = (bf16[32,128,128]{2,1,0:T(8,128)(2,1)}, bf16[32,128,128]{2,1,0:T(8,128)(2,1)S(1)}, u32[]{:S(2)}) copy-start(bf16[32,128,128]{2,1,0:T(8,128)(2,1)S(1)} %all-to-all-done.1.refs_1_.refs_3_.refs_5_) | copy-start | bytes 3145732 | tf_op jit(solution)/shard_map/cond
  79.7 26.6 %collective-permute-start.3 = (bf16[32,128,128]{2,1,0:T(8,128)(2,1)S(1)}, bf16[32,128,128]{2,1,0:T(8,128)(2,1)}, u32[]{:S(2)}, u32[]{:S(2)}) collective-permute-start(bf16[32,128,128]{2,1,0:T(8,128)(2,1)S(1)} %all-to-all-done.1.refs_1_.refs_3_.refs_5_), channel_id=1, source_target_pairs={{0,32},{32,64},{64,96},{96,0},{1,33},{33,65},{65,97},{97,1},{2,34}... | collective-permute-start | bytes 3145736 | tf_op jit(solution)/shard_map/cond/branch_1_fun/ppermute | solution.py:439
  79.7 26.6 %collective-permute-start.4 = (bf16[32,128,128]{2,1,0:T(8,128)(2,1)S(1)}, bf16[32,128,128]{2,1,0:T(8,128)(2,1)}, u32[]{:S(2)}, u32[]{:S(2)}) collective-permute-start(bf16[32,128,128]{2,1,0:T(8,128)(2,1)S(1)} %all-to-all-done.1.refs_1_.refs_3_.refs_5_), channel_id=1, source_target_pairs={{0,96},{32,0},{64,32},{96,64},{1,97},{33,1},{65,33},{97,65},{2,98}... | collective-permute-start | bytes 3145736 | tf_op jit(solution)/shard_map/cond/branch_1_fun/ppermute | solution.py:439
  83.0 13.5 %all-to-all-start.2 = ((s32[32,4,128]{2,1,0:T(4,128)}), s32[32,4,128]{2,1,0:T(4,128)S(1)}, u32[]{:S(2)}, u32[]{:S(2)}) async-start(s32[32,4,128]{2,1,0:T(4,128)} %broadcast_in_dim.8), calls=%async_computation.2 | async-start | bytes 131072 | tf_op jit(solution)/shard_map/cond/branch_1_fun/all_to_all | solution.py:481
  88.7 47.8 %collective-permute-start.2 = (bf16[32,128,128]{2,1,0:T(8,128)(2,1)}, bf16[32,128,128]{2,1,0:T(8,128)(2,1)}, u32[]{:S(2)}, u32[]{:S(2)}) collective-permute-start(bf16[32,128,128]{2,1,0:T(8,128)(2,1)} %collective-permute-done.refs_0_.refs_2_), channel_id=1, source_target_pairs={{0,32},{32,64},{64,96},{96,0},{1,33},{33,65},{65,97},{97,1},{2,34}... | collective-permute-start | bytes 3145736 | tf_op jit(solution)/shard_map/cond/branch_1_fun/ppermute | solution.py:439
  106.3 30.1 %collective-permute-start.5 = (bf16[32,128,128]{2,1,0:T(8,128)(2,1)}, bf16[32,128,128]{2,1,0:T(8,128)(2,1)}, u32[]{:S(2)}, u32[]{:S(2)}) collective-permute-start(bf16[32,128,128]{2,1,0:T(8,128)(2,1)} %collective-permute-done.4.refs_5_.refs_7_.refs_3_), channel_id=1, source_target_pairs={{0,96},{32,0},{64,32},{96,64},{1,97},{33,1},{65,33},{97,65},{2,98}... | collective-permute-start | bytes 3145736 | tf_op jit(solution)/shard_map/cond/branch_1_fun/ppermute | solution.py:439
  136.5 19.0 %copy-start.1 = (bf16[32,128,128]{2,1,0:T(8,128)(2,1)S(1)}, bf16[32,128,128]{2,1,0:T(8,128)(2,1)}, u32[]{:S(2)}) copy-start(bf16[32,128,128]{2,1,0:T(8,128)(2,1)} %copy-done) | copy-start | bytes 3145732 | tf_op jit(solution)/shard_map/cond
Sparse Core Ops, SparseCore 0:
  23.6 95.1 all-gather.2
